TPU v7x, 128 devices: a whole 4x4x4 slice. The times are simulated.
128 devices in a mesh: ctx: 4 (over x), batch: 32 (over z, y, core).
Axes of the slice: x: 4, y: 4, z: 4, core: 2. Of those that a mesh axis runs over, the one named last changes fastest.
Arguments:
- queries: bfloat16 [32, 2, 32, 512], P('batch', None, 'ctx'), may hold values from -32 to 32
- latent_cache: bfloat16 [32, 2, 4096, 512], P('batch', None, 'ctx'), may hold values from -4 to 4
- token_latent: bfloat16 [32, 2, 512], P('batch'), may hold values from -4 to 4
- lengths: int32 [32, 2], P('batch'), may hold values from 512 to 4096, as said below
- value_up_weight: bfloat16 [32, 512, 128], P('ctx'), may hold values from -0.25 to 0.25
- out_proj: bfloat16 [4096, 2304], P('ctx'), may hold values from -0.09375 to 0.09375
- residual: bfloat16 [32, 2, 2304], P('batch'), may hold values from -6 to 6
- norm_gain: bfloat16 [2304], replicated, may hold values from 0.5 to 1.5
- router: bfloat16 [2304, 128], replicated, may hold values from -0.125 to 0.125
- expert_ids: int32 [32, 2, 8], replicated, may hold values from 0 to 127, all different within a row; in each aligned block of 64 rows (0 to 63, 64 to 127, ..., all dimensions but the last counted through in order) at most 8 rows name the same one
- expert_gate_up: bfloat16 [128, 2304, 2048], P(('ctx', 'batch')), may hold values from -0.125 to 0.125
- expert_down: bfloat16 [128, 1024, 2304], P(('ctx', 'batch')), may hold values from -0.1875 to 0.1875
- shared_gate_up: bfloat16 [2, 2304, 1024], P(None, None, 'ctx'), may hold values from -0.125 to 0.125
- shared_down: bfloat16 [1024, 2304], P('ctx'), may hold values from -0.1875 to 0.1875
Outputs:
- layer_out: bfloat16 [32, 2, 2304], P('batch')
Inputs may be any that keep to these rules, and one draw needn't show every extreme that they name: `lengths`: each block of 2 rows along the second dimension has a row with all 4096 positions valid. `expert_ids`: each row names 8 different experts; over all 64 rows no expert is named by more than 8 rows, a bound that some block reaches.
All inputs are finite; a program needn't handle non-finite values.
Results may differ from a plain program's by a relative error of at most 0.012.
Values may be sent and summed in bfloat16 or wider, within the bound.
No kernel may reach another device: no remote copies, remote signals or barrier semaphores. Data moves between devices by JAX's collectives and lax.ppermute only.
A program may use at most 128 MiB of HBM per device.

v0:
```python
import jax
import jax.numpy as jnp
from jax import lax
from jax.sharding import PartitionSpec as P

QK = 192


NEG_FILL = -1e30
ROUTE_SCALE = 2.446
EPSILON = 1e-06


def joined(array, axis, combine):
    everything = jax.tree.map(lambda part: lax.all_gather(part, axis), array)
    leading = jax.tree.map(lambda part: part[0], everything)

    def lap(k, so_far):
        return combine(so_far, jax.tree.map(lambda part: part[k], everything))

    return lax.fori_loop(1, lax.axis_size(axis), lap, leading)


def merge_parts(earlier, later_part):
    peak_a, mass_a, blend_a = earlier
    peak_b, mass_b, blend_b = later_part
    joint = jnp.maximum(peak_a, peak_b)
    factor_a = jnp.exp(peak_a - joint)
    factor_b = jnp.exp(peak_b - joint)
    return (
        joint,
        mass_a * factor_a + mass_b * factor_b,
        blend_a * factor_a[..., None] + blend_b * factor_b[..., None],
    )


def local(
    queries,
    latent_cache,
    token_latent,
    lengths,
    value_up_weight,
    out_proj,
    residual,
    norm_gain,
    router,
    expert_ids,
    expert_gate_up,
    expert_down,
    shared_gate_up,
    shared_down,
):
    ctx_index = lax.axis_index("ctx")
    batch_count = lax.axis_size("batch")
    batch_index = lax.axis_index("batch")
    own_query = queries[0]
    heads_here = own_query.shape[1]
    score_scale = QK ** (-0.5)
    every_query = lax.all_gather(queries, "ctx", axis=2, tiled=True)[0]
    cache = latent_cache[0]
    span = cache.shape[1]
    row_number = cache.shape[0]
    scores = (
        jnp.einsum("rhl,rpl->rhp", every_query, cache, preferred_element_type=jnp.float32)
        * score_scale
    )
    position = ctx_index * span + jnp.arange(span, dtype=jnp.int32)
    valid_key = position[None, None, :] < lengths[0][:, None, None]
    valid_key = jnp.broadcast_to(valid_key, scores.shape)
    scores = jnp.where(valid_key, scores, NEG_FILL)
    peak_score = jnp.max(scores, axis=-1)
    probability = jnp.where(valid_key, jnp.exp(scores - peak_score[..., None]), 0.0).astype(
        jnp.bfloat16
    )
    mass_sum = jnp.sum(probability.astype(jnp.float32), axis=-1)
    blend_sum = jnp.einsum("rhp,rpl->rhl", probability, cache, preferred_element_type=jnp.float32)
    first_head = ctx_index * heads_here
    peak_score, mass_sum, blend_sum = joined((peak_score, mass_sum, blend_sum), "ctx", merge_parts)
    peak_score = lax.dynamic_slice_in_dim(peak_score, first_head, heads_here, 1)
    mass_sum = lax.dynamic_slice_in_dim(mass_sum, first_head, heads_here, 1)
    blend_sum = lax.dynamic_slice_in_dim(blend_sum, first_head, heads_here, 1)
    fresh = token_latent[0]
    fresh_score = (
        jnp.einsum("rhl,rl->rh", own_query, fresh, preferred_element_type=jnp.float32) * score_scale
    )
    new_peak = jnp.maximum(peak_score, fresh_score)
    keep_factor = jnp.exp(peak_score - new_peak)
    fresh_weight = jnp.exp(fresh_score - new_peak).astype(jnp.bfloat16).astype(jnp.float32)
    mass_sum = mass_sum * keep_factor + fresh_weight
    blend_sum = (
        blend_sum * keep_factor[..., None]
        + fresh_weight[..., None] * fresh.astype(jnp.float32)[:, None, :]
    )
    latent_out = (blend_sum / mass_sum[..., None]).astype(jnp.bfloat16)
    head_values = jnp.einsum(
        "rhl,hlv->rhv", latent_out, value_up_weight, preferred_element_type=jnp.float32
    )
    head_values = head_values.astype(jnp.bfloat16).reshape(row_number, -1)
    attention = lax.psum(jnp.dot(head_values, out_proj, preferred_element_type=jnp.float32), "ctx")
    hidden = residual[0].astype(jnp.float32) + attention
    inverse = lax.rsqrt(jnp.mean(hidden * hidden, axis=-1, keepdims=True) + EPSILON)
    normed = (hidden * inverse * norm_gain.astype(jnp.float32)).astype(jnp.bfloat16)
    logits = jnp.dot(normed, router, preferred_element_type=jnp.float32)
    experts_total = router.shape[1]
    picks = lax.dynamic_index_in_dim(expert_ids, batch_index, 0, keepdims=False)
    choose_k = picks.shape[1]
    expert_range = jnp.arange(experts_total, dtype=jnp.int32)
    chosen = jnp.sum(
        jnp.where(picks[:, :, None] == expert_range[None, None, :], logits[:, None, :], 0.0),
        axis=-1,
    )
    gate_score = jax.nn.sigmoid(chosen)
    route_weight = (ROUTE_SCALE * gate_score / jnp.sum(gate_score, axis=-1, keepdims=True)).astype(
        jnp.bfloat16
    )
    shared_mid = jnp.einsum(
        "rd,gdf->grf", normed, shared_gate_up, preferred_element_type=jnp.float32
    )
    shared_act = (jax.nn.silu(shared_mid[0]) * shared_mid[1]).astype(jnp.bfloat16)
    shared_part = jnp.dot(shared_act, shared_down, preferred_element_type=jnp.float32)
    every_rows, every_weight = (
        lax.all_gather(normed, "batch", axis=0, tiled=True),
        lax.all_gather(route_weight, "batch", axis=0, tiled=True),
    )
    total_rows = every_rows.shape[0]
    all_picks = expert_ids.reshape(total_rows, choose_k)
    capacity = max(2, 2 * total_rows * choose_k // experts_total)
    own_expert = ctx_index * batch_count + batch_index
    own_match = all_picks == own_expert
    row_hit = jnp.sum(own_match.astype(jnp.int32), axis=1)
    row_rank = jnp.cumsum(row_hit) - row_hit
    slot_range = jnp.arange(capacity, dtype=jnp.int32)
    selector = ((slot_range[:, None] == row_rank[None, :]) & (row_hit[None, :] > 0)).astype(
        jnp.bfloat16
    )
    expert_in = jnp.dot(selector, every_rows, preferred_element_type=jnp.float32).astype(
        jnp.bfloat16
    )
    expert_width = expert_down.shape[1]
    middle = jnp.dot(expert_in, expert_gate_up[0], preferred_element_type=jnp.float32)
    active = (jax.nn.silu(middle[:, :expert_width]) * middle[:, expert_width:]).astype(jnp.bfloat16)
    answer = jnp.dot(active, expert_down[0], preferred_element_type=jnp.float32).astype(
        jnp.bfloat16
    )
    every_answer = lax.all_gather(answer, ("ctx", "batch"), axis=0, tiled=True)
    picked_all = jnp.sum(
        (all_picks[None, :, :] == expert_range[:, None, None]).astype(jnp.int32), axis=2
    )
    ranks_all = jnp.cumsum(picked_all, axis=1) - picked_all
    own_ranks = lax.dynamic_slice_in_dim(ranks_all, batch_index * row_number, row_number, 1)
    pick_hot = picks[:, :, None] == expert_range[None, None, :]
    pick_rank = jnp.sum(jnp.where(pick_hot, own_ranks.T[:, None, :], 0), axis=-1)
    slot_index = picks * capacity + pick_rank
    all_slots = jnp.arange(every_answer.shape[0], dtype=jnp.int32)
    mixing = jnp.sum(
        jnp.where(
            all_slots[None, None, :] == slot_index[:, :, None],
            route_weight.astype(jnp.float32)[:, :, None],
            0.0,
        ),
        axis=1,
    )
    routed = jnp.dot(mixing.astype(jnp.bfloat16), every_answer, preferred_element_type=jnp.float32)
    shared_sum = lax.psum(shared_part, "ctx")
    result = hidden + shared_sum + routed
    return result.astype(jnp.bfloat16)[None]


def solution(mesh):
    return jax.shard_map(
        local,
        mesh=mesh,
        in_specs=(
            P("batch", None, "ctx", None),
            P("batch", None, "ctx", None),
            P("batch", None, None),
            P("batch", None),
            P("ctx", None, None),
            P("ctx", None),
            P("batch", None, None),
            P(),
            P(),
            P(),
            P(("ctx", "batch"), None, None),
            P(("ctx", "batch"), None, None),
            P(None, None, "ctx"),
            P("ctx", None),
        ),
        out_specs=P("batch", None, None),
        check_vma=False,
    )
```

profile of v0, /device:TPU:1, one launch (start us, length us, event | category | flops | bytes accessed | tf_op | source)
XLA Modules:
  0.0 188.1 jit_solution(11548866682679423672)
XLA Ops:
  6.6 10.5 %all_gather.27 = bf16[1,2,32,512]{3,2,1,0:T(8,128)(2,1)S(1)} all-gather(bf16[1,2,8,512]{3,2,1,0:T(8,128)(2,1)} %param.16), channel_id=1, replica_groups=mesh['ctx'=4,'batch'=32] {'ctx'}, dimensions={2}, use_global_device_ids=true | all-gather | bytes 81920 | tf_op jit(solution)/shard_map/all_gather | solution.py:59
  17.1 0.7 broadcast_compare_fusion
  17.8 2.4 %fusion.64 = (f32[2,32]{1,0:T(2,128)S(1)}, f32[2,32,1024]{2,1,0:T(8,128)S(1)}) fusion(bf16[1,2,1024,512]{3,2,1,0:T(8,128)(2,1)} %param.17, bf16[1,2,32,512]{3,2,1,0:T(8,128)(2,1)S(1)} %all_gather.27, pred[2,1024]{1,0:T(4,128)(4,1)S(1)} %broadcast_compare_fusion), kind=kOutput, calls=%fused_computation.94 | convolution fusion | flops 67305408 | bytes 2427136 | tf_op jit(solution)/shard_map/rhl,rpl->rhp/dot_general | solution.py:64
  20.2 2.1 %fusion.12 = f32[2,32,512]{2,1,0:T(8,128)S(1)} fusion(bf16[1,2,1024,512]{3,2,1,0:T(8,128)(2,1)} %param.17, f32[2,32,1024]{2,1,0:T(8,128)S(1)} %get-tuple-element.210, f32[2,32]{1,0:T(2,128)S(1)} %get-tuple-element.209, pred[2,1024]{1,0:T(4,128)(4,1)S(1)} %broadcast_compare_fusion), kind=kOutput, calls=%fused_computation.18 | convolution fusion | flops 67305472 | bytes 2492672 | tf_op jit(solution)/shard_map/rhp,rpl->rhl/dot_general | solution.py:76
  22.9 9.9 %all-gather.2 = f32[8,32,512]{2,1,0:T(8,128)S(1)} all-gather(f32[2,32,512]{2,1,0:T(8,128)S(1)} %fusion.12), channel_id=4, replica_groups=mesh['ctx'=4,'batch'=32] {'ctx'}, dimensions={0}, use_global_device_ids=true | all-gather | bytes 655360 | tf_op jit(solution)/shard_map/all_gather | solution.py:15
  32.8 7.3 %all-gather.4 = f32[4,2,32]{2,1,0:T(2,128)S(1)} all-gather(f32[1,2,32]{2,1,0:T(2,128)S(1)} %bitcast.112), channel_id=3, replica_groups=mesh['ctx'=4,'batch'=32] {'ctx'}, dimensions={0}, use_global_device_ids=true | all-gather | bytes 1280 | tf_op jit(solution)/shard_map/all_gather | solution.py:15
  40.1 5.2 %all-gather.3 = f32[4,2,32]{2,1,0:T(2,128)S(1)} all-gather(f32[1,2,32]{2,1,0:T(2,128)S(1)} %bitcast.111), channel_id=2, replica_groups=mesh['ctx'=4,'batch'=32] {'ctx'}, dimensions={0}, use_global_device_ids=true | all-gather | bytes 1280 | tf_op jit(solution)/shard_map/all_gather | solution.py:15
  45.3 0.4 while.19
  46.1 3.6 %fusion.23 = f32[2,2304]{1,0:T(2,128)S(1)} fusion(bf16[1024,2304]{1,0:T(8,128)(2,1)} %param.21, bf16[8,512,128]{2,1,0:T(8,128)(2,1)} %param.20, bf16[2,8,512]{2,1,0:T(8,128)(2,1)S(1)} %divide_convert_fusion), kind=kOutput, calls=%fused_computation.27 | convolution fusion | flops 11536384 | bytes 5801984 | tf_op jit(solution)/shard_map/dot_general | solution.py:99
  49.6 12.2 %psum.14 = f32[2,2304]{1,0:T(2,128)S(1)} all-reduce(f32[2,2304]{1,0:T(2,128)S(1)} %fusion.23), channel_id=1, replica_groups=mesh['ctx'=4,'batch'=32] {'ctx'}, use_global_device_ids=true, to_apply=%region_4.5 | all-reduce | flops 4608 | bytes 36864 | tf_op jit(solution)/shard_map/psum | solution.py:99
  62.5 40.4 %all-gather.5 = bf16[32,2,2304]{2,1,0:T(2,128)(2,1)S(1)} all-gather(bf16[1,2,2304]{2,1,0:T(2,128)(2,1)S(1)} %bitcast.109), channel_id=1, replica_groups=mesh['ctx'=4,'batch'=32] {'batch'}, dimensions={0}, use_global_device_ids=true | all-gather | bytes 304128 | tf_op jit(solution)/shard_map/all_gather | solution.py:122
  103.2 5.7 %fusion.3 = f32[8,2048]{1,0:T(8,128)} fusion(bf16[1,2304,2048]{2,1,0:T(8,128)(2,1)} %param.26, bf16[64,2304]{1,0:T(8,128)(2,1)S(1)} %reshape.162, s32[64]{0:T(128)S(1)} %sub.49, pred[64]{0:T(512)(128)(4,1)S(1)} %broadcast_compare_fusion.1), kind=kOutput, calls=%fused_computation.9 | convolution fusion | flops 77876224 | bytes 9797952 | tf_op jit(solution)/shard_map/dot_general | solution.py:140
  108.9 3.8 %fusion.7 = bf16[8,2304]{1,0:T(8,128)(2,1)} fusion(bf16[1,1024,2304]{2,1,0:T(8,128)(2,1)} %param.27, f32[8,2048]{1,0:T(8,128)} %fusion.3), kind=kOutput, calls=%fused_computation.14 | convolution fusion | flops 37816320 | bytes 4820992 | tf_op jit(solution)/shard_map/dot_general | solution.py:142
  112.7 1.4 copy.26
  114.1 1.5 convert_reduce_fusion
  115.6 1.4 reduce_window_sum.18
  117.1 0.9 dynamic-slice_reduce_fusion
  118.0 0.4 convolution_bitcast_fusion
  118.4 0.9 fusion.44
  119.3 12.2 %psum.15 = f32[2,2304]{1,0:T(2,128)S(1)} all-reduce(f32[2,2304]{1,0:T(2,128)} %fusion.44), channel_id=1, replica_groups=mesh['ctx'=4,'batch'=32] {'ctx'}, use_global_device_ids=true, to_apply=%region_6.7 | all-reduce | flops 4608 | bytes 36864 | tf_op jit(solution)/shard_map/psum | solution.py:164
  131.5 0.7 fusion.52
  132.2 1.2 fusion.65
  134.2 43.4 %all-gather.8.cloned.1.call-done = bf16[1024,2304]{1,0:T(8,128)(2,1)} async-done(((bf16[8,2304]{1,0:T(8,128)(2,1)}), bf16[1024,2304]{1,0:T(8,128)(2,1)}) %all-gather.8.cloned.1.call-update) | async-done | bytes 4718608 | tf_op jit(solution)/shard_map/all_gather | solution.py:145
  177.6 3.7 %fusion.11 = bf16[1,2,2304]{2,1,0:T(2,128)(2,1)} fusion(bf16[1024,2304]{1,0:T(8,128)(2,1)} %all-gather.8.cloned.1.call-done, f32[2,2304]{1,0:T(2,128)S(1)} %psum.15, bf16[2,1024]{1,0:T(2,128)(2,1)S(1)} %select_reduce_fusion, f32[2,2304]{1,0:T(2,128)} %copy-done.2, bf16[1,2,2304]{2,1,0:T(2,128)(2,1)} %param.22), kind=kOutput, calls=%fused_computation.17 | convolution fusion | flops 9460224 | bytes 4777984 | tf_op jit(solution)/shard_map/dot_general | solution.py:163
  (52 shorter events, 2.8 us)
Async XLA Ops:
  6.5 111.4 %copy-start = (bf16[2,2304,256]{2,1,0:T(8,128)(2,1)S(1)}, bf16[2,2304,256]{2,1,0:T(8,128)(2,1)}, u32[]{:S(2)}) copy-start(bf16[2,2304,256]{2,1,0:T(8,128)(2,1)} %param.28) | copy-start | bytes 7077892
  6.5 39.3 %copy-start.5 = (bf16[1,2,8,512]{3,2,1,0:T(8,128)(2,1)S(1)}, bf16[1,2,8,512]{3,2,1,0:T(8,128)(2,1)}, u32[]{:S(2)}) copy-start(bf16[1,2,8,512]{3,2,1,0:T(8,128)(2,1)} %param.16) | copy-start | bytes 49156
  6.5 16.0 %copy-start.4 = (s32[32,2,8]{0,2,1:T(8,128)S(1)}, s32[32,2,8]{0,2,1:T(8,128)}, u32[]{:S(2)}) copy-start(s32[32,2,8]{0,2,1:T(8,128)} %param.25) | copy-start | bytes 6148
  6.5 39.2 %copy-start.7 = (bf16[1,2,512]{2,1,0:T(2,128)(2,1)S(1)}, bf16[1,2,512]{2,1,0:T(2,128)(2,1)}, u32[]{:S(2)}) copy-start(bf16[1,2,512]{2,1,0:T(2,128)(2,1)} %param.18) | copy-start | bytes 6148
  6.5 171.0 %all-gather.8.cloned.1.call-start = ((), (), s32[]{:S(2)}) async-start(), calls=%async_computation | async-start | bytes 4755456 | tf_op jit(solution)/shard_map/all_gather | solution.py:145
  22.3 39.5 %copy-start.3 = (bf16[1,2,2304]{2,1,0:T(2,128)(2,1)S(1)}, bf16[1,2,2304]{2,1,0:T(2,128)(2,1)}, u32[]{:S(2)}) copy-start(bf16[1,2,2304]{2,1,0:T(2,128)(2,1)} %param.22) | copy-start | bytes 27652
  22.5 39.5 %copy-start.6 = (bf16[2304]{0:T(1024)(128)(2,1)S(1)}, bf16[2304]{0:T(1024)(128)(2,1)}, u32[]{:S(2)}) copy-start(bf16[2304]{0:T(1024)(128)(2,1)} %param.23) | copy-start | bytes 13828
  61.9 0.6 copy-start.2
  108.9 9.5 %copy-start.1 = (bf16[256,2304]{1,0:T(8,128)(2,1)S(1)}, bf16[256,2304]{1,0:T(8,128)(2,1)}, u32[]{:S(2)}) copy-start(bf16[256,2304]{1,0:T(8,128)(2,1)} %param.29) | copy-start | bytes 3538948
Sparse Core Ops, SparseCore 0:
  112.9 64.6 all-gather.7
where the time goes:
time: 189 us; the launch traced here: 188 us
  blocking collectives  97.7 us (52%)
  waiting for transfers between devices  43.4 us (23%)
  matrix products  23.9 us (13%)
  between operations  13.6 us (7%)
  other arithmetic  6.29 us (3%)
  local copies, waits for them, and re-layouts  3.07 us (2%)
    all_gather x1, waiting for transfers between devices, local(): every_answer = lax.all_gather(answer, ('ctx', 'batch'), axis=0, tiled=True)  43.4 us
    all_gather x1, blocking collectives, local(): lax.all_gather(normed, 'batch', axis=0, tiled=True)  40.4 us
    all_gather x3, blocking collectives, joined(): everything = jax.tree.map(lambda part: lax.all_gather(part, axis), array)  22.5 us
    psum x1, blocking collectives, local(): lax.psum(jnp.dot(head_values, out_proj, preferred_element_type=jnp.float3...  12.2 us
    psum x1, blocking collectives, local(): shared_sum = lax.psum(shared_part, 'ctx')  12.2 us
    all_gather x1, blocking collectives, local(): every_query = lax.all_gather(queries, 'ctx', axis=2, tiled=True)[0]  10.5 us
    dot_general x1, matrix products, local(): jnp.dot(expert_in, expert_gate_up[0], preferred_element_type=jnp.float32)  5.72 us
    dot_general x1, matrix products, local(): jnp.dot(active, expert_down[0], preferred_element_type=jnp.float32)  3.8 us
  transfers between devices with their start and end apart: 1, of which 1 were waited for; matrix products, arithmetic and copies ran while one was open for 5% of the time, Pallas kernels for 0%

commit v1 on v0

v1 whole, which is shorter than its diff:
```python
import jax
import jax.numpy as jnp
from jax import lax
from jax.sharding import PartitionSpec as P

QK = 192


NEG_FILL = -1e30
ROUTE_SCALE = 2.446
EPSILON = 1e-06


def spread(part, axis):
    copies = jnp.broadcast_to(part[None], (lax.axis_size(axis),) + part.shape)
    return lax.all_to_all(copies, axis, 0, 0)


def local(
    queries,
    latent_cache,
    token_latent,
    lengths,
    value_up_weight,
    out_proj,
    residual,
    norm_gain,
    router,
    expert_ids,
    expert_gate_up,
    expert_down,
    shared_gate_up,
    shared_down,
):
    ctx_index = lax.axis_index("ctx")
    ctx_count = lax.axis_size("ctx")
    batch_count = lax.axis_size("batch")
    batch_index = lax.axis_index("batch")
    own_query = queries[0]
    row_number, heads_here, latent_width = own_query.shape
    score_scale = QK ** (-0.5)
    cache = latent_cache[0]
    span = cache.shape[1]

    every_query = spread(own_query, "ctx").transpose(1, 0, 2, 3)
    every_query = every_query.reshape(row_number, ctx_count * heads_here, latent_width)
    scores = (
        jnp.einsum("rhl,rpl->rhp", every_query, cache, preferred_element_type=jnp.float32)
        * score_scale
    )
    position = ctx_index * span + jnp.arange(span, dtype=jnp.int32)
    valid_key = position[None, None, :] < lengths[0][:, None, None]
    scores = jnp.where(valid_key, scores, NEG_FILL)
    peak = jnp.max(scores, axis=-1, keepdims=True)
    prob = jnp.where(valid_key, jnp.exp(scores - peak), 0.0).astype(jnp.bfloat16)
    mass = jnp.sum(prob.astype(jnp.float32), axis=-1, keepdims=True)
    blend = jnp.einsum("rhp,rpl->rhl", prob, cache, preferred_element_type=jnp.float32)

    pad = jnp.zeros((row_number, ctx_count * heads_here, 126), jnp.float32)
    packed = jnp.concatenate([blend, peak, mass, pad], axis=-1)
    packed = packed.reshape(row_number, ctx_count, heads_here, -1).transpose(1, 0, 2, 3)
    packed = lax.all_to_all(packed, "ctx", 0, 0)
    blends = packed[..., :latent_width]
    peaks = packed[..., latent_width]
    masses = packed[..., latent_width + 1]
    fresh = token_latent[0]
    fresh_score = (
        jnp.einsum("rhl,rl->rh", own_query, fresh, preferred_element_type=jnp.float32) * score_scale
    )
    top = jnp.maximum(jnp.max(peaks, axis=0), fresh_score)
    factors = jnp.exp(peaks - top[None])
    fresh_weight = jnp.exp(fresh_score - top).astype(jnp.bfloat16).astype(jnp.float32)
    mass_sum = jnp.sum(masses * factors, axis=0) + fresh_weight
    blend_sum = (
        jnp.sum(blends * factors[..., None], axis=0)
        + fresh_weight[..., None] * fresh.astype(jnp.float32)[:, None, :]
    )
    latent_out = (blend_sum / mass_sum[..., None]).astype(jnp.bfloat16)
    head_values = jnp.einsum(
        "rhl,hlv->rhv", latent_out, value_up_weight, preferred_element_type=jnp.float32
    )
    head_values = head_values.astype(jnp.bfloat16).reshape(row_number, -1)
    terms = spread(jnp.dot(head_values, out_proj, preferred_element_type=jnp.float32), "ctx")
    hidden = residual[0].astype(jnp.float32) + jnp.sum(terms, axis=0)
    inverse = lax.rsqrt(jnp.mean(hidden * hidden, axis=-1, keepdims=True) + EPSILON)
    normed = (hidden * inverse * norm_gain.astype(jnp.float32)).astype(jnp.bfloat16)

    every_rows = spread(normed, "batch").reshape(batch_count * row_number, -1)
    total_rows = every_rows.shape[0]
    experts_total = router.shape[1]
    all_picks = expert_ids.reshape(total_rows, -1)
    expert_range = jnp.arange(experts_total, dtype=jnp.int32)
    picked = jnp.any(all_picks[:, :, None] == expert_range[None, None, :], axis=1)
    own_expert = ctx_index * batch_count + batch_index
    logits = jnp.dot(every_rows, router, preferred_element_type=jnp.float32)
    gate_score = jnp.where(picked, jax.nn.sigmoid(logits), 0.0)
    own_score = jnp.sum(
        jnp.where(expert_range[None, :] == own_expert, gate_score, 0.0), axis=-1, keepdims=True
    )
    own_weight = (
        (ROUTE_SCALE * own_score / jnp.sum(gate_score, axis=-1, keepdims=True))
        .astype(jnp.bfloat16)
        .astype(jnp.float32)
    )
    expert_width = expert_down.shape[1]
    middle = jnp.dot(every_rows, expert_gate_up[0], preferred_element_type=jnp.float32)
    active = (jax.nn.silu(middle[:, :expert_width]) * middle[:, expert_width:]).astype(jnp.bfloat16)
    answer = jnp.dot(active, expert_down[0], preferred_element_type=jnp.float32).astype(
        jnp.bfloat16
    )
    weighted = (own_weight * answer.astype(jnp.float32)).astype(jnp.bfloat16)

    weighted = weighted.reshape(batch_count, row_number, -1)
    routed = jnp.sum(lax.all_to_all(weighted, "batch", 0, 0).astype(jnp.float32), axis=0)

    shared_mid = jnp.einsum(
        "rd,gdf->grf", normed, shared_gate_up, preferred_element_type=jnp.float32
    )
    shared_act = (jax.nn.silu(shared_mid[0]) * shared_mid[1]).astype(jnp.bfloat16)
    shared_part = jnp.dot(shared_act, shared_down, preferred_element_type=jnp.float32)
    result = hidden + jnp.sum(spread(routed + shared_part, "ctx"), axis=0)
    return result.astype(jnp.bfloat16)[None]


def solution(mesh):
    return jax.shard_map(
        local,
        mesh=mesh,
        in_specs=(
            P("batch", None, "ctx", None),
            P("batch", None, "ctx", None),
            P("batch", None, None),
            P("batch", None),
            P("ctx", None, None),
            P("ctx", None),
            P("batch", None, None),
            P(),
            P(),
            P(),
            P(("ctx", "batch"), None, None),
            P(("ctx", "batch"), None, None),
            P(None, None, "ctx"),
            P("ctx", None),
        ),
        out_specs=P("batch", None, None),
        check_vma=False,
    )
```

time: 189 us -> 99.7 us (0.53)
  blocking collectives: 97.7 us -> 6.89 us
  starting transfers between devices: 0.03 us -> 29 us
  waiting for transfers between devices: 43.4 us -> 28.2 us
  between operations: 13.6 us -> 0.26 us
  matrix products: 23.9 us -> 16.8 us
  other arithmetic: 6.29 us -> 10.5 us
  local copies, waits for them, and re-layouts: 3.07 us -> 6.88 us
    all_gather x5 -> x0, blocking collectives: 73.3 us -> none  [the longest x1 40.4 us: local(): lax.all_gather(normed, 'batch', axis=0, tiled=True)]
    all_gather x1 -> x0, waiting for transfers between devices: 43.4 us -> none  [local(): every_answer = lax.all_gather(answer, ('ctx', 'batch'), axis=0, tiled=True)]
    all_to_all x0 -> x5, starting transfers between devices: none -> 29 us  [the longest x3 20.6 us: spread(): return lax.all_to_all(copies, axis, 0, 0)]
    all_to_all x0 -> x5, waiting for transfers between devices: none -> 28.2 us  [the longest x3 15.7 us: spread(): return lax.all_to_all(copies, axis, 0, 0)]
    psum x2 -> x0, blocking collectives: 24.4 us -> none  [the longest x1 12.2 us: local(): lax.psum(jnp.dot(head_values, out_proj, preferred_element_type=jnp.float3...]
    all_to_all x0 -> x1, blocking collectives: none -> 6.89 us  [spread(): return lax.all_to_all(copies, axis, 0, 0)]
    dot_general x4 -> x3, matrix products: 12.8 us -> 6.46 us  [the longest x1 5.58 us: local(): jnp.dot(every_rows, expert_gate_up[0], preferred_element_type=jnp.float32)]
    broadcast_in_dim x0 -> x5, local copies, waits for them, and re-layouts: none -> 3.04 us  [the longest x4 3.04 us: spread(): copies = jnp.broadcast_to(part[None], (lax.axis_size(axis),) + part.shape)]
  transfers between devices with their start and end apart: 1 -> 5, of which waited for: 1 -> 5; matrix products, arithmetic and copies ran while one was open for 5% -> 4% of each run, Pallas kernels for 0% -> 0%
where the time goes in v1:
time: 99.7 us; the launch traced here: 98.5 us
  starting transfers between devices  29 us (29%)
  waiting for transfers between devices  28.2 us (28%)
  matrix products  16.8 us (17%)
  other arithmetic  10.5 us (11%)
  blocking collectives  6.89 us (7%)
  local copies, waits for them, and re-layouts  6.88 us (7%)
    all_to_all x3, starting transfers between devices, spread(): return lax.all_to_all(copies, axis, 0, 0)  20.6 us
    all_to_all x3, waiting for transfers between devices, spread(): return lax.all_to_all(copies, axis, 0, 0)  15.7 us
    all_to_all x1, waiting for transfers between devices, local(): lax.all_to_all(weighted, 'batch', 0, 0).astype(jnp.float32)  8.17 us
    all_to_all x1, blocking collectives, spread(): return lax.all_to_all(copies, axis, 0, 0)  6.89 us
    dot_general x1, matrix products, local(): jnp.dot(every_rows, expert_gate_up[0], preferred_element_type=jnp.float32)  5.58 us
    all_to_all x1, starting transfers between devices, local(): lax.all_to_all(weighted, 'batch', 0, 0).astype(jnp.float32)  4.44 us
    all_to_all x1, waiting for transfers between devices, local(): packed = lax.all_to_all(packed, 'ctx', 0, 0)  4.37 us
    all_to_all x1, starting transfers between devices, local(): packed = lax.all_to_all(packed, 'ctx', 0, 0)  3.97 us
  transfers between devices with their start and end apart: 5, of which 5 were waited for; matrix products, arithmetic and copies ran while one was open for 4% of the time, Pallas kernels for 0%

profile of v1, /device:TPU:1, one launch (start us, length us, event | category | flops | bytes accessed | tf_op | source)
XLA Modules:
  0.0 98.5 jit_solution(2298306268389699483)
XLA Ops:
  0.0 1.5 %broadcast_in_dim.48 = bf16[4,2,8,512]{3,2,1,0:T(8,128)(2,1)} broadcast(bf16[2,8,512]{2,1,0:T(8,128)(2,1)} %bitcast.110), dimensions={1,2,3} | broadcast | bytes 81920 | tf_op jit(solution)/shard_map/broadcast_in_dim | solution.py:15
  1.5 4.8 %all-to-all-start = ((bf16[4,2,8,512]{3,2,1,0:T(8,128)(2,1)}), bf16[4,2,8,512]{3,2,1,0:T(8,128)(2,1)S(1)}, u32[]{:S(2)}, u32[]{:S(2)}) async-start(bf16[4,2,8,512]{3,2,1,0:T(8,128)(2,1)} %broadcast_in_dim.48), calls=%async_computation | async-start | bytes 131072 | tf_op jit(solution)/shard_map/all_to_all | solution.py:16
  6.3 1.4 %fusion.48 = f32[2,1,8]{2,1,0:T(1,128)} fusion(bf16[2,512,1]{1,0,2:T(2,128)(2,1)} %bitcast.113, bf16[1,2,8,512]{3,2,1,0:T(8,128)(2,1)} %param.14), kind=kOutput, calls=%fused_computation.55 | convolution fusion | flops 16384 | bytes 18496 | tf_op jit(solution)/shard_map/rhl,rl->rh/dot_general | solution.py:68
  8.6 2.3 %all-to-all-done = bf16[4,2,8,512]{3,2,1,0:T(8,128)(2,1)S(1)} async-done(((bf16[4,2,8,512]{3,2,1,0:T(8,128)(2,1)}), bf16[4,2,8,512]{3,2,1,0:T(8,128)(2,1)S(1)}, u32[]{:S(2)}, u32[]{:S(2)}) %all-to-all-start) | async-done | bytes 65568 | tf_op jit(solution)/shard_map/all_to_all | solution.py:16
  10.8 2.5 %fusion.61 = (f32[2,32]{1,0:T(2,128)S(1)}, f32[2,32,1024]{2,1,0:T(8,128)S(1)}) fusion(bf16[1,2,1024,512]{3,2,1,0:T(8,128)(2,1)} %param.15, pred[2,1024]{1,0:T(4,128)(4,1)S(1)} %broadcast_compare_fusion, bf16[4,2,8,512]{3,2,1,0:T(8,128)(2,1)S(1)} %all-to-all-done), kind=kOutput, calls=%fused_computation.79 | convolution fusion | flops 67305408 | bytes 2427136 | tf_op jit(solution)/shard_map/rhl,rpl->rhp/dot_general | solution.py:48
  15.7 1.5 %maximum_bitcast_fusion = f32[4,2,8,640]{3,2,1,0:T(8,128)} fusion(f32[2,4,8,1]{3,2,0,1:T(8,128)} %copy.63, f32[2,4,8,1]{3,2,0,1:T(8,128)} %copy.62, f32[640]{0:T(1024)S(1)} %pad.3.clone, f32[2,4,8,512]{3,2,1,0:T(8,128)S(1)} %fusion.26), kind=kLoop, calls=%fused_computation.32 | loop fusion | flops 122880 | bytes 297984 | tf_op jit(solution)/shard_map/transpose | solution.py:61
  17.2 4.0 %all-to-all-start.1 = ((f32[4,2,8,640]{3,2,1,0:T(8,128)}), f32[4,2,8,640]{3,2,1,0:T(8,128)}, u32[]{:S(2)}, u32[]{:S(2)}) async-start(f32[4,2,8,640]{3,2,1,0:T(8,128)} %maximum_bitcast_fusion), calls=%async_computation.1 | async-start | bytes 327680 | tf_op jit(solution)/shard_map/all_to_all | solution.py:62
  21.9 4.4 %all-to-all-done.1 = f32[4,2,8,640]{3,2,1,0:T(8,128)} async-done(((f32[4,2,8,640]{3,2,1,0:T(8,128)}), f32[4,2,8,640]{3,2,1,0:T(8,128)}, u32[]{:S(2)}, u32[]{:S(2)}) %all-to-all-start.1) | async-done | bytes 163872 | tf_op jit(solution)/shard_map/all_to_all | solution.py:62
  27.8 1.0 %slice_reduce_fusion.1 = (f32[4,2,8]{2,1,0:T(2,128)S(1)}, f32[4,2,8]{2,1,0:T(2,128)S(1)}, f32[4,2,8]{2,1,0:T(2,128)S(1)}) fusion(f32[4,2,8,640]{3,2,1,0:T(8,128)} %all-to-all-done.1, f32[2,8]{1,0:T(2,128)S(1)} %multiply_maximum_fusion), kind=kLoop, calls=%fused_computation.42 | loop fusion | flops 64 | bytes 1344 | tf_op jit(solution)/shard_map/slice | solution.py:64
  29.5 1.0 %fusion.38 = f32[2,8,512]{2,1,0:T(8,128)S(1)} fusion(f32[4,2,8,640]{3,2,1,0:T(8,128)} %all-to-all-done.1, f32[4,2,8]{2,1,0:T(2,128)S(1)} %get-tuple-element.6), kind=kLoop, calls=%fused_computation.34 | loop fusion | flops 57344 | bytes 164096 | tf_op jit(solution)/shard_map/reduce_sum | solution.py:75
  30.6 3.2 %fusion.34 = f32[2,2304]{1,0:T(2,128)S(1)} fusion(bf16[1024,2304]{1,0:T(8,128)(2,1)} %param.19, bf16[8,512,128]{2,1,0:T(8,128)(2,1)S(1)} %copy-done.3, bf16[2,8,512]{2,1,0:T(8,128)(2,1)S(1)} %divide_convert_fusion), kind=kOutput, calls=%fused_computation.24 | convolution fusion | flops 11536384 | bytes 5801984 | tf_op jit(solution)/shard_map/dot_general | solution.py:83
  34.5 3.3 %all-to-all-start.2 = ((f32[4,2,2304]{2,1,0:T(2,128)}), f32[4,2,2304]{2,1,0:T(2,128)S(1)}, u32[]{:S(2)}, u32[]{:S(2)}) async-start(f32[4,2,2304]{2,1,0:T(2,128)} %broadcast_in_dim.83), calls=%async_computation.2 | async-start | bytes 147456 | tf_op jit(solution)/shard_map/all_to_all | solution.py:16
  37.9 4.5 %all-to-all-done.2 = f32[4,2,2304]{2,1,0:T(2,128)S(1)} async-done(((f32[4,2,2304]{2,1,0:T(2,128)}), f32[4,2,2304]{2,1,0:T(2,128)S(1)}, u32[]{:S(2)}, u32[]{:S(2)}) %all-to-all-start.2) | async-done | bytes 73760 | tf_op jit(solution)/shard_map/all_to_all | solution.py:16
  43.5 12.5 %all-to-all-start.3 = ((bf16[32,2,2304]{2,1,0:T(2,128)(2,1)}), bf16[32,2,2304]{2,1,0:T(2,128)(2,1)S(1)}, u32[]{:S(2)}, u32[]{:S(2)}) async-start(bf16[32,2,2304]{2,1,0:T(2,128)(2,1)} %broadcast_in_dim.86), calls=%async_computation.3 | async-start | bytes 589824 | tf_op jit(solution)/shard_map/all_to_all | solution.py:16
  56.3 8.9 %all-to-all-done.3 = bf16[32,2,2304]{2,1,0:T(2,128)(2,1)S(1)} async-done(((bf16[32,2,2304]{2,1,0:T(2,128)(2,1)}), bf16[32,2,2304]{2,1,0:T(2,128)(2,1)S(1)}, u32[]{:S(2)}, u32[]{:S(2)}) %all-to-all-start.3) | async-done | bytes 294944 | tf_op jit(solution)/shard_map/all_to_all | solution.py:16
  65.3 5.6 %fusion = f32[64,2048]{1,0:T(8,128)S(1)} fusion(bf16[64,2304]{1,0:T(8,128)(2,1)S(1)} %reshape.113, bf16[1,2304,2048]{2,1,0:T(8,128)(2,1)} %param.24), kind=kOutput, calls=%fused_computation | convolution fusion | flops 603979776 | bytes 10256384 | tf_op jit(solution)/shard_map/dot_general | solution.py:106
  71.4 1.6 %fusion.13 = bf16[64,2304]{1,0:T(8,128)(2,1)} fusion(bf16[1,1024,2304]{2,1,0:T(8,128)(2,1)S(1)} %bitcast.108, f32[64]{0:T(128)S(1)} %convert_convert_fusion, f32[64,2048]{1,0:T(8,128)S(1)} %fusion), kind=kOutput, calls=%fused_computation.7 | convolution fusion | flops 302972928 | bytes 5538048 | tf_op jit(solution)/shard_map/dot_general | solution.py:108
  73.0 1.9 %reshape.114 = bf16[32,2,2304]{2,1,0:T(2,128)(2,1)} reshape(bf16[64,2304]{1,0:T(8,128)(2,1)} %fusion.13) | data formatting | bytes 589824 | tf_op jit(solution)/shard_map/reshape | solution.py:113
  74.9 4.4 %all-to-all-start.4 = ((bf16[32,2,2304]{2,1,0:T(2,128)(2,1)}), bf16[32,2,2304]{2,1,0:T(2,128)(2,1)}, u32[]{:S(2)}, u32[]{:S(2)}) async-start(bf16[32,2,2304]{2,1,0:T(2,128)(2,1)} %reshape.114), calls=%async_computation.4 | async-start | bytes 589824 | tf_op jit(solution)/shard_map/all_to_all | solution.py:114
  79.3 1.2 %convolution_bitcast_fusion = f32[2,2,256]{2,1,0:T(2,128)S(1)} fusion(bf16[2,2304,256]{2,1,0:T(8,128)(2,1)S(1)} %copy-done, f32[2,2304]{1,0:T(2,128)} %copy-done.5, bf16[1,2,2304]{2,1,0:T(2,128)(2,1)S(1)} %copy-done.6, f32[2]{0:T(128)} %copy-done.10, f32[2304]{0:T(1024)} %copy-done.7), kind=kOutput, calls=%fused_computation.23 | convolution fusion | flops 4741632 | bytes 2400264 | tf_op jit(solution)/shard_map/rd,gdf->grf/dot_general | solution.py:116
  80.5 8.2 %all-to-all-done.4 = bf16[32,2,2304]{2,1,0:T(2,128)(2,1)} async-done(((bf16[32,2,2304]{2,1,0:T(2,128)(2,1)}), bf16[32,2,2304]{2,1,0:T(2,128)(2,1)}, u32[]{:S(2)}, u32[]{:S(2)}) %all-to-all-start.4) | async-done | bytes 294944 | tf_op jit(solution)/shard_map/all_to_all | solution.py:114
  88.7 1.2 %convert_reduce_fusion = f32[2,2304]{1,0:T(2,128)S(1)} fusion(bf16[32,2,2304]{2,1,0:T(2,128)(2,1)} %all-to-all-done.4), kind=kLoop, calls=%fused_computation.25 | loop fusion | flops 290304 | bytes 313344 | tf_op jit(solution)/shard_map/reduce_sum | solution.py:114
  90.3 6.9 %all_to_all.30 = f32[4,2,2304]{2,1,0:T(2,128)S(1)} all-to-all(f32[4,2,2304]{2,1,0:T(2,128)S(1)} %broadcast_in_dim.88), channel_id=1, replica_groups=mesh['ctx'=4,'batch'=32] {'ctx'}, dimensions={0} | all-to-all | bytes 147456 | tf_op jit(solution)/shard_map/all_to_all | solution.py:16
  97.2 1.3 %fusion.43 = bf16[1,2,2304]{2,1,0:T(2,128)(2,1)} fusion(f32[2,2304]{1,0:T(2,128)S(1)} %reduce_sum.94, f32[2,2304]{1,0:T(2,128)} %copy-done.5, bf16[1,2,2304]{2,1,0:T(2,128)(2,1)S(1)} %copy-done.6), kind=kLoop, calls=%fused_computation.48 | loop fusion | flops 18432 | bytes 55296 | tf_op jit(solution)/shard_map/convert_element_type | solution.py:122
  (59 shorter events, 9.1 us)
Async XLA Ops:
  0.0 79.3 %copy-start = (bf16[2,2304,256]{2,1,0:T(8,128)(2,1)S(1)}, bf16[2,2304,256]{2,1,0:T(8,128)(2,1)}, u32[]{:S(2)}) copy-start(bf16[2,2304,256]{2,1,0:T(8,128)(2,1)} %param.26) | copy-start | bytes 7077892
  1.5 9.3 %all-to-all-start = ((bf16[4,2,8,512]{3,2,1,0:T(8,128)(2,1)}), bf16[4,2,8,512]{3,2,1,0:T(8,128)(2,1)S(1)}, u32[]{:S(2)}, u32[]{:S(2)}) async-start(bf16[4,2,8,512]{3,2,1,0:T(8,128)(2,1)} %broadcast_in_dim.48), calls=%async_computation | async-start | bytes 131072 | tf_op jit(solution)/shard_map/all_to_all | solution.py:16
  10.8 2.8 %copy-start.1 = (bf16[1,2,1024,512]{3,2,1,0:T(8,128)(2,1)S(1)}, bf16[1,2,1024,512]{3,2,1,0:T(8,128)(2,1)}, u32[]{:S(2)}) copy-start(bf16[1,2,1024,512]{3,2,1,0:T(8,128)(2,1)} %param.15) | copy-start | bytes 6291460
  13.4 17.2 %copy-start.3 = (bf16[8,512,128]{2,1,0:T(8,128)(2,1)S(1)}, bf16[8,512,128]{2,1,0:T(8,128)(2,1)}, u32[]{:S(2)}) copy-start(bf16[8,512,128]{2,1,0:T(8,128)(2,1)} %param.18) | copy-start | bytes 3145732
  17.2 9.0 %all-to-all-start.1 = ((f32[4,2,8,640]{3,2,1,0:T(8,128)}), f32[4,2,8,640]{3,2,1,0:T(8,128)}, u32[]{:S(2)}, u32[]{:S(2)}) async-start(f32[4,2,8,640]{3,2,1,0:T(8,128)} %maximum_bitcast_fusion), calls=%async_computation.1 | async-start | bytes 327680 | tf_op jit(solution)/shard_map/all_to_all | solution.py:62
  30.6 7.2 %copy-start.9 = (bf16[2304]{0:T(1024)(128)(2,1)S(1)}, bf16[2304]{0:T(1024)(128)(2,1)}, u32[]{:S(2)}) copy-start(bf16[2304]{0:T(1024)(128)(2,1)} %param.21) | copy-start | bytes 13828
  30.6 11.7 %copy-start.6 = (bf16[1,2,2304]{2,1,0:T(2,128)(2,1)S(1)}, bf16[1,2,2304]{2,1,0:T(2,128)(2,1)}, u32[]{:S(2)}) copy-start(bf16[1,2,2304]{2,1,0:T(2,128)(2,1)} %param.20) | copy-start | bytes 27652
  30.6 25.4 %copy-start.8 = (s32[32,2,8]{0,2,1:T(8,128)S(1)}, s32[32,2,8]{0,2,1:T(8,128)}, u32[]{:S(2)}) copy-start(s32[32,2,8]{0,2,1:T(8,128)} %param.23) | copy-start | bytes 6148
  34.5 7.8 %all-to-all-start.2 = ((f32[4,2,2304]{2,1,0:T(2,128)}), f32[4,2,2304]{2,1,0:T(2,128)S(1)}, u32[]{:S(2)}, u32[]{:S(2)}) async-start(f32[4,2,2304]{2,1,0:T(2,128)} %broadcast_in_dim.83), calls=%async_computation.2 | async-start | bytes 147456 | tf_op jit(solution)/shard_map/all_to_all | solution.py:16
  37.8 5.6 %copy-start.7 = (f32[2304]{0:T(1024)}, f32[2304]{0:T(1024)S(1)}, u32[]{:S(2)}) copy-start(f32[2304]{0:T(1024)S(1)} %convert_element_type.96) | copy-start | bytes 27652
  42.4 1.1 %copy-start.5 = (f32[2,2304]{1,0:T(2,128)}, f32[2,2304]{1,0:T(2,128)S(1)}, u32[]{:S(2)}) copy-start(f32[2,2304]{1,0:T(2,128)S(1)} %reduce_sum.88) | copy-start | bytes 55300
  42.5 1.0 copy-start.10
  43.5 21.7 %all-to-all-start.3 = ((bf16[32,2,2304]{2,1,0:T(2,128)(2,1)}), bf16[32,2,2304]{2,1,0:T(2,128)(2,1)S(1)}, u32[]{:S(2)}, u32[]{:S(2)}) async-start(bf16[32,2,2304]{2,1,0:T(2,128)(2,1)} %broadcast_in_dim.86), calls=%async_computation.3 | async-start | bytes 589824 | tf_op jit(solution)/shard_map/all_to_all | solution.py:16
  65.2 6.1 %slice-start = ((s8[4718592]{0:T(1024)(128)(4,1)}), s8[524288]{0:T(1024)(128)(4,1)S(1)}, s32[]{:S(2)}) async-start(s8[4718592]{0:T(1024)(128)(4,1)} %bitcast.107), calls=%async_computation.6 | async-start | bytes 1048576
  65.3 5.6 %copy-start.4 = (bf16[2304,128]{1,0:T(8,128)(2,1)S(1)}, bf16[2304,128]{1,0:T(8,128)(2,1)}, u32[]{:S(2)}) copy-start(bf16[2304,128]{1,0:T(8,128)(2,1)} %param.22) | copy-start | bytes 1769476
  65.3 6.0 %slice-start.1 = ((s8[4718592]{0:T(1024)(128)(4,1)}), s8[4194304]{0:T(1024)(128)(4,1)S(1)}, s32[]{:S(2)}) async-start(s8[4718592]{0:T(1024)(128)(4,1)} %bitcast.107), calls=%async_computation.7 | async-start | bytes 8388608
  73.0 16.9 %copy-start.2 = (bf16[256,2304]{1,0:T(8,128)(2,1)S(1)}, bf16[256,2304]{1,0:T(8,128)(2,1)}, u32[]{:S(2)}) copy-start(bf16[256,2304]{1,0:T(8,128)(2,1)} %param.27) | copy-start | bytes 3538948
  74.9 13.8 %all-to-all-start.4 = ((bf16[32,2,2304]{2,1,0:T(2,128)(2,1)}), bf16[32,2,2304]{2,1,0:T(2,128)(2,1)}, u32[]{:S(2)}, u32[]{:S(2)}) async-start(bf16[32,2,2304]{2,1,0:T(2,128)(2,1)} %reshape.114), calls=%async_computation.4 | async-start | bytes 589824 | tf_op jit(solution)/shard_map/all_to_all | solution.py:114

commit v2 on v1

v2 whole, which is shorter than its diff:
```python
import jax
import jax.numpy as jnp
from jax import lax
from jax.experimental import pallas as pl
from jax.experimental.pallas import tpu as pltpu
from jax.sharding import PartitionSpec as P

QK = 192
NEG_FILL = -1e30
ROUTE_SCALE = 2.446
EPSILON = 1e-06
SCALE = QK ** (-0.5)
BF16, F32 = jnp.bfloat16, jnp.float32
VMEM = pl.BlockSpec(memory_space=pltpu.VMEM)
SMEM = pl.BlockSpec(memory_space=pltpu.SMEM)


def call(kernel, out_shape, args, specs=None, limit=16 << 20, scratch=(), cost=None):
    return pl.pallas_call(
        kernel,
        out_shape=out_shape,
        in_specs=specs or [VMEM] * len(args),
        out_specs=jax.tree.map(lambda _: VMEM, out_shape),
        scratch_shapes=list(scratch),
        compiler_params=pltpu.CompilerParams(vmem_limit_bytes=limit),
        cost_estimate=cost,
    )(*args)


def attend_kernel(span_ref, q_ref, cache_ref, out_ref):
    rows, span, width = cache_ref.shape
    parts = q_ref.shape[0]
    heads = q_ref.shape[1] // rows
    every = q_ref[...].astype(F32)
    for r in range(rows):
        own = slice(r * heads, (r + 1) * heads)
        q = every[:, own, :].reshape(parts * heads, width).astype(BF16)
        scores = lax.dot_general(
            q, cache_ref[r], (((1,), (1,)), ((), ())), preferred_element_type=F32
        )
        scores = scores * SCALE
        position = span_ref[rows] + lax.broadcasted_iota(jnp.int32, scores.shape, 1)
        valid = position < span_ref[r]
        scores = jnp.where(valid, scores, NEG_FILL)
        peak = jnp.max(scores, axis=-1, keepdims=True)
        prob = jnp.where(valid, jnp.exp(scores - peak), 0.0).astype(BF16)
        mass = jnp.sum(prob.astype(F32), axis=-1, keepdims=True)
        blend = jnp.dot(prob, cache_ref[r], preferred_element_type=F32)
        lane = lax.broadcasted_iota(jnp.int32, (parts * heads, 128), 1)
        tail = jnp.where(lane == 0, peak, jnp.where(lane == 1, mass, 0.0))
        out_ref[:, own, :width] = blend.reshape(parts, heads, width)
        out_ref[:, own, width:] = tail.reshape(parts, heads, 128)


def project_kernel(parts_ref, q_ref, token_ref, up_ref, proj_ref, out_ref):
    heads, width, _ = up_ref.shape
    rows = token_ref.shape[0]
    token = token_ref[...].astype(F32)
    token = jnp.concatenate(
        [jnp.broadcast_to(token[r : r + 1], (heads, width)) for r in range(rows)], axis=0
    )
    fresh = jnp.sum(q_ref[...].astype(F32) * token, axis=-1, keepdims=True) * SCALE
    peaks = parts_ref[:, :, width : width + 1]
    masses = parts_ref[:, :, width + 1 : width + 2]
    top = jnp.maximum(jnp.max(peaks, axis=0), fresh)
    factors = jnp.exp(peaks - top[None])
    fresh_weight = jnp.exp(fresh - top).astype(BF16).astype(F32)
    mass = jnp.sum(masses * factors, axis=0) + fresh_weight
    blend = jnp.sum(parts_ref[:, :, :width] * factors, axis=0) + fresh_weight * token
    latent = (blend / mass).astype(BF16)
    head = lax.rem(
        lax.broadcasted_iota(jnp.int32, (rows * heads, up_ref.shape[2]), 0), jnp.int32(heads)
    )
    values = [
        jnp.where(head == h, jnp.dot(latent, up_ref[h], preferred_element_type=F32), 0.0).astype(
            BF16
        )
        for h in range(heads)
    ]
    values = jnp.concatenate(values, axis=1)
    step = 256
    for n in range(0, proj_ref.shape[1], step):
        terms = jnp.dot(values, proj_ref[:, n : n + step], preferred_element_type=F32)
        sums = [
            jnp.sum(terms[r * heads : (r + 1) * heads], axis=0, keepdims=True) for r in range(rows)
        ]
        sums = jnp.concatenate(sums, axis=0)
        for c in range(out_ref.shape[0]):
            out_ref[c, :, n : n + step] = sums


def norm_kernel(terms_ref, residual_ref, gain_ref, hidden_ref, normed_ref, copies_ref):
    hidden = residual_ref[...].astype(F32) + jnp.sum(terms_ref[...], axis=0)
    inverse = lax.rsqrt(jnp.mean(hidden * hidden, axis=-1, keepdims=True) + EPSILON)
    normed = (hidden * inverse * gain_ref[...].astype(F32)).astype(BF16)
    hidden_ref[...] = hidden
    normed_ref[...] = normed
    for b in range(copies_ref.shape[0]):
        copies_ref[b] = normed


def expert_kernel(own_ref, rows_ref, picked_ref, router_ref, gate_up_ref, down_ref, out_ref, act):
    rows = rows_ref[...]
    count = rows.shape[0]
    group = out_ref.shape[1]
    width, model = down_ref.shape
    logits = jnp.dot(rows, router_ref[...], preferred_element_type=F32)
    score = jnp.where(picked_ref[...] > 0, jax.nn.sigmoid(logits), 0.0)
    expert = lax.broadcasted_iota(jnp.int32, score.shape, 1)
    own = jnp.sum(jnp.where(expert == own_ref[0], score, 0.0), axis=-1, keepdims=True)
    weight = (ROUTE_SCALE * own / jnp.sum(score, axis=-1, keepdims=True)).astype(BF16).astype(F32)
    step = 256
    for n in range(0, width, step):
        gate = jnp.dot(rows, gate_up_ref[:, n : n + step], preferred_element_type=F32)
        up = jnp.dot(rows, gate_up_ref[:, width + n : width + n + step], preferred_element_type=F32)
        act[:, n : n + step] = (jax.nn.silu(gate) * up).astype(BF16)
    for n in range(0, model, step):
        answer = jnp.dot(act[...], down_ref[:, n : n + step], preferred_element_type=F32)
        answer = weight * answer.astype(BF16).astype(F32)
        out_ref[:, :, n : n + step] = answer.reshape(count // group, group, step).astype(BF16)


def gather_sum_kernel(parts_ref, shared_ref, out_ref):
    total = jnp.sum(parts_ref[...].astype(F32), axis=0) + shared_ref[...]
    for c in range(out_ref.shape[0]):
        out_ref[c] = total


def final_kernel(hidden_ref, terms_ref, out_ref):
    out_ref[...] = (hidden_ref[...] + jnp.sum(terms_ref[...], axis=0)).astype(BF16)


def spread(part, axis):
    copies = jnp.broadcast_to(part[None], (lax.axis_size(axis),) + part.shape)
    return lax.all_to_all(copies, axis, 0, 0)


def local(
    queries,
    latent_cache,
    token_latent,
    lengths,
    value_up_weight,
    out_proj,
    residual,
    norm_gain,
    router,
    expert_ids,
    expert_gate_up,
    expert_down,
    shared_gate_up,
    shared_down,
):
    ctx_index = lax.axis_index("ctx")
    ctx_count = lax.axis_size("ctx")
    batch_count = lax.axis_size("batch")
    batch_index = lax.axis_index("batch")
    _, rows, heads, width = queries.shape
    model = residual.shape[-1]
    experts = router.shape[1]
    total_rows = batch_count * rows
    shape = jax.ShapeDtypeStruct

    own_query = queries.reshape(rows * heads, width)
    every_query = spread(own_query, "ctx")
    start = (ctx_index * latent_cache.shape[2]).astype(jnp.int32)
    span = jnp.concatenate([lengths[0], start[None]])
    parts = call(
        attend_kernel,
        shape((ctx_count, rows * heads, width + 128), F32),
        [span, every_query, latent_cache[0]],
        [SMEM, VMEM, VMEM],
    )
    parts = lax.all_to_all(parts, "ctx", 0, 0)
    terms = call(
        project_kernel,
        shape((ctx_count, rows, model), F32),
        [parts, own_query, token_latent[0], value_up_weight, out_proj],
    )
    terms = lax.all_to_all(terms, "ctx", 0, 0)
    hidden, normed, copies = call(
        norm_kernel,
        (
            shape((rows, model), F32),
            shape((rows, model), BF16),
            shape((batch_count, rows, model), BF16),
        ),
        [terms, residual[0], norm_gain[None]],
    )

    every_rows = lax.all_to_all(copies, "batch", 0, 0).reshape(total_rows, model)
    all_picks = expert_ids.reshape(total_rows, -1)
    expert_range = jnp.arange(experts, dtype=jnp.int32)
    picked = jnp.any(all_picks[:, :, None] == expert_range[None, None, :], axis=1).astype(F32)
    own_expert = (ctx_index * batch_count + batch_index).astype(jnp.int32)[None]
    weighted = call(
        expert_kernel,
        shape((batch_count, rows, model), BF16),
        [own_expert, every_rows, picked, router, expert_gate_up[0], expert_down[0]],
        [SMEM] + [VMEM] * 5,
        scratch=[pltpu.VMEM((total_rows, expert_down.shape[1]), BF16)],
    )
    weighted = lax.all_to_all(weighted, "batch", 0, 0)
    shared_mid = jnp.einsum("rd,gdf->grf", normed, shared_gate_up, preferred_element_type=F32)
    shared_act = (jax.nn.silu(shared_mid[0]) * shared_mid[1]).astype(BF16)
    shared_part = jnp.dot(shared_act, shared_down, preferred_element_type=F32)
    totals = call(
        gather_sum_kernel, shape((ctx_count, rows, model), F32), [weighted, shared_part]
    )
    totals = lax.all_to_all(totals, "ctx", 0, 0)
    return call(final_kernel, shape((rows, model), BF16), [hidden, totals])[None]


def solution(mesh):
    return jax.shard_map(
        local,
        mesh=mesh,
        in_specs=(
            P("batch", None, "ctx", None),
            P("batch", None, "ctx", None),
            P("batch", None, None),
            P("batch", None),
            P("ctx", None, None),
            P("ctx", None),
            P("batch", None, None),
            P(),
            P(),
            P(),
            P(("ctx", "batch"), None, None),
            P(("ctx", "batch"), None, None),
            P(None, None, "ctx"),
            P("ctx", None),
        ),
        out_specs=P("batch", None, None),
        check_vma=False,
    )
```

time: 99.7 us -> 88.2 us (0.88)
  matrix products: 16.8 us -> 0.68 us
  other arithmetic: 10.5 us -> 0.91 us
  Pallas kernels: 0 us -> 8.6 us
  blocking collectives: 6.89 us -> 14.2 us
  local copies, waits for them, and re-layouts: 6.88 us -> 13.5 us
  starting transfers between devices: 29 us -> 24.5 us
  waiting for transfers between devices: 28.2 us -> 25 us
    all_to_all x3 -> x1, starting transfers between devices: 20.6 us -> 4.84 us  [spread(): return lax.all_to_all(copies, axis, 0, 0)]
    dot_general x8 -> x1, matrix products: 15.6 us -> 0.27 us  [local(): shared_part = jnp.dot(shared_act, shared_down, preferred_element_type=F32)]
    all_to_all x3 -> x1, waiting for transfers between devices: 15.7 us -> 3.75 us  [spread(): return lax.all_to_all(copies, axis, 0, 0)]
    all_to_all x2 -> x3, starting transfers between devices: 8.41 us -> 19.6 us  [the longest x1 12.6 us: local(): lax.all_to_all(copies, 'batch', 0, 0).reshape(total_rows, model)]
    unnamed x27, local copies, waits for them, and re-layouts: 0.15 us -> 10.9 us
    all_to_all x2 -> x3, waiting for transfers between devices: 12.5 us -> 21.2 us  [the longest x1 8.98 us: local(): lax.all_to_all(copies, 'batch', 0, 0).reshape(total_rows, model)]
    pallas_call x0 -> x6, Pallas kernels: none -> 8.6 us  [call(): pl.pallas_call(kernel, out_shape=out_shape, in_specs=specs or [VMEM] * le...]
    all_to_all x1 -> x2, blocking collectives: 6.89 us -> 14.2 us  [the longest x1 7.35 us: local(): parts = lax.all_to_all(parts, 'ctx', 0, 0)]
  transfers between devices with their start and end apart: 5 -> 4, of which waited for: 5 -> 4; matrix products, arithmetic and copies ran while one was open for 4% -> 2% of each run, Pallas kernels for 0% -> 0%
where the time goes in v2:
time: 88.2 us; the launch traced here: 87.5 us
  waiting for transfers between devices  25 us (28%)
  starting transfers between devices  24.5 us (28%)
  blocking collectives  14.2 us (16%)
  local copies, waits for them, and re-layouts  13.5 us (15%)
  Pallas kernels  8.6 us (10%)
  other arithmetic  0.91 us (1%)
    all_to_all x1, starting transfers between devices, local(): lax.all_to_all(copies, 'batch', 0, 0).reshape(total_rows, model)  12.6 us
    unnamed x27, local copies, waits for them, and re-layouts  10.9 us
    all_to_all x1, waiting for transfers between devices, local(): lax.all_to_all(copies, 'batch', 0, 0).reshape(total_rows, model)  8.98 us
    pallas_call x6, Pallas kernels, call(): pl.pallas_call(kernel, out_shape=out_shape, in_specs=specs or [VMEM] * le...  8.6 us
    all_to_all x1, waiting for transfers between devices, local(): weighted = lax.all_to_all(weighted, 'batch', 0, 0)  7.79 us
    all_to_all x1, blocking collectives, local(): parts = lax.all_to_all(parts, 'ctx', 0, 0)  7.35 us
    all_to_all x1, blocking collectives, local(): totals = lax.all_to_all(totals, 'ctx', 0, 0)  6.88 us
    all_to_all x1, starting transfers between devices, spread(): return lax.all_to_all(copies, axis, 0, 0)  4.84 us
  transfers between devices with their start and end apart: 4, of which 4 were waited for; matrix products, arithmetic and copies ran while one was open for 2% of the time, Pallas kernels for 0%

profile of v2, /device:TPU:1, one launch (start us, length us, event | category | flops | bytes accessed | tf_op | source)
XLA Modules:
  0.0 87.5 jit_solution(663722839248556794)
XLA Ops:
  0.0 1.5 %broadcast_in_dim.22 = bf16[4,16,512]{2,1,0:T(8,128)(2,1)} broadcast(bf16[16,512]{1,0:T(8,128)(2,1)} %bitcast.35), dimensions={1,2} | broadcast | bytes 81920 | tf_op jit(solution)/shard_map/broadcast_in_dim | solution.py:134
  1.5 4.8 %all-to-all-start = ((bf16[4,16,512]{2,1,0:T(8,128)(2,1)}), bf16[4,16,512]{2,1,0:T(8,128)(2,1)S(1)}, u32[]{:S(2)}, u32[]{:S(2)}) async-start(bf16[4,16,512]{2,1,0:T(8,128)(2,1)} %broadcast_in_dim.22), calls=%async_computation | async-start | bytes 131072 | tf_op jit(solution)/shard_map/all_to_all | solution.py:135
  6.4 0.7 pad_add_fusion.span_ref
  7.1 3.7 %all-to-all-done.q_ref = bf16[4,16,512]{2,1,0:T(8,128)(2,1)S(1)} async-done(((bf16[4,16,512]{2,1,0:T(8,128)(2,1)}), bf16[4,16,512]{2,1,0:T(8,128)(2,1)S(1)}, u32[]{:S(2)}, u32[]{:S(2)}) %all-to-all-start) | async-done | bytes 65568 | tf_op jit(solution)/shard_map/all_to_all | solution.py:135
  10.8 1.6 %copy-done.4 = bf16[1,2,1024,512]{3,2,1,0:T(8,128)(2,1)S(1)} copy-done((bf16[1,2,1024,512]{3,2,1,0:T(8,128)(2,1)S(1)}, bf16[1,2,1024,512]{3,2,1,0:T(8,128)(2,1)}, u32[]{:S(2)}) %copy-start.4) | copy-done | bytes 2097176
  12.4 1.9 %shard_map.136 = f32[4,16,640]{2,1,0:T(8,128)S(1)} custom-call(s32[3]{0:T(128)S(1)} %pad_add_fusion.span_ref, bf16[4,16,512]{2,1,0:T(8,128)(2,1)S(1)} %all-to-all-done.q_ref, bf16[2,1024,512]{2,1,0:T(8,128)(2,1)S(1)} %bitcast.34), custom_call_target="tpu_custom_call" | custom-call | tf_op jit(solution)/shard_map/pallas_call | solution.py:19
  14.4 7.4 %all_to_all.30.parts_ref = f32[4,16,640]{2,1,0:T(8,128)S(1)} all-to-all(f32[4,16,640]{2,1,0:T(8,128)S(1)} %shard_map.136), channel_id=1, replica_groups=mesh['ctx'=4,'batch'=32] {'ctx'}, dimensions={0} | all-to-all | bytes 327680 | tf_op jit(solution)/shard_map/all_to_all | solution.py:174
  21.7 2.3 %copy-done.3 = bf16[1024,2304]{1,0:T(8,128)(2,1)S(1)} copy-done((bf16[1024,2304]{1,0:T(8,128)(2,1)S(1)}, bf16[1024,2304]{1,0:T(8,128)(2,1)}, u32[]{:S(2)}) %copy-start.3) | copy-done | bytes 4718616
  24.1 1.8 %shard_map.137 = f32[4,2,2304]{2,1,0:T(2,128)} custom-call(f32[4,16,640]{2,1,0:T(8,128)S(1)} %all_to_all.30.parts_ref, bf16[16,512]{1,0:T(8,128)(2,1)S(1)} %bitcast.36, bf16[2,512]{1,0:T(2,128)(2,1)S(1)} %bitcast.38, bf16[8,512,128]{2,1,0:T(8,128)(2,1)S(1)} %copy-done.5, bf16[1024,2304]{1,0:T(8,128)(2,1)S(1)} %copy-done.3), custom_call_target="tpu_custom_call" | custom-call | tf_op jit(solution)/shard_map/pallas_call | solution.py:19
  25.9 3.3 %all-to-all-start.2 = ((f32[4,2,2304]{2,1,0:T(2,128)}), f32[4,2,2304]{2,1,0:T(2,128)S(1)}, u32[]{:S(2)}, u32[]{:S(2)}) async-start(f32[4,2,2304]{2,1,0:T(2,128)} %shard_map.137), calls=%async_computation.2 | async-start | bytes 147456 | tf_op jit(solution)/shard_map/all_to_all | solution.py:180
  29.2 4.5 %all-to-all-done.2.terms_ref = f32[4,2,2304]{2,1,0:T(2,128)S(1)} async-done(((f32[4,2,2304]{2,1,0:T(2,128)}), f32[4,2,2304]{2,1,0:T(2,128)S(1)}, u32[]{:S(2)}, u32[]{:S(2)}) %all-to-all-start.2) | async-done | bytes 73760 | tf_op jit(solution)/shard_map/all_to_all | solution.py:180
  33.7 0.9 %shard_map.138 = (f32[2,2304]{1,0:T(2,128)S(1)}, bf16[2,2304]{1,0:T(2,128)(2,1)S(1)}, bf16[32,2,2304]{2,1,0:T(2,128)(2,1)}) custom-call(f32[4,2,2304]{2,1,0:T(2,128)S(1)} %all-to-all-done.2.terms_ref, bf16[2,2304]{1,0:T(2,128)(2,1)S(1)} %bitcast.37, bf16[1,2304]{1,0:T(2,128)(2,1)S(1)} %broadcast_in_dim.23.gain_ref), custom_call_target="tpu_custom_call" | custom-call | tf_op jit(solution)/shard_map/pallas_call | solution.py:19
  34.6 12.6 %all-to-all-start.3 = ((bf16[32,2,2304]{2,1,0:T(2,128)(2,1)}), bf16[32,2,2304]{2,1,0:T(2,128)(2,1)}, u32[]{:S(2)}, u32[]{:S(2)}) async-start(bf16[32,2,2304]{2,1,0:T(2,128)(2,1)} %get-tuple-element.9), calls=%async_computation.3 | async-start | bytes 589824 | tf_op jit(solution)/shard_map/all_to_all | solution.py:191
  47.4 9.0 %all-to-all-done.3 = bf16[32,2,2304]{2,1,0:T(2,128)(2,1)} async-done(((bf16[32,2,2304]{2,1,0:T(2,128)(2,1)}), bf16[32,2,2304]{2,1,0:T(2,128)(2,1)}, u32[]{:S(2)}, u32[]{:S(2)}) %all-to-all-start.3) | async-done | bytes 294944 | tf_op jit(solution)/shard_map/all_to_all | solution.py:191
  56.4 1.1 %reshape.6.rows_ref = bf16[64,2304]{1,0:T(8,128)(2,1)S(1)} reshape(bf16[32,2,2304]{2,1,0:T(2,128)(2,1)} %all-to-all-done.3) | data formatting | bytes 589824 | tf_op jit(solution)/shard_map/reshape | solution.py:191
  57.5 3.7 %copy-done.1 = bf16[1,2304,2048]{2,1,0:T(8,128)(2,1)S(1)} copy-done((bf16[1,2304,2048]{2,1,0:T(8,128)(2,1)S(1)}, bf16[1,2304,2048]{2,1,0:T(8,128)(2,1)}, u32[]{:S(2)}) %copy-start.1) | copy-done | bytes 9437208
  61.2 2.3 %copy-done.2 = bf16[1,1024,2304]{2,1,0:T(8,128)(2,1)S(1)} copy-done((bf16[1,1024,2304]{2,1,0:T(8,128)(2,1)S(1)}, bf16[1,1024,2304]{2,1,0:T(8,128)(2,1)}, u32[]{:S(2)}) %copy-start.2) | copy-done | bytes 4718616
  63.5 3.0 %shard_map.139 = bf16[32,2,2304]{2,1,0:T(2,128)(2,1)} custom-call(s32[1]{0:T(128)} %bitcast.6.own_ref, bf16[64,2304]{1,0:T(8,128)(2,1)S(1)} %reshape.6.rows_ref, f32[64,128]{1,0:T(8,128)S(1)} %convert_element_type.6.picked_ref, bf16[2304,128]{1,0:T(8,128)(2,1)S(1)} %copy-done.6, bf16[2304,2048]{1,0:T(8,128)(2,1)S(1)} %bitcast.32, bf16[1024,2304]{1,0:T(8,128)(2,1)S(1)} %bitcast.33), custom_call_target="tpu_custom_call" | custom-call | tf_op jit(solution)/shard_map/pallas_call | solution.py:19
  66.5 3.8 %all-to-all-start.4 = ((bf16[32,2,2304]{2,1,0:T(2,128)(2,1)}), bf16[32,2,2304]{2,1,0:T(2,128)(2,1)S(1)}, u32[]{:S(2)}, u32[]{:S(2)}) async-start(bf16[32,2,2304]{2,1,0:T(2,128)(2,1)} %shard_map.139), calls=%async_computation.4 | async-start | bytes 589824 | tf_op jit(solution)/shard_map/all_to_all | solution.py:203
  70.4 0.4 convolution_bitcast_fusion
  70.8 0.8 copy-done.10
  71.9 7.8 %all-to-all-done.4.parts_ref = bf16[32,2,2304]{2,1,0:T(2,128)(2,1)S(1)} async-done(((bf16[32,2,2304]{2,1,0:T(2,128)(2,1)}), bf16[32,2,2304]{2,1,0:T(2,128)(2,1)S(1)}, u32[]{:S(2)}, u32[]{:S(2)}) %all-to-all-start.4) | async-done | bytes 294944 | tf_op jit(solution)/shard_map/all_to_all | solution.py:203
  80.0 6.9 %all_to_all.31.terms_ref = f32[4,2,2304]{2,1,0:T(2,128)S(1)} all-to-all(f32[4,2,2304]{2,1,0:T(2,128)S(1)} %shard_map.140), channel_id=1, replica_groups=mesh['ctx'=4,'batch'=32] {'ctx'}, dimensions={0} | all-to-all | bytes 147456 | tf_op jit(solution)/shard_map/all_to_all | solution.py:210
  86.8 0.6 shard_map.141
  (27 shorter events, 0.9 us)
Async XLA Ops:
  0.0 70.4 %copy-start = (bf16[2,2304,256]{2,1,0:T(8,128)(2,1)S(1)}, bf16[2,2304,256]{2,1,0:T(8,128)(2,1)}, u32[]{:S(2)}) copy-start(bf16[2,2304,256]{2,1,0:T(8,128)(2,1)} %param.26) | copy-start | bytes 7077892
  0.0 21.7 %copy-start.7 = (bf16[1,2,8,512]{3,2,1,0:T(8,128)(2,1)S(1)}, bf16[1,2,8,512]{3,2,1,0:T(8,128)(2,1)}, u32[]{:S(2)}) copy-start(bf16[1,2,8,512]{3,2,1,0:T(8,128)(2,1)} %param.14) | copy-start | bytes 49156
  0.0 21.7 %copy-start.9 = (bf16[1,2,512]{2,1,0:T(2,128)(2,1)S(1)}, bf16[1,2,512]{2,1,0:T(2,128)(2,1)}, u32[]{:S(2)}) copy-start(bf16[1,2,512]{2,1,0:T(2,128)(2,1)} %param.16) | copy-start | bytes 6148
  1.5 9.3 %all-to-all-start = ((bf16[4,16,512]{2,1,0:T(8,128)(2,1)}), bf16[4,16,512]{2,1,0:T(8,128)(2,1)S(1)}, u32[]{:S(2)}, u32[]{:S(2)}) async-start(bf16[4,16,512]{2,1,0:T(8,128)(2,1)} %broadcast_in_dim.22), calls=%async_computation | async-start | bytes 131072 | tf_op jit(solution)/shard_map/all_to_all | solution.py:135
  10.8 1.6 %copy-start.4 = (bf16[1,2,1024,512]{3,2,1,0:T(8,128)(2,1)S(1)}, bf16[1,2,1024,512]{3,2,1,0:T(8,128)(2,1)}, u32[]{:S(2)}) copy-start(bf16[1,2,1024,512]{3,2,1,0:T(8,128)(2,1)} %param.15) | copy-start | bytes 6291460
  12.4 9.3 %copy-start.5 = (bf16[8,512,128]{2,1,0:T(8,128)(2,1)S(1)}, bf16[8,512,128]{2,1,0:T(8,128)(2,1)}, u32[]{:S(2)}) copy-start(bf16[8,512,128]{2,1,0:T(8,128)(2,1)} %up_ref.1) | copy-start | bytes 3145732
  21.7 2.3 %copy-start.3 = (bf16[1024,2304]{1,0:T(8,128)(2,1)S(1)}, bf16[1024,2304]{1,0:T(8,128)(2,1)}, u32[]{:S(2)}) copy-start(bf16[1024,2304]{1,0:T(8,128)(2,1)} %proj_ref.1) | copy-start | bytes 14155780
  24.1 5.1 %copy-start.12 = (bf16[2304]{0:T(1024)(128)(2,1)S(1)}, bf16[2304]{0:T(1024)(128)(2,1)}, u32[]{:S(2)}) copy-start(bf16[2304]{0:T(1024)(128)(2,1)} %param.21) | copy-start | bytes 13828
  24.1 9.6 %copy-start.8 = (bf16[1,2,2304]{2,1,0:T(2,128)(2,1)S(1)}, bf16[1,2,2304]{2,1,0:T(2,128)(2,1)}, u32[]{:S(2)}) copy-start(bf16[1,2,2304]{2,1,0:T(2,128)(2,1)} %param.20) | copy-start | bytes 27652
  24.1 23.0 %copy-start.11 = (s32[32,2,8]{0,2,1:T(8,128)S(1)}, s32[32,2,8]{0,2,1:T(8,128)}, u32[]{:S(2)}) copy-start(s32[32,2,8]{0,2,1:T(8,128)} %param.23) | copy-start | bytes 6148
  24.1 33.4 %copy-start.6 = (bf16[2304,128]{1,0:T(8,128)(2,1)S(1)}, bf16[2304,128]{1,0:T(8,128)(2,1)}, u32[]{:S(2)}) copy-start(bf16[2304,128]{1,0:T(8,128)(2,1)} %router_ref.1) | copy-start | bytes 1769476
  25.9 7.8 %all-to-all-start.2 = ((f32[4,2,2304]{2,1,0:T(2,128)}), f32[4,2,2304]{2,1,0:T(2,128)S(1)}, u32[]{:S(2)}, u32[]{:S(2)}) async-start(f32[4,2,2304]{2,1,0:T(2,128)} %shard_map.137), calls=%async_computation.2 | async-start | bytes 147456 | tf_op jit(solution)/shard_map/all_to_all | solution.py:180
  34.6 21.8 %all-to-all-start.3 = ((bf16[32,2,2304]{2,1,0:T(2,128)(2,1)}), bf16[32,2,2304]{2,1,0:T(2,128)(2,1)}, u32[]{:S(2)}, u32[]{:S(2)}) async-start(bf16[32,2,2304]{2,1,0:T(2,128)(2,1)} %get-tuple-element.9), calls=%async_computation.3 | async-start | bytes 589824 | tf_op jit(solution)/shard_map/all_to_all | solution.py:191
  57.5 3.7 %copy-start.1 = (bf16[1,2304,2048]{2,1,0:T(8,128)(2,1)S(1)}, bf16[1,2304,2048]{2,1,0:T(8,128)(2,1)}, u32[]{:S(2)}) copy-start(bf16[1,2304,2048]{2,1,0:T(8,128)(2,1)} %param.24) | copy-start | bytes 28311556
  61.2 2.3 %copy-start.2 = (bf16[1,1024,2304]{2,1,0:T(8,128)(2,1)S(1)}, bf16[1,1024,2304]{2,1,0:T(8,128)(2,1)}, u32[]{:S(2)}) copy-start(bf16[1,1024,2304]{2,1,0:T(8,128)(2,1)} %param.25) | copy-start | bytes 14155780
  66.5 13.1 %all-to-all-start.4 = ((bf16[32,2,2304]{2,1,0:T(2,128)(2,1)}), bf16[32,2,2304]{2,1,0:T(2,128)(2,1)S(1)}, u32[]{:S(2)}, u32[]{:S(2)}) async-start(bf16[32,2,2304]{2,1,0:T(2,128)(2,1)} %shard_map.139), calls=%async_computation.4 | async-start | bytes 589824 | tf_op jit(solution)/shard_map/all_to_all | solution.py:203
  70.3 1.3 %copy-start.10 = (bf16[256,2304]{1,0:T(8,128)(2,1)S(1)}, bf16[256,2304]{1,0:T(8,128)(2,1)}, u32[]{:S(2)}) copy-start(bf16[256,2304]{1,0:T(8,128)(2,1)} %param.27) | copy-start | bytes 3538948

commit v3 on v2

--- a/solution.py
+++ b/solution.py
@@ -10,24 +10,37 @@
 ROUTE_SCALE = 2.446
 EPSILON = 1e-06
 SCALE = QK ** (-0.5)
+LIMIT = 8 << 20
 BF16, F32 = jnp.bfloat16, jnp.float32
 VMEM = pl.BlockSpec(memory_space=pltpu.VMEM)
+HBM = pl.BlockSpec(memory_space=pltpu.HBM)
 SMEM = pl.BlockSpec(memory_space=pltpu.SMEM)
 
 
-def call(kernel, out_shape, args, specs=None, limit=16 << 20, scratch=(), cost=None):
+def call(kernel, out_shape, args, specs=None, limit=LIMIT, scratch=(), beside=()):
+    beside = [pltpu.with_memory_space_constraint(array, pltpu.HBM) for array in beside]
+    count = len(args)
+
+    def body(*refs):
+        kernel(*refs[:count], *refs[count + len(beside) :])
+
     return pl.pallas_call(
-        kernel,
+        body,
         out_shape=out_shape,
-        in_specs=specs or [VMEM] * len(args),
+        in_specs=(specs or [VMEM] * count) + [HBM] * len(beside),
         out_specs=jax.tree.map(lambda _: VMEM, out_shape),
         scratch_shapes=list(scratch),
         compiler_params=pltpu.CompilerParams(vmem_limit_bytes=limit),
-        cost_estimate=cost,
-    )(*args)
-
-
-def attend_kernel(span_ref, q_ref, cache_ref, out_ref):
+    )(*args, *beside)
+
+
+def copies_kernel(part_ref, out_ref):
+    for c in range(out_ref.shape[0]):
+        out_ref[c] = part_ref[...]
+
+
+def attend_kernel(span_ref, q_ref, cache_ref, picked_ref, out_ref, kept_ref):
+    kept_ref[...] = picked_ref[...]
     rows, span, width = cache_ref.shape
     parts = q_ref.shape[0]
     heads = q_ref.shape[1] // rows
@@ -92,7 +105,7 @@
 def norm_kernel(terms_ref, residual_ref, gain_ref, hidden_ref, normed_ref, copies_ref):
     hidden = residual_ref[...].astype(F32) + jnp.sum(terms_ref[...], axis=0)
     inverse = lax.rsqrt(jnp.mean(hidden * hidden, axis=-1, keepdims=True) + EPSILON)
-    normed = (hidden * inverse * gain_ref[...].astype(F32)).astype(BF16)
+    normed = (hidden * inverse * gain_ref[...].astype(F32)[None]).astype(BF16)
     hidden_ref[...] = hidden
     normed_ref[...] = normed
     for b in range(copies_ref.shape[0]):
@@ -100,14 +113,14 @@
 
 
 def expert_kernel(own_ref, rows_ref, picked_ref, router_ref, gate_up_ref, down_ref, out_ref, act):
-    rows = rows_ref[...]
-    count = rows.shape[0]
+    count = act.shape[0]
+    rows = rows_ref[...].astype(F32).reshape(count, rows_ref.shape[2]).astype(BF16)
     group = out_ref.shape[1]
     width, model = down_ref.shape
     logits = jnp.dot(rows, router_ref[...], preferred_element_type=F32)
     score = jnp.where(picked_ref[...] > 0, jax.nn.sigmoid(logits), 0.0)
     expert = lax.broadcasted_iota(jnp.int32, score.shape, 1)
-    own = jnp.sum(jnp.where(expert == own_ref[0], score, 0.0), axis=-1, keepdims=True)
+    own = jnp.sum(jnp.where(expert == own_ref[own_ref.shape[0] - 1], score, 0.0), axis=-1, keepdims=True)
     weight = (ROUTE_SCALE * own / jnp.sum(score, axis=-1, keepdims=True)).astype(BF16).astype(F32)
     step = 256
     for n in range(0, width, step):
@@ -120,6 +133,22 @@
         out_ref[:, :, n : n + step] = answer.reshape(count // group, group, step).astype(BF16)
 
 
+def shared_kernel(normed_ref, gate_up_ref, down_ref, out_ref, gate_up, down, sems):
+    first = pltpu.make_async_copy(gate_up_ref, gate_up, sems.at[0])
+    second = pltpu.make_async_copy(down_ref, down, sems.at[1])
+    first.start()
+    second.start()
+    rows, model = normed_ref.shape
+    normed = jnp.broadcast_to(normed_ref[...].astype(F32)[None], (8 // rows, rows, model))
+    normed = normed.reshape(8, model).astype(BF16)
+    first.wait()
+    gate = jnp.dot(normed, gate_up[0], preferred_element_type=F32)
+    up = jnp.dot(normed, gate_up[1], preferred_element_type=F32)
+    act = (jax.nn.silu(gate) * up).astype(BF16)
+    second.wait()
+    out_ref[...] = jnp.dot(act, down[...], preferred_element_type=F32)[:rows]
+
+
 def gather_sum_kernel(parts_ref, shared_ref, out_ref):
     total = jnp.sum(parts_ref[...].astype(F32), axis=0) + shared_ref[...]
     for c in range(out_ref.shape[0]):
@@ -128,11 +157,6 @@
 
 def final_kernel(hidden_ref, terms_ref, out_ref):
     out_ref[...] = (hidden_ref[...] + jnp.sum(terms_ref[...], axis=0)).astype(BF16)
-
-
-def spread(part, axis):
-    copies = jnp.broadcast_to(part[None], (lax.axis_size(axis),) + part.shape)
-    return lax.all_to_all(copies, axis, 0, 0)
 
 
 def local(
@@ -162,14 +186,28 @@
     shape = jax.ShapeDtypeStruct
 
     own_query = queries.reshape(rows * heads, width)
-    every_query = spread(own_query, "ctx")
-    start = (ctx_index * latent_cache.shape[2]).astype(jnp.int32)
-    span = jnp.concatenate([lengths[0], start[None]])
-    parts = call(
+    copies = call(
+        copies_kernel,
+        shape((ctx_count, rows * heads, width), BF16),
+        [own_query],
+        beside=[expert_down],
+    )
+    every_query = lax.all_to_all(copies, "ctx", 0, 0)
+    start = ctx_index * latent_cache.shape[2]
+    own_expert = ctx_index * batch_count + batch_index
+    span = jnp.concatenate([lengths[0], jnp.stack([start, own_expert]).astype(jnp.int32)])
+    all_picks = expert_ids.reshape(total_rows, -1)
+    expert_range = jnp.arange(experts, dtype=jnp.int32)
+    picked = jnp.any(all_picks[:, :, None] == expert_range[None, None, :], axis=1).astype(F32)
+    parts, picked = call(
         attend_kernel,
-        shape((ctx_count, rows * heads, width + 128), F32),
-        [span, every_query, latent_cache[0]],
-        [SMEM, VMEM, VMEM],
+        (
+            shape((ctx_count, rows * heads, width + 128), F32),
+            shape((total_rows, experts), F32),
+        ),
+        [span, every_query, latent_cache[0], picked],
+        [SMEM, VMEM, VMEM, VMEM],
+        beside=[expert_gate_up] * 3,
     )
     parts = lax.all_to_all(parts, "ctx", 0, 0)
     terms = call(
@@ -185,25 +223,34 @@
             shape((rows, model), BF16),
             shape((batch_count, rows, model), BF16),
         ),
-        [terms, residual[0], norm_gain[None]],
-    )
-
-    every_rows = lax.all_to_all(copies, "batch", 0, 0).reshape(total_rows, model)
-    all_picks = expert_ids.reshape(total_rows, -1)
-    expert_range = jnp.arange(experts, dtype=jnp.int32)
-    picked = jnp.any(all_picks[:, :, None] == expert_range[None, None, :], axis=1).astype(F32)
-    own_expert = (ctx_index * batch_count + batch_index).astype(jnp.int32)[None]
+        [terms, residual[0], norm_gain],
+        beside=[expert_gate_up] * 4,
+    )
+
+    every_rows = lax.all_to_all(copies, "batch", 0, 0)
     weighted = call(
         expert_kernel,
         shape((batch_count, rows, model), BF16),
-        [own_expert, every_rows, picked, router, expert_gate_up[0], expert_down[0]],
+        [span, every_rows, picked, router, expert_gate_up[0], expert_down[0]],
         [SMEM] + [VMEM] * 5,
         scratch=[pltpu.VMEM((total_rows, expert_down.shape[1]), BF16)],
     )
     weighted = lax.all_to_all(weighted, "batch", 0, 0)
-    shared_mid = jnp.einsum("rd,gdf->grf", normed, shared_gate_up, preferred_element_type=F32)
-    shared_act = (jax.nn.silu(shared_mid[0]) * shared_mid[1]).astype(BF16)
-    shared_part = jnp.dot(shared_act, shared_down, preferred_element_type=F32)
+    shared_part = call(
+        shared_kernel,
+        shape((rows, model), F32),
+        [
+            normed,
+            pltpu.with_memory_space_constraint(shared_gate_up, pltpu.HBM),
+            pltpu.with_memory_space_constraint(shared_down, pltpu.HBM),
+        ],
+        [VMEM, HBM, HBM],
+        scratch=[
+            pltpu.VMEM(shared_gate_up.shape, BF16),
+            pltpu.VMEM(shared_down.shape, BF16),
+            pltpu.SemaphoreType.DMA((2,)),
+        ],
+    )
     totals = call(
         gather_sum_kernel, shape((ctx_count, rows, model), F32), [weighted, shared_part]
     )

time: 88.2 us -> 75.7 us (0.86)
  blocking collectives: 14.2 us -> 43.2 us
  starting transfers between devices: 24.5 us -> 8.64 us
  waiting for transfers between devices: 25 us -> 11 us
  local copies, waits for them, and re-layouts: 13.5 us -> 1.03 us
  Pallas kernels: 8.6 us -> 10.8 us
    all_to_all x0 -> x2, blocking collectives: none -> 28.8 us  [the longest x1 21.8 us: local(): every_rows = lax.all_to_all(copies, 'batch', 0, 0)]
    all_to_all x3 -> x1, starting transfers between devices: 20.7 us -> 4.84 us  [local(): every_query = lax.all_to_all(copies, 'ctx', 0, 0)]
    all_to_all x3 -> x1, waiting for transfers between devices: 17.2 us -> 4.12 us  [local(): every_query = lax.all_to_all(copies, 'ctx', 0, 0)]
    unnamed x27 -> x35, local copies, waits for them, and re-layouts: 10.9 us -> 1.03 us
    pallas_call x6 -> x8, Pallas kernels: 8.6 us -> 10.8 us  [call(): pl.pallas_call(body, out_shape=out_shape, in_specs=(specs or [VMEM] * cou...]
    broadcast_in_dim x2 -> x0, local copies, waits for them, and re-layouts: 1.51 us -> none  [the longest x1 1.5 us: spread(): copies = jnp.broadcast_to(part[None], (lax.axis_size(axis),) + part.shape)]
    reshape x1 -> x0, local copies, waits for them, and re-layouts: 1.07 us -> none  [local(): lax.all_to_all(copies, 'batch', 0, 0).reshape(total_rows, model)]
  transfers between devices with their start and end apart: 4 -> 2, of which waited for: 4 -> 2; matrix products, arithmetic and copies ran while one was open for 2% -> 0% of each run, Pallas kernels for 0% -> 3%
where the time goes in v3:
time: 75.7 us; the launch traced here: 75.1 us
  blocking collectives  43.2 us (57%)
  waiting for transfers between devices  11 us (15%)
  Pallas kernels  10.8 us (14%)
  starting transfers between devices  8.64 us (11%)
  local copies, waits for them, and re-layouts  1.03 us (1%)
    all_to_all x1, blocking collectives, local(): every_rows = lax.all_to_all(copies, 'batch', 0, 0)  21.8 us
    pallas_call x8, Pallas kernels, call(): pl.pallas_call(body, out_shape=out_shape, in_specs=(specs or [VMEM] * cou...  10.8 us
    all_to_all x1, blocking collectives, local(): parts = lax.all_to_all(parts, 'ctx', 0, 0)  7.49 us
    all_to_all x1, blocking collectives, local(): terms = lax.all_to_all(terms, 'ctx', 0, 0)  7.02 us
    all_to_all x1, waiting for transfers between devices, local(): weighted = lax.all_to_all(weighted, 'batch', 0, 0)  6.92 us
    all_to_all x1, blocking collectives, local(): totals = lax.all_to_all(totals, 'ctx', 0, 0)  6.88 us
    all_to_all x1, starting transfers between devices, local(): every_query = lax.all_to_all(copies, 'ctx', 0, 0)  4.84 us
    all_to_all x1, waiting for transfers between devices, local(): every_query = lax.all_to_all(copies, 'ctx', 0, 0)  4.12 us
  transfers between devices with their start and end apart: 2, of which 2 were waited for; matrix products, arithmetic and copies ran while one was open for 0% of the time, Pallas kernels for 3%

profile of v3, /device:TPU:1, one launch (start us, length us, event | category | flops | bytes accessed | tf_op | source)
XLA Modules:
  0.0 75.1 jit_solution(3730760674006556049)
XLA Ops:
  0.0 0.9 %copy-done.3 = bf16[1,2,8,512]{3,2,1,0:T(8,128)(2,1)S(1)} copy-done((bf16[1,2,8,512]{3,2,1,0:T(8,128)(2,1)S(1)}, bf16[1,2,8,512]{3,2,1,0:T(8,128)(2,1)}, u32[]{:S(2)}) %copy-start.3) | copy-done | bytes 16408
  0.9 0.6 shard_map.136
  1.5 4.8 %all-to-all-start = ((bf16[4,16,512]{2,1,0:T(8,128)(2,1)}), bf16[4,16,512]{2,1,0:T(8,128)(2,1)S(1)}, u32[]{:S(2)}, u32[]{:S(2)}) async-start(bf16[4,16,512]{2,1,0:T(8,128)(2,1)} %shard_map.136), calls=%async_computation | async-start | bytes 131072 | tf_op jit(solution)/shard_map/all_to_all | solution.py:195
  6.3 0.1 copy.16
  6.4 0.2 fusion
  6.6 0.1 pad_add_fusion.refs_0_
  6.7 4.1 %all-to-all-done.refs_1_ = bf16[4,16,512]{2,1,0:T(8,128)(2,1)S(1)} async-done(((bf16[4,16,512]{2,1,0:T(8,128)(2,1)}), bf16[4,16,512]{2,1,0:T(8,128)(2,1)S(1)}, u32[]{:S(2)}, u32[]{:S(2)}) %all-to-all-start) | async-done | bytes 65568 | tf_op jit(solution)/shard_map/all_to_all | solution.py:195
  10.8 0.0 copy-start.7
  10.8 2.0 %shard_map.137 = (f32[4,16,640]{2,1,0:T(8,128)S(1)}, f32[64,128]{1,0:T(8,128)S(1)}) custom-call(s32[4]{0:T(128)S(1)} %pad_add_fusion.refs_0_, bf16[4,16,512]{2,1,0:T(8,128)(2,1)S(1)} %all-to-all-done.refs_1_, bf16[2,1024,512]{2,1,0:T(8,128)(2,1)S(1)} %bitcast.19, f32[64,128]{1,0:T(8,128)S(1)} %convert_element_type.3.refs_3_, bf16[1,2304,2048]{2,1,0:T(8,128)(2,1)} %refs_6_.3, ...), custom_call_target="tpu_custom_call" | custom-call | tf_op jit(solution)/shard_map/pallas_call | solution.py:27
  12.8 0.0 copy-start.6
  12.8 7.5 %all_to_all.30.refs_0_ = f32[4,16,640]{2,1,0:T(8,128)S(1)} all-to-all(f32[4,16,640]{2,1,0:T(8,128)S(1)} %get-tuple-element.10), channel_id=1, replica_groups=mesh['ctx'=4,'batch'=32] {'ctx'}, dimensions={0} | all-to-all | bytes 327680 | tf_op jit(solution)/shard_map/all_to_all | solution.py:212
  20.3 0.0 slice-start.3
  20.4 1.2 %shard_map.138 = f32[4,2,2304]{2,1,0:T(2,128)S(1)} custom-call(f32[4,16,640]{2,1,0:T(8,128)S(1)} %all_to_all.30.refs_0_, bf16[16,512]{1,0:T(8,128)(2,1)S(1)} %bitcast.21, bf16[2,512]{1,0:T(2,128)(2,1)S(1)} %bitcast.23, bf16[8,512,128]{2,1,0:T(8,128)(2,1)S(1)} %copy-done.1, bf16[1024,2304]{1,0:T(8,128)(2,1)S(1)} %bitcast.18), custom_call_target="tpu_custom_call" | custom-call | tf_op jit(solution)/shard_map/pallas_call | solution.py:27
  21.5 7.0 %all_to_all.31.refs_0_ = f32[4,2,2304]{2,1,0:T(2,128)S(1)} all-to-all(f32[4,2,2304]{2,1,0:T(2,128)S(1)} %shard_map.138), channel_id=1, replica_groups=mesh['ctx'=4,'batch'=32] {'ctx'}, dimensions={0} | all-to-all | bytes 147456 | tf_op jit(solution)/shard_map/all_to_all | solution.py:218
  28.6 0.0 slice-start.4
  28.6 0.2 shard_map.139
  28.8 21.8 %all_to_all.32.refs_1_ = bf16[32,2,2304]{2,1,0:T(2,128)(2,1)S(1)} all-to-all(bf16[32,2,2304]{2,1,0:T(2,128)(2,1)S(1)} %get-tuple-element.12), channel_id=1, replica_groups=mesh['ctx'=4,'batch'=32] {'batch'}, dimensions={0} | all-to-all | bytes 589824 | tf_op jit(solution)/shard_map/all_to_all | solution.py:230
  50.6 3.6 %shard_map.140 = bf16[32,2,2304]{2,1,0:T(2,128)(2,1)} custom-call(s32[4]{0:T(128)S(1)} %pad_add_fusion.refs_0_, bf16[32,2,2304]{2,1,0:T(2,128)(2,1)S(1)} %all_to_all.32.refs_1_, f32[64,128]{1,0:T(8,128)S(1)} %get-tuple-element.13.refs_2_, bf16[2304,128]{1,0:T(8,128)(2,1)S(1)} %copy-done.2, bf16[2304,2048]{1,0:T(8,128)(2,1)S(1)} %bitcast.13, ...), custom_call_target="tpu_custom_call" | custom-call | tf_op jit(solution)/shard_map/pallas_call | solution.py:27
  54.2 3.8 %all-to-all-start.4 = ((bf16[32,2,2304]{2,1,0:T(2,128)(2,1)}), bf16[32,2,2304]{2,1,0:T(2,128)(2,1)S(1)}, u32[]{:S(2)}, u32[]{:S(2)}) async-start(bf16[32,2,2304]{2,1,0:T(2,128)(2,1)} %shard_map.140), calls=%async_computation.4 | async-start | bytes 589824 | tf_op jit(solution)/shard_map/all_to_all | solution.py:238
  58.0 2.4 %shard_map.141.refs_1_ = f32[2,2304]{1,0:T(2,128)S(1)} custom-call(bf16[2,2304]{1,0:T(2,128)(2,1)S(1)} %get-tuple-element.14.refs_0_, bf16[2,2304,256]{2,1,0:T(8,128)(2,1)} %refs_1_.3, bf16[256,2304]{1,0:T(8,128)(2,1)} %refs_2_.3), custom_call_target="tpu_custom_call" | custom-call | tf_op jit(solution)/shard_map/pallas_call | solution.py:27
  60.4 6.9 %all-to-all-done.4.refs_0_ = bf16[32,2,2304]{2,1,0:T(2,128)(2,1)S(1)} async-done(((bf16[32,2,2304]{2,1,0:T(2,128)(2,1)}), bf16[32,2,2304]{2,1,0:T(2,128)(2,1)S(1)}, u32[]{:S(2)}, u32[]{:S(2)}) %all-to-all-start.4) | async-done | bytes 294944 | tf_op jit(solution)/shard_map/all_to_all | solution.py:238
  67.3 0.3 shard_map.142
  67.6 6.9 %all_to_all.33.refs_1_ = f32[4,2,2304]{2,1,0:T(2,128)S(1)} all-to-all(f32[4,2,2304]{2,1,0:T(2,128)S(1)} %shard_map.142), channel_id=1, replica_groups=mesh['ctx'=4,'batch'=32] {'ctx'}, dimensions={0} | all-to-all | bytes 147456 | tf_op jit(solution)/shard_map/all_to_all | solution.py:257
  74.5 0.6 shard_map.143
  (33 shorter events, 0.1 us)
Async XLA Ops:
  0.0 10.8 %copy-start = (bf16[1,2,1024,512]{3,2,1,0:T(8,128)(2,1)S(1)}, bf16[1,2,1024,512]{3,2,1,0:T(8,128)(2,1)}, u32[]{:S(2)}) copy-start(bf16[1,2,1024,512]{3,2,1,0:T(8,128)(2,1)} %param.15) | copy-start | bytes 6291460
  0.0 0.9 %copy-start.3 = (bf16[1,2,8,512]{3,2,1,0:T(8,128)(2,1)S(1)}, bf16[1,2,8,512]{3,2,1,0:T(8,128)(2,1)}, u32[]{:S(2)}) copy-start(bf16[1,2,8,512]{3,2,1,0:T(8,128)(2,1)} %param.14) | copy-start | bytes 49156
  0.9 5.5 %copy-start.8 = (s32[32,2,8]{0,2,1:T(8,128)S(1)}, s32[32,2,8]{0,2,1:T(8,128)}, u32[]{:S(2)}) copy-start(s32[32,2,8]{0,2,1:T(8,128)} %param.23) | copy-start | bytes 6148
  0.9 5.7 %copy-start.9 = (s32[1,2]{1,0:T(1,128)S(1)}, s32[1,2]{1,0:T(1,128)}, u32[]{:S(2)}) copy-start(s32[1,2]{1,0:T(1,128)} %param.17) | copy-start | bytes 28
  0.9 19.4 %slice-start.5 = ((s8[4718592]{0:T(1024)(128)(4,1)}), s8[524288]{0:T(1024)(128)(4,1)S(1)}, s32[]{:S(2)}) async-start(s8[4718592]{0:T(1024)(128)(4,1)} %bitcast.17), calls=%async_computation.11 | async-start | bytes 1048576
  1.5 9.3 %all-to-all-start = ((bf16[4,16,512]{2,1,0:T(8,128)(2,1)}), bf16[4,16,512]{2,1,0:T(8,128)(2,1)S(1)}, u32[]{:S(2)}, u32[]{:S(2)}) async-start(bf16[4,16,512]{2,1,0:T(8,128)(2,1)} %shard_map.136), calls=%async_computation | async-start | bytes 131072 | tf_op jit(solution)/shard_map/all_to_all | solution.py:195
  10.8 9.5 %slice-start.6 = ((s8[4718592]{0:T(1024)(128)(4,1)}), s8[4194304]{0:T(1024)(128)(4,1)S(1)}, s32[]{:S(2)}) async-start(s8[4718592]{0:T(1024)(128)(4,1)} %bitcast.17), calls=%async_computation.12 | async-start | bytes 8388608
  10.8 9.5 %copy-start.1 = (bf16[8,512,128]{2,1,0:T(8,128)(2,1)S(1)}, bf16[8,512,128]{2,1,0:T(8,128)(2,1)}, u32[]{:S(2)}) copy-start(bf16[8,512,128]{2,1,0:T(8,128)(2,1)} %refs_3_.3) | copy-start | bytes 3145732
  10.8 9.5 %copy-start.4 = (bf16[1,2,8,512]{3,2,1,0:T(8,128)(2,1)S(1)}, bf16[1,2,8,512]{3,2,1,0:T(8,128)(2,1)}, u32[]{:S(2)}) copy-start(bf16[1,2,8,512]{3,2,1,0:T(8,128)(2,1)} %param.14) | copy-start | bytes 49156
  10.8 9.5 %copy-start.7 = (bf16[1,2,512]{2,1,0:T(2,128)(2,1)S(1)}, bf16[1,2,512]{2,1,0:T(2,128)(2,1)}, u32[]{:S(2)}) copy-start(bf16[1,2,512]{2,1,0:T(2,128)(2,1)} %param.16) | copy-start | bytes 6148
  12.8 15.8 %copy-start.5 = (bf16[1,2,2304]{2,1,0:T(2,128)(2,1)S(1)}, bf16[1,2,2304]{2,1,0:T(2,128)(2,1)}, u32[]{:S(2)}) copy-start(bf16[1,2,2304]{2,1,0:T(2,128)(2,1)} %param.20) | copy-start | bytes 27652
  12.8 15.8 %copy-start.6 = (bf16[2304]{0:T(1024)(128)(2,1)S(1)}, bf16[2304]{0:T(1024)(128)(2,1)}, u32[]{:S(2)}) copy-start(bf16[2304]{0:T(1024)(128)(2,1)} %refs_2_.2) | copy-start | bytes 13828
  20.3 30.2 %slice-start.3 = ((s8[4718592]{0:T(1024)(128)(4,1)}), s8[4194304]{0:T(1024)(128)(4,1)S(1)}, s32[]{:S(2)}) async-start(s8[4718592]{0:T(1024)(128)(4,1)} %bitcast.14), calls=%async_computation.9 | async-start | bytes 8388608
  28.5 22.0 %slice-start = ((s8[9437184]{0:T(1024)(128)(4,1)}), s8[4194304]{0:T(1024)(128)(4,1)S(1)}, s32[]{:S(2)}) async-start(s8[9437184]{0:T(1024)(128)(4,1)} %bitcast.11), calls=%async_computation.6 | async-start | bytes 8388608
  28.6 22.0 %slice-start.1 = ((s8[9437184]{0:T(1024)(128)(4,1)}), s8[4194304]{0:T(1024)(128)(4,1)S(1)}, s32[]{:S(2)}) async-start(s8[9437184]{0:T(1024)(128)(4,1)} %bitcast.11), calls=%async_computation.7 | async-start | bytes 8388608
  28.6 22.0 %slice-start.2 = ((s8[9437184]{0:T(1024)(128)(4,1)}), s8[1048576]{0:T(1024)(128)(4,1)S(1)}, s32[]{:S(2)}) async-start(s8[9437184]{0:T(1024)(128)(4,1)} %bitcast.11), calls=%async_computation.8 | async-start | bytes 2097152
  28.6 22.0 %slice-start.4 = ((s8[4718592]{0:T(1024)(128)(4,1)}), s8[524288]{0:T(1024)(128)(4,1)S(1)}, s32[]{:S(2)}) async-start(s8[4718592]{0:T(1024)(128)(4,1)} %bitcast.14), calls=%async_computation.10 | async-start | bytes 1048576
  28.6 22.0 %copy-start.2 = (bf16[2304,128]{1,0:T(8,128)(2,1)S(1)}, bf16[2304,128]{1,0:T(8,128)(2,1)}, u32[]{:S(2)}) copy-start(bf16[2304,128]{1,0:T(8,128)(2,1)} %refs_3_.5) | copy-start | bytes 1769476
  54.2 13.1 %all-to-all-start.4 = ((bf16[32,2,2304]{2,1,0:T(2,128)(2,1)}), bf16[32,2,2304]{2,1,0:T(2,128)(2,1)S(1)}, u32[]{:S(2)}, u32[]{:S(2)}) async-start(bf16[32,2,2304]{2,1,0:T(2,128)(2,1)} %shard_map.140), calls=%async_computation.4 | async-start | bytes 589824 | tf_op jit(solution)/shard_map/all_to_all | solution.py:238

commit v4 on v3

--- a/solution.py
+++ b/solution.py
@@ -1,3 +1,5 @@
+import functools
+
 import jax
 import jax.numpy as jnp
 from jax import lax
@@ -34,38 +36,63 @@
     )(*args, *beside)
 
 
-def copies_kernel(part_ref, out_ref):
-    for c in range(out_ref.shape[0]):
-        out_ref[c] = part_ref[...]
-
-
-def attend_kernel(span_ref, q_ref, cache_ref, picked_ref, out_ref, kept_ref):
-    kept_ref[...] = picked_ref[...]
+def picked_kernel(ids_ref, out_ref):
+    group, choices, count = ids_ref.shape
+    total, experts = out_ref.shape
+    expert = lax.broadcasted_iota(jnp.int32, (experts, count), 0)
+    row = lax.broadcasted_iota(jnp.int32, (total, count), 0)
+    batch = lax.broadcasted_iota(jnp.int32, (total, count), 1)
+    picked = jnp.zeros((total, experts), F32)
+    for r in range(group):
+        named = jnp.zeros((experts, count), F32)
+        for k in range(choices):
+            named = jnp.where(ids_ref[r, k : k + 1, :] == expert, 1.0, named)
+        place = jnp.where(row == batch * group + r, 1.0, 0.0).astype(BF16)
+        picked = picked + lax.dot_general(
+            place, named.astype(BF16), (((1,), (1,)), ((), ())), preferred_element_type=F32
+        )
+    out_ref[...] = picked
+
+
+def attend_kernel(span_ref, *refs):
+    count = (len(refs) - 3) // 2
+    q_refs, part_refs = refs[:count], refs[count + 2 : -1]
+    cache_ref, picked_ref = refs[count : count + 2]
+    refs[-1][...] = picked_ref[...]
     rows, span, width = cache_ref.shape
-    parts = q_ref.shape[0]
-    heads = q_ref.shape[1] // rows
-    every = q_ref[...].astype(F32)
+    heads = q_refs[0].shape[0] // rows
+    total = count * heads
+    every = [q_ref[...].astype(F32) for q_ref in q_refs]
+    scores = []
     for r in range(rows):
+        q = jnp.concatenate([q[r * heads : (r + 1) * heads] for q in every], axis=0).astype(BF16)
+        scores.append(
+            lax.dot_general(
+                q, cache_ref[r], (((1,), (1,)), ((), ())), preferred_element_type=F32
+            )
+        )
+    position = span_ref[rows] + lax.broadcasted_iota(jnp.int32, (total, span), 1)
+    probs, tails = [], []
+    lane = lax.broadcasted_iota(jnp.int32, (total, 128), 1)
+    for r in range(rows):
+        valid = position < span_ref[r]
+        score = jnp.where(valid, scores[r] * SCALE, NEG_FILL)
+        peak = jnp.max(score, axis=-1, keepdims=True)
+        prob = jnp.where(valid, jnp.exp(score - peak), 0.0).astype(BF16)
+        mass = jnp.sum(prob.astype(F32), axis=-1, keepdims=True)
+        probs.append(prob)
+        tails.append(jnp.where(lane == 0, peak, jnp.where(lane == 1, mass, 0.0)))
+    for r in range(rows):
+        blend = jnp.dot(probs[r], cache_ref[r], preferred_element_type=F32)
         own = slice(r * heads, (r + 1) * heads)
-        q = every[:, own, :].reshape(parts * heads, width).astype(BF16)
-        scores = lax.dot_general(
-            q, cache_ref[r], (((1,), (1,)), ((), ())), preferred_element_type=F32
-        )
-        scores = scores * SCALE
-        position = span_ref[rows] + lax.broadcasted_iota(jnp.int32, scores.shape, 1)
-        valid = position < span_ref[r]
-        scores = jnp.where(valid, scores, NEG_FILL)
-        peak = jnp.max(scores, axis=-1, keepdims=True)
-        prob = jnp.where(valid, jnp.exp(scores - peak), 0.0).astype(BF16)
-        mass = jnp.sum(prob.astype(F32), axis=-1, keepdims=True)
-        blend = jnp.dot(prob, cache_ref[r], preferred_element_type=F32)
-        lane = lax.broadcasted_iota(jnp.int32, (parts * heads, 128), 1)
-        tail = jnp.where(lane == 0, peak, jnp.where(lane == 1, mass, 0.0))
-        out_ref[:, own, :width] = blend.reshape(parts, heads, width)
-        out_ref[:, own, width:] = tail.reshape(parts, heads, 128)
-
-
-def project_kernel(parts_ref, q_ref, token_ref, up_ref, proj_ref, out_ref):
+        for m, part_ref in enumerate(part_refs):
+            there = slice(m * heads, (m + 1) * heads)
+            part_ref[own, :width] = blend[there]
+            part_ref[own, width:] = tails[r][there]
+
+
+def project_kernel(q_ref, token_ref, up_ref, proj_ref, *refs):
+    part_refs, out_ref = refs[:-1], refs[-1]
     heads, width, _ = up_ref.shape
     rows = token_ref.shape[0]
     token = token_ref[...].astype(F32)
@@ -73,13 +100,14 @@
         [jnp.broadcast_to(token[r : r + 1], (heads, width)) for r in range(rows)], axis=0
     )
     fresh = jnp.sum(q_ref[...].astype(F32) * token, axis=-1, keepdims=True) * SCALE
-    peaks = parts_ref[:, :, width : width + 1]
-    masses = parts_ref[:, :, width + 1 : width + 2]
-    top = jnp.maximum(jnp.max(peaks, axis=0), fresh)
-    factors = jnp.exp(peaks - top[None])
-    fresh_weight = jnp.exp(fresh - top).astype(BF16).astype(F32)
-    mass = jnp.sum(masses * factors, axis=0) + fresh_weight
-    blend = jnp.sum(parts_ref[:, :, :width] * factors, axis=0) + fresh_weight * token
+    peaks = [part_ref[:, width : width + 1] for part_ref in part_refs]
+    top = functools.reduce(jnp.maximum, peaks, fresh)
+    mass = jnp.exp(fresh - top).astype(BF16).astype(F32)
+    blend = mass * token
+    for peak, part_ref in zip(peaks, part_refs):
+        factor = jnp.exp(peak - top)
+        mass = mass + part_ref[:, width + 1 : width + 2] * factor
+        blend = blend + part_ref[:, :width] * factor
     latent = (blend / mass).astype(BF16)
     head = lax.rem(
         lax.broadcasted_iota(jnp.int32, (rows * heads, up_ref.shape[2]), 0), jnp.int32(heads)
@@ -98,12 +126,12 @@
             jnp.sum(terms[r * heads : (r + 1) * heads], axis=0, keepdims=True) for r in range(rows)
         ]
         sums = jnp.concatenate(sums, axis=0)
-        for c in range(out_ref.shape[0]):
-            out_ref[c, :, n : n + step] = sums
-
-
-def norm_kernel(terms_ref, residual_ref, gain_ref, hidden_ref, normed_ref, copies_ref):
-    hidden = residual_ref[...].astype(F32) + jnp.sum(terms_ref[...], axis=0)
+        out_ref[:, n : n + step] = sums
+
+
+def norm_kernel(residual_ref, gain_ref, *refs):
+    hidden_ref, normed_ref, copies_ref = refs[-3:]
+    hidden = residual_ref[...].astype(F32) + sum(ref[...] for ref in refs[:-3])
     inverse = lax.rsqrt(jnp.mean(hidden * hidden, axis=-1, keepdims=True) + EPSILON)
     normed = (hidden * inverse * gain_ref[...].astype(F32)[None]).astype(BF16)
     hidden_ref[...] = hidden
@@ -151,12 +179,19 @@
 
 def gather_sum_kernel(parts_ref, shared_ref, out_ref):
     total = jnp.sum(parts_ref[...].astype(F32), axis=0) + shared_ref[...]
-    for c in range(out_ref.shape[0]):
-        out_ref[c] = total
-
-
-def final_kernel(hidden_ref, terms_ref, out_ref):
-    out_ref[...] = (hidden_ref[...] + jnp.sum(terms_ref[...], axis=0)).astype(BF16)
+    out_ref[...] = total
+
+
+def final_kernel(hidden_ref, *refs):
+    refs[-1][...] = (hidden_ref[...] + sum(ref[...] for ref in refs[:-1])).astype(BF16)
+
+
+def swaps(arrays, axis):
+    size = lax.axis_size(axis)
+    return [
+        lax.ppermute(array, axis, [(place, place ^ m) for place in range(size)])
+        for m, array in enumerate(arrays, 1)
+    ]
 
 
 def local(
@@ -186,36 +221,31 @@
     shape = jax.ShapeDtypeStruct
 
     own_query = queries.reshape(rows * heads, width)
-    copies = call(
-        copies_kernel,
-        shape((ctx_count, rows * heads, width), BF16),
-        [own_query],
-        beside=[expert_down],
-    )
-    every_query = lax.all_to_all(copies, "ctx", 0, 0)
+    every_query = [own_query] + swaps([own_query] * (ctx_count - 1), "ctx")
     start = ctx_index * latent_cache.shape[2]
     own_expert = ctx_index * batch_count + batch_index
     span = jnp.concatenate([lengths[0], jnp.stack([start, own_expert]).astype(jnp.int32)])
-    all_picks = expert_ids.reshape(total_rows, -1)
-    expert_range = jnp.arange(experts, dtype=jnp.int32)
-    picked = jnp.any(all_picks[:, :, None] == expert_range[None, None, :], axis=1).astype(F32)
-    parts, picked = call(
+    picked = call(
+        picked_kernel,
+        shape((total_rows, experts), F32),
+        [expert_ids.transpose(1, 2, 0)],
+        beside=[expert_gate_up],
+    )
+    *parts, picked = call(
         attend_kernel,
-        (
-            shape((ctx_count, rows * heads, width + 128), F32),
-            shape((total_rows, experts), F32),
-        ),
-        [span, every_query, latent_cache[0], picked],
-        [SMEM, VMEM, VMEM, VMEM],
+        [shape((rows * heads, width + 128), F32)] * ctx_count
+        + [shape((total_rows, experts), F32)],
+        [span, *every_query, latent_cache[0], picked],
+        [SMEM] + [VMEM] * (ctx_count + 2),
         beside=[expert_gate_up] * 3,
     )
-    parts = lax.all_to_all(parts, "ctx", 0, 0)
+    parts = [parts[0]] + swaps(parts[1:], "ctx")
     terms = call(
         project_kernel,
-        shape((ctx_count, rows, model), F32),
-        [parts, own_query, token_latent[0], value_up_weight, out_proj],
-    )
-    terms = lax.all_to_all(terms, "ctx", 0, 0)
+        shape((rows, model), F32),
+        [own_query, token_latent[0], value_up_weight, out_proj, *parts],
+    )
+    terms = [terms] + swaps([terms] * (ctx_count - 1), "ctx")
     hidden, normed, copies = call(
         norm_kernel,
         (
@@ -223,7 +253,7 @@
             shape((rows, model), BF16),
             shape((batch_count, rows, model), BF16),
         ),
-        [terms, residual[0], norm_gain],
+        [residual[0], norm_gain, *terms],
         beside=[expert_gate_up] * 4,
     )
 
@@ -252,10 +282,10 @@
         ],
     )
     totals = call(
-        gather_sum_kernel, shape((ctx_count, rows, model), F32), [weighted, shared_part]
-    )
-    totals = lax.all_to_all(totals, "ctx", 0, 0)
-    return call(final_kernel, shape((rows, model), BF16), [hidden, totals])[None]
+        gather_sum_kernel, shape((rows, model), F32), [weighted, shared_part]
+    )
+    totals = [totals] + swaps([totals] * (ctx_count - 1), "ctx")
+    return call(final_kernel, shape((rows, model), BF16), [hidden, *totals])[None]
 
 
 def solution(mesh):

time: 75.7 us -> 69.4 us (0.917)
  blocking collectives: 43.2 us -> 22.5 us
  starting transfers between devices: 8.64 us -> 18.3 us
  waiting for transfers between devices: 11 us -> 16.3 us
    all_to_all x3 -> x0, blocking collectives: 21.4 us -> none  [the longest x1 7.49 us: local(): parts = lax.all_to_all(parts, 'ctx', 0, 0)]
    ppermute x0 -> x12, starting transfers between devices: none -> 14.5 us  [swaps(): lax.ppermute(array, axis, [(place, place ^ m) for place in range(size)])]
    ppermute x0 -> x12, waiting for transfers between devices: none -> 9.39 us  [swaps(): lax.ppermute(array, axis, [(place, place ^ m) for place in range(size)])]
    all_to_all x1 -> x0, starting transfers between devices: 4.84 us -> none  [local(): every_query = lax.all_to_all(copies, 'ctx', 0, 0)]
    all_to_all x1 -> x0, waiting for transfers between devices: 4.12 us -> none  [local(): every_query = lax.all_to_all(copies, 'ctx', 0, 0)]
  transfers between devices with their start and end apart: 2 -> 13, of which waited for: 2 -> 9; matrix products, arithmetic and copies ran while one was open for 0% -> 1% of each run, Pallas kernels for 3% -> 4%
where the time goes in v4:
time: 69.4 us; the launch traced here: 68.9 us
  blocking collectives  22.5 us (32%)
  starting transfers between devices  18.3 us (26%)
  waiting for transfers between devices  16.3 us (23%)
  Pallas kernels  10.1 us (15%)
  local copies, waits for them, and re-layouts  0.77 us (1%)
  other arithmetic  0.73 us (1%)
    all_to_all x1, blocking collectives, local(): every_rows = lax.all_to_all(copies, 'batch', 0, 0)  22.5 us
    ppermute x12, starting transfers between devices, swaps(): lax.ppermute(array, axis, [(place, place ^ m) for place in range(size)])  14.5 us
    pallas_call x8, Pallas kernels, call(): pl.pallas_call(body, out_shape=out_shape, in_specs=(specs or [VMEM] * cou...  10.1 us
    ppermute x12, waiting for transfers between devices, swaps(): lax.ppermute(array, axis, [(place, place ^ m) for place in range(size)])  9.39 us
    all_to_all x1, waiting for transfers between devices, local(): weighted = lax.all_to_all(weighted, 'batch', 0, 0)  6.92 us
    all_to_all x1, starting transfers between devices, local(): weighted = lax.all_to_all(weighted, 'batch', 0, 0)  3.8 us
  transfers between devices with their start and end apart: 13, of which 9 were waited for; matrix products, arithmetic and copies ran while one was open for 1% of the time, Pallas kernels for 4%

profile of v4, /device:TPU:1, one launch (start us, length us, event | category | flops | bytes accessed | tf_op | source)
XLA Modules:
  0.0 68.9 jit_solution(6226354856880939570)
XLA Ops:
  0.0 3.3 %collective-permute-start.2 = (bf16[16,512]{1,0:T(8,128)(2,1)}, bf16[16,512]{1,0:T(8,128)(2,1)S(1)}, u32[]{:S(2)}, u32[]{:S(2)}) collective-permute-start(bf16[16,512]{1,0:T(8,128)(2,1)} %bitcast.20), channel_id=1, source_target_pairs={{0,96},{32,64},{64,32},{96,0},{1,97},{33,65},{65,33},{97,1},{2,98}... | collective-permute-start | bytes 49160 | tf_op jit(solution)/shard_map/ppermute | solution.py:192
  3.9 0.7 %pad_add_fusion.refs_0_ = s32[4]{0:T(128)S(1)} fusion(s32[1]{0:T(128)} %bitcast.5, s32[1]{0:T(128)} %bitcast.4, s32[2]{0:T(128)} %bitcast.28), kind=kLoop, calls=%fused_computation | loop fusion | flops 8 | bytes 32 | tf_op jit(solution)/shard_map/concatenate | solution.py:227
  4.6 0.7 %copy-done.5 = s32[32,2,8]{0,2,1:T(8,128)S(1)} copy-done((s32[32,2,8]{0,2,1:T(8,128)S(1)}, s32[32,2,8]{0,2,1:T(8,128)}, u32[]{:S(2)}) %copy-start.5) | copy-done | bytes 2072
  5.5 2.1 %collective-permute-done.1.refs_3_ = bf16[16,512]{1,0:T(8,128)(2,1)S(1)} collective-permute-done((bf16[16,512]{1,0:T(8,128)(2,1)}, bf16[16,512]{1,0:T(8,128)(2,1)S(1)}, u32[]{:S(2)}, u32[]{:S(2)}) %collective-permute-start.1) | collective-permute-done | bytes 16416 | tf_op jit(solution)/shard_map/ppermute | solution.py:192
  7.7 1.7 %shard_map.137 = (f32[16,640]{1,0:T(8,128)S(1)}, f32[16,640]{1,0:T(8,128)S(1)}, f32[16,640]{1,0:T(8,128)S(1)}, f32[16,640]{1,0:T(8,128)S(1)}, f32[64,128]{1,0:T(8,128)S(1)}) custom-call(s32[4]{0:T(128)S(1)} %pad_add_fusion.refs_0_, bf16[16,512]{1,0:T(8,128)(2,1)S(1)} %bitcast.23, bf16[16,512]{1,0:T(8,128)(2,1)S(1)} %collective-permute-done.refs_2_, ...), custom_call_target="tpu_custom_call" | custom-call | tf_op jit(solution)/shard_map/pallas_call | solution.py:29
  9.3 0.7 %collective-permute-start.3 = (f32[16,640]{1,0:T(8,128)S(1)}, f32[16,640]{1,0:T(8,128)S(1)}, u32[]{:S(2)}, u32[]{:S(2)}) collective-permute-start(f32[16,640]{1,0:T(8,128)S(1)} %get-tuple-element.14), channel_id=1, source_target_pairs={{0,32},{32,0},{64,96},{96,64},{1,33},{33,1},{65,97},{97,65},{2,34}... | collective-permute-start | bytes 122888 | tf_op jit(solution)/shard_map/ppermute | solution.py:192
  10.1 2.5 %collective-permute-start.4 = (f32[16,640]{1,0:T(8,128)S(1)}, f32[16,640]{1,0:T(8,128)S(1)}, u32[]{:S(2)}, u32[]{:S(2)}) collective-permute-start(f32[16,640]{1,0:T(8,128)S(1)} %get-tuple-element.15), channel_id=1, source_target_pairs={{0,64},{32,96},{64,0},{96,32},{1,65},{33,97},{65,1},{97,33},{2,66}... | collective-permute-start | bytes 122888 | tf_op jit(solution)/shard_map/ppermute | solution.py:192
  12.5 0.7 %collective-permute-start.5 = (f32[16,640]{1,0:T(8,128)S(1)}, f32[16,640]{1,0:T(8,128)S(1)}, u32[]{:S(2)}, u32[]{:S(2)}) collective-permute-start(f32[16,640]{1,0:T(8,128)S(1)} %get-tuple-element.16), channel_id=1, source_target_pairs={{0,96},{32,64},{64,32},{96,0},{1,97},{33,65},{65,33},{97,1},{2,98}... | collective-permute-start | bytes 122888 | tf_op jit(solution)/shard_map/ppermute | solution.py:192
  13.3 1.2 %collective-permute-done.4.refs_6_ = f32[16,640]{1,0:T(8,128)S(1)} collective-permute-done((f32[16,640]{1,0:T(8,128)S(1)}, f32[16,640]{1,0:T(8,128)S(1)}, u32[]{:S(2)}, u32[]{:S(2)}) %collective-permute-start.4) | collective-permute-done | bytes 40992 | tf_op jit(solution)/shard_map/ppermute | solution.py:192
  14.4 2.6 %collective-permute-done.5.refs_7_ = f32[16,640]{1,0:T(8,128)S(1)} collective-permute-done((f32[16,640]{1,0:T(8,128)S(1)}, f32[16,640]{1,0:T(8,128)S(1)}, u32[]{:S(2)}, u32[]{:S(2)}) %collective-permute-start.5) | collective-permute-done | bytes 40992 | tf_op jit(solution)/shard_map/ppermute | solution.py:192
  17.1 1.3 %shard_map.138.refs_2_ = f32[2,2304]{1,0:T(2,128)S(1)} custom-call(bf16[16,512]{1,0:T(8,128)(2,1)S(1)} %bitcast.24, bf16[2,512]{1,0:T(2,128)(2,1)S(1)} %bitcast.27, bf16[8,512,128]{2,1,0:T(8,128)(2,1)S(1)} %copy-done.1, bf16[1024,2304]{1,0:T(8,128)(2,1)S(1)} %bitcast.18, f32[16,640]{1,0:T(8,128)S(1)} %get-tuple-element.13.refs_4_, ...), custom_call_target="tpu_custom_call" | custom-call | tf_op jit(solution)/shard_map/pallas_call | solution.py:29
  18.8 2.8 %collective-permute-start.6 = (f32[2,2304]{1,0:T(2,128)S(1)}, f32[2,2304]{1,0:T(2,128)S(1)}, u32[]{:S(2)}, u32[]{:S(2)}) collective-permute-start(f32[2,2304]{1,0:T(2,128)S(1)} %shard_map.138.refs_2_), channel_id=1, source_target_pairs={{0,32},{32,0},{64,96},{96,64},{1,33},{33,1},{65,97},{97,65},{2,34}... | collective-permute-start | bytes 55304 | tf_op jit(solution)/shard_map/ppermute | solution.py:192
  21.7 0.6 collective-permute-done.8.refs_5_
  22.2 0.6 collective-permute-done.7.refs_4_
  23.2 22.5 %all_to_all.10.refs_1_ = bf16[32,2,2304]{2,1,0:T(2,128)(2,1)S(1)} all-to-all(bf16[32,2,2304]{2,1,0:T(2,128)(2,1)S(1)} %get-tuple-element.18), channel_id=1, replica_groups=mesh['ctx'=4,'batch'=32] {'batch'}, dimensions={0} | all-to-all | bytes 589824 | tf_op jit(solution)/shard_map/all_to_all | solution.py:260
  45.7 3.6 %shard_map.140 = bf16[32,2,2304]{2,1,0:T(2,128)(2,1)} custom-call(s32[4]{0:T(128)S(1)} %pad_add_fusion.refs_0_, bf16[32,2,2304]{2,1,0:T(2,128)(2,1)S(1)} %all_to_all.10.refs_1_, f32[64,128]{1,0:T(8,128)S(1)} %get-tuple-element.19.refs_2_, bf16[2304,128]{1,0:T(8,128)(2,1)S(1)} %copy-done.2, bf16[2304,2048]{1,0:T(8,128)(2,1)S(1)} %bitcast.13, ...), custom_call_target="tpu_custom_call" | custom-call | tf_op jit(solution)/shard_map/pallas_call | solution.py:29
  49.3 3.8 %all-to-all-start.1 = ((bf16[32,2,2304]{2,1,0:T(2,128)(2,1)}), bf16[32,2,2304]{2,1,0:T(2,128)(2,1)S(1)}, u32[]{:S(2)}, u32[]{:S(2)}) async-start(bf16[32,2,2304]{2,1,0:T(2,128)(2,1)} %shard_map.140), calls=%async_computation.1 | async-start | bytes 589824 | tf_op jit(solution)/shard_map/all_to_all | solution.py:268
  53.1 2.4 %shard_map.141.refs_1_ = f32[2,2304]{1,0:T(2,128)S(1)} custom-call(bf16[2,2304]{1,0:T(2,128)(2,1)S(1)} %get-tuple-element.20.refs_0_, bf16[2,2304,256]{2,1,0:T(8,128)(2,1)} %refs_1_.5, bf16[256,2304]{1,0:T(8,128)(2,1)} %refs_2_.3), custom_call_target="tpu_custom_call" | custom-call | tf_op jit(solution)/shard_map/pallas_call | solution.py:29
  55.5 6.9 %all-to-all-done.1.refs_0_ = bf16[32,2,2304]{2,1,0:T(2,128)(2,1)S(1)} async-done(((bf16[32,2,2304]{2,1,0:T(2,128)(2,1)}), bf16[32,2,2304]{2,1,0:T(2,128)(2,1)S(1)}, u32[]{:S(2)}, u32[]{:S(2)}) %all-to-all-start.1) | async-done | bytes 294944 | tf_op jit(solution)/shard_map/all_to_all | solution.py:268
  62.7 1.4 %collective-permute-start.11 = (f32[2,2304]{1,0:T(2,128)S(1)}, f32[2,2304]{1,0:T(2,128)S(1)}, u32[]{:S(2)}, u32[]{:S(2)}) collective-permute-start(f32[2,2304]{1,0:T(2,128)S(1)} %shard_map.142.refs_1_), channel_id=1, source_target_pairs={{0,96},{32,64},{64,32},{96,0},{1,97},{33,65},{65,33},{97,1},{2,98}... | collective-permute-start | bytes 55304 | tf_op jit(solution)/shard_map/ppermute | solution.py:192
  64.1 1.1 %collective-permute-start.10 = (f32[2,2304]{1,0:T(2,128)S(1)}, f32[2,2304]{1,0:T(2,128)S(1)}, u32[]{:S(2)}, u32[]{:S(2)}) collective-permute-start(f32[2,2304]{1,0:T(2,128)S(1)} %shard_map.142.refs_1_), channel_id=1, source_target_pairs={{0,64},{32,96},{64,0},{96,32},{1,65},{33,97},{65,1},{97,33},{2,66}... | collective-permute-start | bytes 55304 | tf_op jit(solution)/shard_map/ppermute | solution.py:192
  65.3 0.8 %collective-permute-start.9 = (f32[2,2304]{1,0:T(2,128)S(1)}, f32[2,2304]{1,0:T(2,128)S(1)}, u32[]{:S(2)}, u32[]{:S(2)}) collective-permute-start(f32[2,2304]{1,0:T(2,128)S(1)} %shard_map.142.refs_1_), channel_id=1, source_target_pairs={{0,32},{32,0},{64,96},{96,64},{1,33},{33,1},{65,97},{97,65},{2,34}... | collective-permute-start | bytes 55304 | tf_op jit(solution)/shard_map/ppermute | solution.py:192
  66.6 1.6 %collective-permute-done.10.refs_3_ = f32[2,2304]{1,0:T(2,128)S(1)} collective-permute-done((f32[2,2304]{1,0:T(2,128)S(1)}, f32[2,2304]{1,0:T(2,128)S(1)}, u32[]{:S(2)}, u32[]{:S(2)}) %collective-permute-start.10) | collective-permute-done | bytes 18464 | tf_op jit(solution)/shard_map/ppermute | solution.py:192
  68.3 0.6 shard_map.143
  (45 shorter events, 2.6 us)
Async XLA Ops:
  0.0 5.5 %collective-permute-start.2 = (bf16[16,512]{1,0:T(8,128)(2,1)}, bf16[16,512]{1,0:T(8,128)(2,1)S(1)}, u32[]{:S(2)}, u32[]{:S(2)}) collective-permute-start(bf16[16,512]{1,0:T(8,128)(2,1)} %bitcast.20), channel_id=1, source_target_pairs={{0,96},{32,64},{64,32},{96,0},{1,97},{33,65},{65,33},{97,1},{2,98}... | collective-permute-start | bytes 49160 | tf_op jit(solution)/shard_map/ppermute | solution.py:192
  3.3 4.3 %collective-permute-start.1 = (bf16[16,512]{1,0:T(8,128)(2,1)}, bf16[16,512]{1,0:T(8,128)(2,1)S(1)}, u32[]{:S(2)}, u32[]{:S(2)}) collective-permute-start(bf16[16,512]{1,0:T(8,128)(2,1)} %bitcast.21), channel_id=1, source_target_pairs={{0,64},{32,96},{64,0},{96,32},{1,65},{33,97},{65,1},{97,33},{2,66}... | collective-permute-start | bytes 49160 | tf_op jit(solution)/shard_map/ppermute | solution.py:192
  3.8 3.8 %collective-permute-start = (bf16[16,512]{1,0:T(8,128)(2,1)}, bf16[16,512]{1,0:T(8,128)(2,1)S(1)}, u32[]{:S(2)}, u32[]{:S(2)}) collective-permute-start(bf16[16,512]{1,0:T(8,128)(2,1)} %bitcast.22), channel_id=1, source_target_pairs={{0,32},{32,0},{64,96},{96,64},{1,33},{33,1},{65,97},{97,65},{2,34}... | collective-permute-start | bytes 49160 | tf_op jit(solution)/shard_map/ppermute | solution.py:192
  5.3 11.7 %slice-start.5 = ((s8[4718592]{0:T(1024)(128)(4,1)}), s8[4194304]{0:T(1024)(128)(4,1)S(1)}, s32[]{:S(2)}) async-start(s8[4718592]{0:T(1024)(128)(4,1)} %bitcast.17), calls=%async_computation.7 | async-start | bytes 8388608
  7.6 9.4 %slice-start.6 = ((s8[4718592]{0:T(1024)(128)(4,1)}), s8[524288]{0:T(1024)(128)(4,1)S(1)}, s32[]{:S(2)}) async-start(s8[4718592]{0:T(1024)(128)(4,1)} %bitcast.17), calls=%async_computation.8 | async-start | bytes 1048576
  7.6 9.4 %copy-start.1 = (bf16[8,512,128]{2,1,0:T(8,128)(2,1)S(1)}, bf16[8,512,128]{2,1,0:T(8,128)(2,1)}, u32[]{:S(2)}) copy-start(bf16[8,512,128]{2,1,0:T(8,128)(2,1)} %refs_2_.2) | copy-start | bytes 3145732
  9.3 13.7 %copy-start.4 = (bf16[1,2,2304]{2,1,0:T(2,128)(2,1)S(1)}, bf16[1,2,2304]{2,1,0:T(2,128)(2,1)}, u32[]{:S(2)}) copy-start(bf16[1,2,2304]{2,1,0:T(2,128)(2,1)} %param.20) | copy-start | bytes 27652
  9.3 13.7 %copy-start.6 = (bf16[2304]{0:T(1024)(128)(2,1)S(1)}, bf16[2304]{0:T(1024)(128)(2,1)}, u32[]{:S(2)}) copy-start(bf16[2304]{0:T(1024)(128)(2,1)} %refs_1_.4) | copy-start | bytes 13828
  9.3 3.9 %collective-permute-start.3 = (f32[16,640]{1,0:T(8,128)S(1)}, f32[16,640]{1,0:T(8,128)S(1)}, u32[]{:S(2)}, u32[]{:S(2)}) collective-permute-start(f32[16,640]{1,0:T(8,128)S(1)} %get-tuple-element.14), channel_id=1, source_target_pairs={{0,32},{32,0},{64,96},{96,64},{1,33},{33,1},{65,97},{97,65},{2,34}... | collective-permute-start | bytes 122888 | tf_op jit(solution)/shard_map/ppermute | solution.py:192
  10.1 4.4 %collective-permute-start.4 = (f32[16,640]{1,0:T(8,128)S(1)}, f32[16,640]{1,0:T(8,128)S(1)}, u32[]{:S(2)}, u32[]{:S(2)}) collective-permute-start(f32[16,640]{1,0:T(8,128)S(1)} %get-tuple-element.15), channel_id=1, source_target_pairs={{0,64},{32,96},{64,0},{96,32},{1,65},{33,97},{65,1},{97,33},{2,66}... | collective-permute-start | bytes 122888 | tf_op jit(solution)/shard_map/ppermute | solution.py:192
  12.5 4.5 %collective-permute-start.5 = (f32[16,640]{1,0:T(8,128)S(1)}, f32[16,640]{1,0:T(8,128)S(1)}, u32[]{:S(2)}, u32[]{:S(2)}) collective-permute-start(f32[16,640]{1,0:T(8,128)S(1)} %get-tuple-element.16), channel_id=1, source_target_pairs={{0,96},{32,64},{64,32},{96,0},{1,97},{33,65},{65,33},{97,1},{2,98}... | collective-permute-start | bytes 122888 | tf_op jit(solution)/shard_map/ppermute | solution.py:192
  17.1 28.6 %slice-start.3 = ((s8[4718592]{0:T(1024)(128)(4,1)}), s8[4194304]{0:T(1024)(128)(4,1)S(1)}, s32[]{:S(2)}) async-start(s8[4718592]{0:T(1024)(128)(4,1)} %bitcast.14), calls=%async_computation.5 | async-start | bytes 8388608
  18.3 3.9 %collective-permute-start.8 = (f32[2,2304]{1,0:T(2,128)S(1)}, f32[2,2304]{1,0:T(2,128)S(1)}, u32[]{:S(2)}, u32[]{:S(2)}) collective-permute-start(f32[2,2304]{1,0:T(2,128)S(1)} %shard_map.138.refs_2_), channel_id=1, source_target_pairs={{0,96},{32,64},{64,32},{96,0},{1,97},{33,65},{65,33},{97,1},{2,98}... | collective-permute-start | bytes 55304 | tf_op jit(solution)/shard_map/ppermute | solution.py:192
  18.7 4.1 %collective-permute-start.7 = (f32[2,2304]{1,0:T(2,128)S(1)}, f32[2,2304]{1,0:T(2,128)S(1)}, u32[]{:S(2)}, u32[]{:S(2)}) collective-permute-start(f32[2,2304]{1,0:T(2,128)S(1)} %shard_map.138.refs_2_), channel_id=1, source_target_pairs={{0,64},{32,96},{64,0},{96,32},{1,65},{33,97},{65,1},{97,33},{2,66}... | collective-permute-start | bytes 55304 | tf_op jit(solution)/shard_map/ppermute | solution.py:192
  18.8 4.2 %collective-permute-start.6 = (f32[2,2304]{1,0:T(2,128)S(1)}, f32[2,2304]{1,0:T(2,128)S(1)}, u32[]{:S(2)}, u32[]{:S(2)}) collective-permute-start(f32[2,2304]{1,0:T(2,128)S(1)} %shard_map.138.refs_2_), channel_id=1, source_target_pairs={{0,32},{32,0},{64,96},{96,64},{1,33},{33,1},{65,97},{97,65},{2,34}... | collective-permute-start | bytes 55304 | tf_op jit(solution)/shard_map/ppermute | solution.py:192
  23.0 22.7 %slice-start = ((s8[9437184]{0:T(1024)(128)(4,1)}), s8[4194304]{0:T(1024)(128)(4,1)S(1)}, s32[]{:S(2)}) async-start(s8[9437184]{0:T(1024)(128)(4,1)} %bitcast.11), calls=%async_computation.2 | async-start | bytes 8388608
  23.0 22.7 %slice-start.1 = ((s8[9437184]{0:T(1024)(128)(4,1)}), s8[4194304]{0:T(1024)(128)(4,1)S(1)}, s32[]{:S(2)}) async-start(s8[9437184]{0:T(1024)(128)(4,1)} %bitcast.11), calls=%async_computation.3 | async-start | bytes 8388608
  23.0 22.7 %slice-start.2 = ((s8[9437184]{0:T(1024)(128)(4,1)}), s8[1048576]{0:T(1024)(128)(4,1)S(1)}, s32[]{:S(2)}) async-start(s8[9437184]{0:T(1024)(128)(4,1)} %bitcast.11), calls=%async_computation.4 | async-start | bytes 2097152
  23.0 22.7 %slice-start.4 = ((s8[4718592]{0:T(1024)(128)(4,1)}), s8[524288]{0:T(1024)(128)(4,1)S(1)}, s32[]{:S(2)}) async-start(s8[4718592]{0:T(1024)(128)(4,1)} %bitcast.14), calls=%async_computation.6 | async-start | bytes 1048576
  23.1 22.7 %copy-start.2 = (bf16[2304,128]{1,0:T(8,128)(2,1)S(1)}, bf16[2304,128]{1,0:T(8,128)(2,1)}, u32[]{:S(2)}) copy-start(bf16[2304,128]{1,0:T(8,128)(2,1)} %refs_3_.3) | copy-start | bytes 1769476
  49.3 13.1 %all-to-all-start.1 = ((bf16[32,2,2304]{2,1,0:T(2,128)(2,1)}), bf16[32,2,2304]{2,1,0:T(2,128)(2,1)S(1)}, u32[]{:S(2)}, u32[]{:S(2)}) async-start(bf16[32,2,2304]{2,1,0:T(2,128)(2,1)} %shard_map.140), calls=%async_computation.1 | async-start | bytes 589824 | tf_op jit(solution)/shard_map/all_to_all | solution.py:268
  62.7 3.9 %collective-permute-start.11 = (f32[2,2304]{1,0:T(2,128)S(1)}, f32[2,2304]{1,0:T(2,128)S(1)}, u32[]{:S(2)}, u32[]{:S(2)}) collective-permute-start(f32[2,2304]{1,0:T(2,128)S(1)} %shard_map.142.refs_1_), channel_id=1, source_target_pairs={{0,96},{32,64},{64,32},{96,0},{1,97},{33,65},{65,33},{97,1},{2,98}... | collective-permute-start | bytes 55304 | tf_op jit(solution)/shard_map/ppermute | solution.py:192
  64.1 4.1 %collective-permute-start.10 = (f32[2,2304]{1,0:T(2,128)S(1)}, f32[2,2304]{1,0:T(2,128)S(1)}, u32[]{:S(2)}, u32[]{:S(2)}) collective-permute-start(f32[2,2304]{1,0:T(2,128)S(1)} %shard_map.142.refs_1_), channel_id=1, source_target_pairs={{0,64},{32,96},{64,0},{96,32},{1,65},{33,97},{65,1},{97,33},{2,66}... | collective-permute-start | bytes 55304 | tf_op jit(solution)/shard_map/ppermute | solution.py:192
  65.3 3.0 %collective-permute-start.9 = (f32[2,2304]{1,0:T(2,128)S(1)}, f32[2,2304]{1,0:T(2,128)S(1)}, u32[]{:S(2)}, u32[]{:S(2)}) collective-permute-start(f32[2,2304]{1,0:T(2,128)S(1)} %shard_map.142.refs_1_), channel_id=1, source_target_pairs={{0,32},{32,0},{64,96},{96,64},{1,33},{33,1},{65,97},{97,65},{2,34}... | collective-permute-start | bytes 55304 | tf_op jit(solution)/shard_map/ppermute | solution.py:192
  (4 other events, 14.7 us)

commit v5 on v4

v5 whole, which is shorter than its diff:
```python
import functools

import jax
import jax.numpy as jnp
from jax import lax
from jax.experimental import pallas as pl
from jax.experimental.pallas import tpu as pltpu
from jax.sharding import PartitionSpec as P

QK = 192
NEG_FILL = -1e30
ROUTE_SCALE = 2.446
EPSILON = 1e-06
SCALE = QK ** (-0.5)
LIMIT = 8 << 20
BF16, F32 = jnp.bfloat16, jnp.float32
VMEM = pl.BlockSpec(memory_space=pltpu.VMEM)
HBM = pl.BlockSpec(memory_space=pltpu.HBM)


def call(kernel, out_shape, args, specs=None, limit=LIMIT, scratch=(), beside=()):
    beside = [pltpu.with_memory_space_constraint(array, pltpu.HBM) for array in beside]
    count = len(args)

    def body(*refs):
        kernel(*refs[:count], *refs[count + len(beside) :])

    return pl.pallas_call(
        body,
        out_shape=out_shape,
        in_specs=(specs or [VMEM] * count) + [HBM] * len(beside),
        out_specs=jax.tree.map(lambda _: VMEM, out_shape),
        scratch_shapes=list(scratch),
        compiler_params=pltpu.CompilerParams(vmem_limit_bytes=limit),
    )(*args, *beside)


def split(value):
    high = value.astype(BF16).astype(F32)
    middle = (value - high).astype(BF16).astype(F32)
    return high, middle, value - high - middle


def tree_sum(refs):
    values = [ref[...].astype(F32) for ref in refs]
    while len(values) > 1:
        values = [a + b for a, b in zip(values[::2], values[1::2])]
    return values[0]


def picked_kernel(ids_ref, out_ref):
    group, choices, count = ids_ref.shape
    total, experts = out_ref.shape
    expert = lax.broadcasted_iota(jnp.int32, (experts, count), 0)
    row = lax.broadcasted_iota(jnp.int32, (total, count), 0)
    batch = lax.broadcasted_iota(jnp.int32, (total, count), 1)
    picked = jnp.zeros((total, experts), F32)
    for r in range(group):
        named = jnp.zeros((experts, count), F32)
        for k in range(choices):
            named = jnp.where(ids_ref[r, k : k + 1, :] == expert, 1.0, named)
        place = jnp.where(row == batch * group + r, 1.0, 0.0).astype(BF16)
        picked = picked + lax.dot_general(
            place, named.astype(BF16), (((1,), (1,)), ((), ())), preferred_element_type=F32
        )
    out_ref[...] = picked


def attend_kernel(marks_ref, *refs):
    count = (len(refs) - 4) // 2
    q_refs, part_refs = refs[:count], refs[count + 3 : -1]
    cache_ref, token_ref, picked_ref = refs[count : count + 3]
    refs[-1][...] = picked_ref[...]
    rows, span, width = cache_ref.shape
    heads = q_refs[0].shape[0] // rows
    total = count * heads
    every = [q_ref[...].astype(F32) for q_ref in q_refs]
    scores = []
    for r in range(rows):
        q = jnp.concatenate([q[r * heads : (r + 1) * heads] for q in every], axis=0).astype(BF16)
        scores.append(
            lax.dot_general(
                q, cache_ref[r], (((1,), (1,)), ((), ())), preferred_element_type=F32
            )
        )
    position = lax.broadcasted_iota(jnp.int32, (total, span), 1)
    probs, tails = [], []
    lane = lax.broadcasted_iota(jnp.int32, (total, 128), 1)
    for r in range(rows):
        valid = position < marks_ref[:, r : r + 1]
        score = jnp.where(valid, scores[r] * SCALE, NEG_FILL)
        peak = jnp.max(score, axis=-1, keepdims=True)
        prob = jnp.where(valid, jnp.exp(score - peak), 0.0).astype(BF16)
        mass = jnp.sum(prob.astype(F32), axis=-1, keepdims=True)
        probs.append(prob)
        tail = jnp.zeros((total, 128), F32)
        for place, piece in enumerate(split(peak) + split(mass)):
            tail = jnp.where(lane == place, piece, tail)
        tails.append(tail)
    blends = [jnp.dot(probs[r], cache_ref[r], preferred_element_type=F32) for r in range(rows)]
    for m, part_ref in enumerate(part_refs):
        there = slice(m * heads, (m + 1) * heads)
        part = jnp.concatenate([blend[there] for blend in blends])
        tail = jnp.concatenate([tail[there] for tail in tails])
        if m == 0:
            token = token_ref[...].astype(F32)
            token = [jnp.broadcast_to(token[r : r + 1], (heads, width)) for r in range(rows)]
            token = jnp.concatenate(token, axis=0)
            fresh = jnp.sum(every[0] * token, axis=-1, keepdims=True) * SCALE
            for place, piece in enumerate(split(fresh), 6):
                tail = jnp.where(lane[: rows * heads] == place, piece, tail)
            part_ref[rows * heads :, :width] = token.astype(BF16)
            part_ref[rows * heads :, width:] = jnp.zeros((rows * heads, 128), BF16)
        part_ref[: rows * heads, :width] = part.astype(BF16)
        part_ref[: rows * heads, width:] = tail.astype(BF16)


def project_kernel(up_ref, proj_ref, *refs):
    part_refs, out_ref = refs[:-1], refs[-1]
    heads, width, _ = up_ref.shape
    rows = out_ref.shape[0]
    count = rows * heads
    token = part_refs[0][count:, :width].astype(F32)
    tails = [part_ref[:count, width:].astype(F32) for part_ref in part_refs]
    peaks = [tail[:, 0:1] + (tail[:, 1:2] + tail[:, 2:3]) for tail in tails]
    masses = [tail[:, 3:4] + (tail[:, 4:5] + tail[:, 5:6]) for tail in tails]
    fresh = tails[0][:, 6:7] + (tails[0][:, 7:8] + tails[0][:, 8:9])
    top = functools.reduce(jnp.maximum, peaks, fresh)
    mass = jnp.exp(fresh - top).astype(BF16).astype(F32)
    blend = mass * token
    for there, peak, part_ref in zip(masses, peaks, part_refs):
        factor = jnp.exp(peak - top)
        mass = mass + there * factor
        blend = blend + part_ref[:count, :width].astype(F32) * factor
    latent = (blend / mass).astype(BF16)
    head = lax.rem(
        lax.broadcasted_iota(jnp.int32, (rows * heads, up_ref.shape[2]), 0), jnp.int32(heads)
    )
    values = [
        jnp.where(head == h, jnp.dot(latent, up_ref[h], preferred_element_type=F32), 0.0).astype(
            BF16
        )
        for h in range(heads)
    ]
    values = jnp.concatenate(values, axis=1)
    step = 256
    for n in range(0, proj_ref.shape[1], step):
        terms = jnp.dot(values, proj_ref[:, n : n + step], preferred_element_type=F32)
        sums = [
            jnp.sum(terms[r * heads : (r + 1) * heads], axis=0, keepdims=True) for r in range(rows)
        ]
        sums = jnp.concatenate(sums, axis=0)
        out_ref[:, n : n + step] = sums.astype(BF16)


def norm_kernel(residual_ref, gain_ref, *refs):
    hidden_ref, copies_ref = refs[-2:]
    hidden = residual_ref[...].astype(F32) + tree_sum(refs[:-2])
    inverse = lax.rsqrt(jnp.mean(hidden * hidden, axis=-1, keepdims=True) + EPSILON)
    normed = (hidden * inverse * gain_ref[...].astype(F32)[None]).astype(BF16)
    hidden_ref[...] = hidden
    for b in range(copies_ref.shape[0]):
        copies_ref[b] = normed


def expert_kernel(marks_ref, rows_ref, picked_ref, router_ref, gate_up_ref, down_ref, out_ref, act):
    count = act.shape[0]
    rows = rows_ref[...].astype(F32).reshape(count, rows_ref.shape[2]).astype(BF16)
    pairs, cores, group, _ = out_ref.shape
    width, model = down_ref.shape
    logits = jnp.dot(rows, router_ref[...], preferred_element_type=F32)
    score = jnp.where(picked_ref[...] > 0, jax.nn.sigmoid(logits), 0.0)
    expert = lax.broadcasted_iota(jnp.int32, score.shape, 1)
    own = jnp.where(expert == marks_ref[:, group : group + 1], score, 0.0)
    own = jnp.sum(own, axis=-1, keepdims=True)
    weight = (ROUTE_SCALE * own / jnp.sum(score, axis=-1, keepdims=True)).astype(BF16).astype(F32)
    step = 256
    for n in range(0, width, step):
        gate = jnp.dot(rows, gate_up_ref[:, n : n + step], preferred_element_type=F32)
        up = jnp.dot(rows, gate_up_ref[:, width + n : width + n + step], preferred_element_type=F32)
        act[:, n : n + step] = (jax.nn.silu(gate) * up).astype(BF16)
    for n in range(0, model, step):
        answer = jnp.dot(act[...], down_ref[:, n : n + step], preferred_element_type=F32)
        answer = weight * answer.astype(BF16).astype(F32)
        answer = answer.reshape(pairs, cores, group, step).astype(BF16)
        for core in range(cores):
            out_ref[:, core, :, n : n + step] = answer[:, cores - 1 - core]


def shared_kernel(marks_ref, rows_ref, gate_up_ref, down_ref, out_ref, gate_up, down, sems):
    first = pltpu.make_async_copy(gate_up_ref, gate_up, sems.at[0])
    second = pltpu.make_async_copy(down_ref, down, sems.at[1])
    first.start()
    second.start()
    batches, rows, model = rows_ref.shape
    every = rows_ref[...].astype(F32).reshape(batches * rows, model).astype(BF16)
    row = lax.broadcasted_iota(jnp.int32, (8, batches * rows), 0)
    column = lax.broadcasted_iota(jnp.int32, (8, batches * rows), 1)
    first_row = marks_ref[:, rows + 1 : rows + 2]
    chosen = jnp.where((row < rows) & (column == first_row + row), 1.0, 0.0).astype(BF16)
    normed = jnp.dot(chosen, every, preferred_element_type=F32).astype(BF16)
    first.wait()
    gate = jnp.dot(normed, gate_up[0], preferred_element_type=F32)
    up = jnp.dot(normed, gate_up[1], preferred_element_type=F32)
    act = (jax.nn.silu(gate) * up).astype(BF16)
    second.wait()
    out_ref[...] = jnp.dot(act, down[...], preferred_element_type=F32)[:rows]


def gather_sum_kernel(parts_ref, shared_ref, out_ref):
    total = jnp.sum(parts_ref[...].astype(F32), axis=0) + shared_ref[...]
    out_ref[...] = total.astype(BF16)


def final_kernel(hidden_ref, *refs):
    refs[-1][...] = (hidden_ref[...] + tree_sum(refs[:-1])).astype(BF16)


def swaps(arrays):
    size = lax.axis_size("ctx")
    return [
        lax.ppermute(array, "ctx", [(place, place ^ m) for place in range(size)])
        for m, array in enumerate(arrays, 1)
    ]


def crossings(arrays):
    size, count = lax.axis_size("ctx"), lax.axis_size("batch")
    places = [(c, b) for c in range(size) for b in range(count)]
    return [
        lax.ppermute(
            array,
            ("ctx", "batch"),
            [(c * count + b, (c ^ m) * count + (b ^ 1)) for c, b in places],
        )
        for m, array in enumerate(arrays)
    ]


def local(
    queries,
    latent_cache,
    token_latent,
    lengths,
    value_up_weight,
    out_proj,
    residual,
    norm_gain,
    router,
    expert_ids,
    expert_gate_up,
    expert_down,
    shared_gate_up,
    shared_down,
):
    ctx_index = lax.axis_index("ctx")
    ctx_count = lax.axis_size("ctx")
    batch_count = lax.axis_size("batch")
    batch_index = lax.axis_index("batch")
    _, rows, heads, width = queries.shape
    model = residual.shape[-1]
    experts = router.shape[1]
    total_rows = batch_count * rows
    shape = jax.ShapeDtypeStruct

    own_query = queries.reshape(rows * heads, width)
    every_query = [own_query] + swaps([own_query] * (ctx_count - 1))
    valid = lengths - (ctx_index * latent_cache.shape[2]).astype(jnp.int32)
    places = jnp.stack([ctx_index * batch_count + batch_index, (batch_index ^ 1) * rows])
    marks = jnp.concatenate([valid, places.astype(jnp.int32)[None]], axis=1)
    picked = call(
        picked_kernel,
        shape((total_rows, experts), F32),
        [expert_ids.transpose(1, 2, 0)],
        beside=[expert_gate_up],
    )
    *parts, picked = call(
        attend_kernel,
        [shape((2 * rows * heads, width + 128), BF16)]
        + [shape((rows * heads, width + 128), BF16)] * (ctx_count - 1)
        + [shape((total_rows, experts), F32)],
        [marks, *every_query, latent_cache[0], token_latent[0], picked],
        beside=[expert_gate_up] * 3,
    )
    parts = crossings(parts)
    terms = call(
        project_kernel,
        shape((rows, model), BF16),
        [value_up_weight, out_proj, *parts],
    )
    terms = crossings([terms] * ctx_count)
    hidden, copies = call(
        norm_kernel,
        (
            shape((rows, model), F32),
            shape((batch_count, rows, model), BF16),
        ),
        [residual[0], norm_gain, *terms],
        beside=[expert_gate_up] * 4,
    )

    every_rows = lax.all_to_all(copies, "batch", 0, 0)
    weighted = call(
        expert_kernel,
        shape((batch_count // 2, 2, rows, model), BF16),
        [marks, every_rows, picked, router, expert_gate_up[0], expert_down[0]],
        scratch=[pltpu.VMEM((total_rows, expert_down.shape[1]), BF16)],
    )
    weighted = weighted.reshape(batch_count, rows, model)
    weighted = lax.all_to_all(weighted, "batch", 0, 0)
    shared_part = call(
        shared_kernel,
        shape((rows, model), F32),
        [
            marks,
            every_rows,
            pltpu.with_memory_space_constraint(shared_gate_up, pltpu.HBM),
            pltpu.with_memory_space_constraint(shared_down, pltpu.HBM),
        ],
        [VMEM, VMEM, HBM, HBM],
        scratch=[
            pltpu.VMEM(shared_gate_up.shape, BF16),
            pltpu.VMEM(shared_down.shape, BF16),
            pltpu.SemaphoreType.DMA((2,)),
        ],
    )
    totals = call(
        gather_sum_kernel, shape((rows, model), BF16), [weighted, shared_part]
    )
    totals = crossings([totals] * ctx_count)
    return call(final_kernel, shape((rows, model), BF16), [hidden, *totals])[None]


def solution(mesh):
    return jax.shard_map(
        local,
        mesh=mesh,
        in_specs=(
            P("batch", None, "ctx", None),
            P("batch", None, "ctx", None),
            P("batch", None, None),
            P("batch", None),
            P("ctx", None, None),
            P("ctx", None),
            P("batch", None, None),
            P(),
            P(),
            P(),
            P(("ctx", "batch"), None, None),
            P(("ctx", "batch"), None, None),
            P(None, None, "ctx"),
            P("ctx", None),
        ),
        out_specs=P("batch", None, None),
        check_vma=False,
    )
```

time: 69.4 us -> 67.5 us (0.973)
  blocking collectives: 22.5 us -> 17.8 us
  starting transfers between devices: 18.3 us -> 22 us
  Pallas kernels: 10.1 us -> 9.33 us
    all_to_all x1, blocking collectives: 22.5 us -> 17.8 us  [local(): every_rows = lax.all_to_all(copies, 'batch', 0, 0)]
    ppermute x12 -> x15, starting transfers between devices: 14.5 us -> 18.2 us  [the longest x12 14.3 us: crossings(): lax.ppermute(array, ('ctx', 'batch'), [(c * count + b, (c ^ m) * count +...]
    pallas_call x8, Pallas kernels: 10.1 us -> 9.33 us  [call(): pl.pallas_call(body, out_shape=out_shape, in_specs=(specs or [VMEM] * cou...]
    ppermute x12 -> x15, waiting for transfers between devices: 9.39 us -> 9.46 us  [the longest x12 7.46 us: crossings(): lax.ppermute(array, ('ctx', 'batch'), [(c * count + b, (c ^ m) * count +...]
  transfers between devices with their start and end apart: 13 -> 16, of which waited for: 9 -> 8; matrix products, arithmetic and copies ran while one was open for 1% -> 1% of each run, Pallas kernels for 4% -> 4%
where the time goes in v5:
time: 67.5 us; the launch traced here: 67.2 us
  starting transfers between devices  22 us (33%)
  blocking collectives  17.8 us (26%)
  waiting for transfers between devices  16.3 us (24%)
  Pallas kernels  9.33 us (14%)
  other arithmetic  0.81 us (1%)
  local copies, waits for them, and re-layouts  0.77 us (1%)
    all_to_all x1, blocking collectives, local(): every_rows = lax.all_to_all(copies, 'batch', 0, 0)  17.8 us
    ppermute x12, starting transfers between devices, crossings(): lax.ppermute(array, ('ctx', 'batch'), [(c * count + b, (c ^ m) * count +...  14.3 us
    pallas_call x8, Pallas kernels, call(): pl.pallas_call(body, out_shape=out_shape, in_specs=(specs or [VMEM] * cou...  9.33 us
    ppermute x12, waiting for transfers between devices, crossings(): lax.ppermute(array, ('ctx', 'batch'), [(c * count + b, (c ^ m) * count +...  7.46 us
    all_to_all x1, waiting for transfers between devices, local(): weighted = lax.all_to_all(weighted, 'batch', 0, 0)  6.81 us
    ppermute x3, starting transfers between devices, swaps(): lax.ppermute(array, 'ctx', [(place, place ^ m) for place in range(size)])  3.89 us
    all_to_all x1, starting transfers between devices, local(): weighted = lax.all_to_all(weighted, 'batch', 0, 0)  3.79 us
    ppermute x3, waiting for transfers between devices, swaps(): lax.ppermute(array, 'ctx', [(place, place ^ m) for place in range(size)])  2 us
  transfers between devices with their start and end apart: 16, of which 8 were waited for; matrix products, arithmetic and copies ran while one was open for 1% of the time, Pallas kernels for 4%

profile of v5, /device:TPU:1, one launch (start us, length us, event | category | flops | bytes accessed | tf_op | source)
XLA Modules:
  0.0 67.2 jit_solution(10824154330725206273)
XLA Ops:
  0.0 3.3 %collective-permute-start.2 = (bf16[16,512]{1,0:T(8,128)(2,1)}, bf16[16,512]{1,0:T(8,128)(2,1)S(1)}, u32[]{:S(2)}, u32[]{:S(2)}) collective-permute-start(bf16[16,512]{1,0:T(8,128)(2,1)} %bitcast.22), channel_id=1, source_target_pairs={{0,96},{32,64},{64,32},{96,0},{1,97},{33,65},{65,33},{97,1},{2,98}... | collective-permute-start | bytes 49160 | tf_op jit(solution)/shard_map/ppermute | solution.py:222
  4.0 0.7 broadcast_subtract_fusion
  4.7 0.7 %copy-done.5 = s32[32,2,8]{0,2,1:T(8,128)S(1)} copy-done((s32[32,2,8]{0,2,1:T(8,128)S(1)}, s32[32,2,8]{0,2,1:T(8,128)}, u32[]{:S(2)}) %copy-start.5) | copy-done | bytes 2072
  5.6 2.0 %collective-permute-done.1.refs_3_ = bf16[16,512]{1,0:T(8,128)(2,1)S(1)} collective-permute-done((bf16[16,512]{1,0:T(8,128)(2,1)}, bf16[16,512]{1,0:T(8,128)(2,1)S(1)}, u32[]{:S(2)}, u32[]{:S(2)}) %collective-permute-start.1) | collective-permute-done | bytes 16416 | tf_op jit(solution)/shard_map/ppermute | solution.py:222
  7.7 1.1 %shard_map.137 = (bf16[32,640]{1,0:T(8,128)(2,1)S(1)}, bf16[16,640]{1,0:T(8,128)(2,1)S(1)}, bf16[16,640]{1,0:T(8,128)(2,1)S(1)}, bf16[16,640]{1,0:T(8,128)(2,1)S(1)}, f32[64,128]{1,0:T(8,128)S(1)}) custom-call(s32[1,4]{1,0:T(1,128)S(1)} %pad_add_fusion.refs_0_, bf16[16,512]{1,0:T(8,128)(2,1)S(1)} %bitcast.25, ...), custom_call_target="tpu_custom_call" | custom-call | tf_op jit(solution)/shard_map/pallas_call | solution.py:28
  8.8 2.2 %collective-permute-start.3 = (bf16[32,640]{1,0:T(8,128)(2,1)S(1)}, bf16[32,640]{1,0:T(8,128)(2,1)S(1)}, u32[]{:S(2)}, u32[]{:S(2)}) collective-permute-start(bf16[32,640]{1,0:T(8,128)(2,1)S(1)} %get-tuple-element.12), channel_id=1, source_target_pairs={{0,1},{1,0},{2,3},{3,2},{4,5},{5,4},{6,7},{7,6},{8,9},{9,8},{10,11... | collective-permute-start | bytes 122888 | tf_op jit(solution)/shard_map/ppermute | solution.py:231
  11.1 2.8 %collective-permute-start.5 = (bf16[16,640]{1,0:T(8,128)(2,1)S(1)}, bf16[16,640]{1,0:T(8,128)(2,1)S(1)}, u32[]{:S(2)}, u32[]{:S(2)}) collective-permute-start(bf16[16,640]{1,0:T(8,128)(2,1)S(1)} %get-tuple-element.14), channel_id=1, source_target_pairs={{0,65},{1,64},{2,67},{3,66},{4,69},{5,68},{6,71},{7,70},{8,73},{9,... | collective-permute-start | bytes 61448 | tf_op jit(solution)/shard_map/ppermute | solution.py:231
  13.9 1.2 %collective-permute-start.6 = (bf16[16,640]{1,0:T(8,128)(2,1)S(1)}, bf16[16,640]{1,0:T(8,128)(2,1)S(1)}, u32[]{:S(2)}, u32[]{:S(2)}) collective-permute-start(bf16[16,640]{1,0:T(8,128)(2,1)S(1)} %get-tuple-element.15), channel_id=1, source_target_pairs={{0,97},{1,96},{2,99},{3,98},{4,101},{5,100},{6,103},{7,102},{8,105... | collective-permute-start | bytes 61448 | tf_op jit(solution)/shard_map/ppermute | solution.py:231
  15.1 0.8 %collective-permute-done.5.refs_4_ = bf16[16,640]{1,0:T(8,128)(2,1)S(1)} collective-permute-done((bf16[16,640]{1,0:T(8,128)(2,1)S(1)}, bf16[16,640]{1,0:T(8,128)(2,1)S(1)}, u32[]{:S(2)}, u32[]{:S(2)}) %collective-permute-start.5) | collective-permute-done | bytes 20512 | tf_op jit(solution)/shard_map/ppermute | solution.py:231
  15.9 2.4 %collective-permute-done.6.refs_5_ = bf16[16,640]{1,0:T(8,128)(2,1)S(1)} collective-permute-done((bf16[16,640]{1,0:T(8,128)(2,1)S(1)}, bf16[16,640]{1,0:T(8,128)(2,1)S(1)}, u32[]{:S(2)}, u32[]{:S(2)}) %collective-permute-start.6) | collective-permute-done | bytes 20512 | tf_op jit(solution)/shard_map/ppermute | solution.py:231
  18.4 1.4 %shard_map.138 = bf16[2,2304]{1,0:T(2,128)(2,1)S(1)} custom-call(bf16[8,512,128]{2,1,0:T(8,128)(2,1)S(1)} %copy-done.1, bf16[1024,2304]{1,0:T(8,128)(2,1)S(1)} %bitcast.20, bf16[32,640]{1,0:T(8,128)(2,1)S(1)} %collective-permute-done.3.refs_2_, bf16[16,640]{1,0:T(8,128)(2,1)S(1)} %collective-permute-done.4.refs_3_, ...), custom_call_target="tpu_custom_call" | custom-call | tf_op jit(solution)/shard_map/pallas_call | solution.py:28
  19.8 1.3 %collective-permute-start.10 = (bf16[2,2304]{1,0:T(2,128)(2,1)S(1)}, bf16[2,2304]{1,0:T(2,128)(2,1)S(1)}, u32[]{:S(2)}, u32[]{:S(2)}) collective-permute-start(bf16[2,2304]{1,0:T(2,128)(2,1)S(1)} %shard_map.138), channel_id=1, source_target_pairs={{0,97},{1,96},{2,99},{3,98},{4,101},{5,100},{6,103},{7,102},{8,105... | collective-permute-start | bytes 27656 | tf_op jit(solution)/shard_map/ppermute | solution.py:231
  21.1 2.3 %collective-permute-start.8 = (bf16[2,2304]{1,0:T(2,128)(2,1)S(1)}, bf16[2,2304]{1,0:T(2,128)(2,1)S(1)}, u32[]{:S(2)}, u32[]{:S(2)}) collective-permute-start(bf16[2,2304]{1,0:T(2,128)(2,1)S(1)} %shard_map.138), channel_id=1, source_target_pairs={{0,33},{1,32},{2,35},{3,34},{4,37},{5,36},{6,39},{7,38},{8,41},{9,... | collective-permute-start | bytes 27656 | tf_op jit(solution)/shard_map/ppermute | solution.py:231
  24.2 1.5 %collective-permute-done.9.refs_4_ = bf16[2,2304]{1,0:T(2,128)(2,1)S(1)} collective-permute-done((bf16[2,2304]{1,0:T(2,128)(2,1)S(1)}, bf16[2,2304]{1,0:T(2,128)(2,1)S(1)}, u32[]{:S(2)}, u32[]{:S(2)}) %collective-permute-start.9) | collective-permute-done | bytes 9248 | tf_op jit(solution)/shard_map/ppermute | solution.py:231
  25.9 17.8 %all_to_all.10.refs_1_ = bf16[32,2,2304]{2,1,0:T(2,128)(2,1)S(1)} all-to-all(bf16[32,2,2304]{2,1,0:T(2,128)(2,1)S(1)} %get-tuple-element.17), channel_id=1, replica_groups=mesh['ctx'=4,'batch'=32] {'batch'}, dimensions={0} | all-to-all | bytes 589824 | tf_op jit(solution)/shard_map/all_to_all | solution.py:302
  43.8 3.0 %shard_map.140 = bf16[16,2,2,2304]{3,2,1,0:T(2,128)(2,1)} custom-call(s32[1,4]{1,0:T(1,128)S(1)} %pad_add_fusion.refs_0_, bf16[32,2,2304]{2,1,0:T(2,128)(2,1)S(1)} %all_to_all.10.refs_1_, f32[64,128]{1,0:T(8,128)S(1)} %get-tuple-element.18.refs_2_, bf16[2304,128]{1,0:T(8,128)(2,1)S(1)} %copy-done.2, bf16[2304,2048]{1,0:T(8,128)(2,1)S(1)} %bitcast.15, ...), custom_call_target="tpu_custom_call" | custom-call | tf_op jit(solution)/shard_map/pallas_call | solution.py:28
  46.8 3.8 %all-to-all-start.1 = ((bf16[32,2,2304]{2,1,0:T(2,128)(2,1)}), bf16[32,2,2304]{2,1,0:T(2,128)(2,1)S(1)}, u32[]{:S(2)}, u32[]{:S(2)}) async-start(bf16[32,2,2304]{2,1,0:T(2,128)(2,1)} %bitcast.10), calls=%async_computation.1 | async-start | bytes 589824 | tf_op jit(solution)/shard_map/all_to_all | solution.py:310
  50.6 2.5 %shard_map.141.refs_1_ = f32[2,2304]{1,0:T(2,128)S(1)} custom-call(s32[1,4]{1,0:T(1,128)S(1)} %pad_add_fusion.refs_0_, bf16[32,2,2304]{2,1,0:T(2,128)(2,1)S(1)} %all_to_all.10.refs_1_, bf16[2,2304,256]{2,1,0:T(8,128)(2,1)} %refs_2_.1, bf16[256,2304]{1,0:T(8,128)(2,1)} %refs_3_.3), custom_call_target="tpu_custom_call" | custom-call | tf_op jit(solution)/shard_map/pallas_call | solution.py:28
  53.1 6.8 %all-to-all-done.1.refs_0_ = bf16[32,2,2304]{2,1,0:T(2,128)(2,1)S(1)} async-done(((bf16[32,2,2304]{2,1,0:T(2,128)(2,1)}), bf16[32,2,2304]{2,1,0:T(2,128)(2,1)S(1)}, u32[]{:S(2)}, u32[]{:S(2)}) %all-to-all-start.1) | async-done | bytes 294944 | tf_op jit(solution)/shard_map/all_to_all | solution.py:310
  60.2 1.7 %collective-permute-start.14 = (bf16[2,2304]{1,0:T(2,128)(2,1)S(1)}, bf16[2,2304]{1,0:T(2,128)(2,1)S(1)}, u32[]{:S(2)}, u32[]{:S(2)}) collective-permute-start(bf16[2,2304]{1,0:T(2,128)(2,1)S(1)} %shard_map.142), channel_id=1, source_target_pairs={{0,97},{1,96},{2,99},{3,98},{4,101},{5,100},{6,103},{7,102},{8,105... | collective-permute-start | bytes 27656 | tf_op jit(solution)/shard_map/ppermute | solution.py:231
  61.9 1.0 %collective-permute-start.13 = (bf16[2,2304]{1,0:T(2,128)(2,1)S(1)}, bf16[2,2304]{1,0:T(2,128)(2,1)S(1)}, u32[]{:S(2)}, u32[]{:S(2)}) collective-permute-start(bf16[2,2304]{1,0:T(2,128)(2,1)S(1)} %shard_map.142), channel_id=1, source_target_pairs={{0,65},{1,64},{2,67},{3,66},{4,69},{5,68},{6,71},{7,70},{8,73},{9,... | collective-permute-start | bytes 27656 | tf_op jit(solution)/shard_map/ppermute | solution.py:231
  62.9 1.1 %collective-permute-start.12 = (bf16[2,2304]{1,0:T(2,128)(2,1)S(1)}, bf16[2,2304]{1,0:T(2,128)(2,1)S(1)}, u32[]{:S(2)}, u32[]{:S(2)}) collective-permute-start(bf16[2,2304]{1,0:T(2,128)(2,1)S(1)} %shard_map.142), channel_id=1, source_target_pairs={{0,33},{1,32},{2,35},{3,34},{4,37},{5,36},{6,39},{7,38},{8,41},{9,... | collective-permute-start | bytes 27656 | tf_op jit(solution)/shard_map/ppermute | solution.py:231
  64.6 2.0 %collective-permute-done.13.refs_3_ = bf16[2,2304]{1,0:T(2,128)(2,1)S(1)} collective-permute-done((bf16[2,2304]{1,0:T(2,128)(2,1)S(1)}, bf16[2,2304]{1,0:T(2,128)(2,1)S(1)}, u32[]{:S(2)}, u32[]{:S(2)}) %collective-permute-start.13) | collective-permute-done | bytes 9248 | tf_op jit(solution)/shard_map/ppermute | solution.py:231
  66.6 0.6 shard_map.143
  (53 shorter events, 3.0 us)
Async XLA Ops:
  0.0 5.6 %collective-permute-start.2 = (bf16[16,512]{1,0:T(8,128)(2,1)}, bf16[16,512]{1,0:T(8,128)(2,1)S(1)}, u32[]{:S(2)}, u32[]{:S(2)}) collective-permute-start(bf16[16,512]{1,0:T(8,128)(2,1)} %bitcast.22), channel_id=1, source_target_pairs={{0,96},{32,64},{64,32},{96,0},{1,97},{33,65},{65,33},{97,1},{2,98}... | collective-permute-start | bytes 49160 | tf_op jit(solution)/shard_map/ppermute | solution.py:222
  3.3 4.3 %collective-permute-start.1 = (bf16[16,512]{1,0:T(8,128)(2,1)}, bf16[16,512]{1,0:T(8,128)(2,1)S(1)}, u32[]{:S(2)}, u32[]{:S(2)}) collective-permute-start(bf16[16,512]{1,0:T(8,128)(2,1)} %bitcast.23), channel_id=1, source_target_pairs={{0,64},{32,96},{64,0},{96,32},{1,65},{33,97},{65,1},{97,33},{2,66}... | collective-permute-start | bytes 49160 | tf_op jit(solution)/shard_map/ppermute | solution.py:222
  3.8 3.8 %collective-permute-start = (bf16[16,512]{1,0:T(8,128)(2,1)}, bf16[16,512]{1,0:T(8,128)(2,1)S(1)}, u32[]{:S(2)}, u32[]{:S(2)}) collective-permute-start(bf16[16,512]{1,0:T(8,128)(2,1)} %bitcast.24), channel_id=1, source_target_pairs={{0,32},{32,0},{64,96},{96,64},{1,33},{33,1},{65,97},{97,65},{2,34}... | collective-permute-start | bytes 49160 | tf_op jit(solution)/shard_map/ppermute | solution.py:222
  8.8 16.9 %copy-start.4 = (bf16[1,2,2304]{2,1,0:T(2,128)(2,1)S(1)}, bf16[1,2,2304]{2,1,0:T(2,128)(2,1)}, u32[]{:S(2)}) copy-start(bf16[1,2,2304]{2,1,0:T(2,128)(2,1)} %param.20) | copy-start | bytes 27652
  8.8 16.9 %copy-start.6 = (bf16[2304]{0:T(1024)(128)(2,1)S(1)}, bf16[2304]{0:T(1024)(128)(2,1)}, u32[]{:S(2)}) copy-start(bf16[2304]{0:T(1024)(128)(2,1)} %refs_1_.5) | copy-start | bytes 13828
  8.8 9.5 %collective-permute-start.3 = (bf16[32,640]{1,0:T(8,128)(2,1)S(1)}, bf16[32,640]{1,0:T(8,128)(2,1)S(1)}, u32[]{:S(2)}, u32[]{:S(2)}) collective-permute-start(bf16[32,640]{1,0:T(8,128)(2,1)S(1)} %get-tuple-element.12), channel_id=1, source_target_pairs={{0,1},{1,0},{2,3},{3,2},{4,5},{5,4},{6,7},{7,6},{8,9},{9,8},{10,11... | collective-permute-start | bytes 122888 | tf_op jit(solution)/shard_map/ppermute | solution.py:231
  11.0 4.1 %collective-permute-start.4 = (bf16[16,640]{1,0:T(8,128)(2,1)S(1)}, bf16[16,640]{1,0:T(8,128)(2,1)S(1)}, u32[]{:S(2)}, u32[]{:S(2)}) collective-permute-start(bf16[16,640]{1,0:T(8,128)(2,1)S(1)} %get-tuple-element.13), channel_id=1, source_target_pairs={{0,33},{1,32},{2,35},{3,34},{4,37},{5,36},{6,39},{7,38},{8,41},{9,... | collective-permute-start | bytes 61448 | tf_op jit(solution)/shard_map/ppermute | solution.py:231
  11.1 4.7 %collective-permute-start.5 = (bf16[16,640]{1,0:T(8,128)(2,1)S(1)}, bf16[16,640]{1,0:T(8,128)(2,1)S(1)}, u32[]{:S(2)}, u32[]{:S(2)}) collective-permute-start(bf16[16,640]{1,0:T(8,128)(2,1)S(1)} %get-tuple-element.14), channel_id=1, source_target_pairs={{0,65},{1,64},{2,67},{3,66},{4,69},{5,68},{6,71},{7,70},{8,73},{9,... | collective-permute-start | bytes 61448 | tf_op jit(solution)/shard_map/ppermute | solution.py:231
  13.9 4.4 %collective-permute-start.6 = (bf16[16,640]{1,0:T(8,128)(2,1)S(1)}, bf16[16,640]{1,0:T(8,128)(2,1)S(1)}, u32[]{:S(2)}, u32[]{:S(2)}) collective-permute-start(bf16[16,640]{1,0:T(8,128)(2,1)S(1)} %get-tuple-element.15), channel_id=1, source_target_pairs={{0,97},{1,96},{2,99},{3,98},{4,101},{5,100},{6,103},{7,102},{8,105... | collective-permute-start | bytes 61448 | tf_op jit(solution)/shard_map/ppermute | solution.py:231
  18.4 25.4 %slice-start.3 = ((s8[4718592]{0:T(1024)(128)(4,1)}), s8[4194304]{0:T(1024)(128)(4,1)S(1)}, s32[]{:S(2)}) async-start(s8[4718592]{0:T(1024)(128)(4,1)} %bitcast.16), calls=%async_computation.5 | async-start | bytes 8388608
  19.8 4.4 %collective-permute-start.10 = (bf16[2,2304]{1,0:T(2,128)(2,1)S(1)}, bf16[2,2304]{1,0:T(2,128)(2,1)S(1)}, u32[]{:S(2)}, u32[]{:S(2)}) collective-permute-start(bf16[2,2304]{1,0:T(2,128)(2,1)S(1)} %shard_map.138), channel_id=1, source_target_pairs={{0,97},{1,96},{2,99},{3,98},{4,101},{5,100},{6,103},{7,102},{8,105... | collective-permute-start | bytes 27656 | tf_op jit(solution)/shard_map/ppermute | solution.py:231
  21.1 4.6 %collective-permute-start.9 = (bf16[2,2304]{1,0:T(2,128)(2,1)S(1)}, bf16[2,2304]{1,0:T(2,128)(2,1)S(1)}, u32[]{:S(2)}, u32[]{:S(2)}) collective-permute-start(bf16[2,2304]{1,0:T(2,128)(2,1)S(1)} %shard_map.138), channel_id=1, source_target_pairs={{0,65},{1,64},{2,67},{3,66},{4,69},{5,68},{6,71},{7,70},{8,73},{9,... | collective-permute-start | bytes 27656 | tf_op jit(solution)/shard_map/ppermute | solution.py:231
  21.1 4.6 %collective-permute-start.8 = (bf16[2,2304]{1,0:T(2,128)(2,1)S(1)}, bf16[2,2304]{1,0:T(2,128)(2,1)S(1)}, u32[]{:S(2)}, u32[]{:S(2)}) collective-permute-start(bf16[2,2304]{1,0:T(2,128)(2,1)S(1)} %shard_map.138), channel_id=1, source_target_pairs={{0,33},{1,32},{2,35},{3,34},{4,37},{5,36},{6,39},{7,38},{8,41},{9,... | collective-permute-start | bytes 27656 | tf_op jit(solution)/shard_map/ppermute | solution.py:231
  23.4 2.4 %collective-permute-start.7 = (bf16[2,2304]{1,0:T(2,128)(2,1)S(1)}, bf16[2,2304]{1,0:T(2,128)(2,1)S(1)}, u32[]{:S(2)}, u32[]{:S(2)}) collective-permute-start(bf16[2,2304]{1,0:T(2,128)(2,1)S(1)} %shard_map.138), channel_id=1, source_target_pairs={{0,1},{1,0},{2,3},{3,2},{4,5},{5,4},{6,7},{7,6},{8,9},{9,8},{10,11... | collective-permute-start | bytes 27656 | tf_op jit(solution)/shard_map/ppermute | solution.py:231
  25.7 18.0 %slice-start = ((s8[9437184]{0:T(1024)(128)(4,1)}), s8[4194304]{0:T(1024)(128)(4,1)S(1)}, s32[]{:S(2)}) async-start(s8[9437184]{0:T(1024)(128)(4,1)} %bitcast.13), calls=%async_computation.2 | async-start | bytes 8388608
  25.7 18.0 %slice-start.1 = ((s8[9437184]{0:T(1024)(128)(4,1)}), s8[4194304]{0:T(1024)(128)(4,1)S(1)}, s32[]{:S(2)}) async-start(s8[9437184]{0:T(1024)(128)(4,1)} %bitcast.13), calls=%async_computation.3 | async-start | bytes 8388608
  25.8 18.0 %slice-start.2 = ((s8[9437184]{0:T(1024)(128)(4,1)}), s8[1048576]{0:T(1024)(128)(4,1)S(1)}, s32[]{:S(2)}) async-start(s8[9437184]{0:T(1024)(128)(4,1)} %bitcast.13), calls=%async_computation.4 | async-start | bytes 2097152
  25.8 18.0 %slice-start.4 = ((s8[4718592]{0:T(1024)(128)(4,1)}), s8[524288]{0:T(1024)(128)(4,1)S(1)}, s32[]{:S(2)}) async-start(s8[4718592]{0:T(1024)(128)(4,1)} %bitcast.16), calls=%async_computation.6 | async-start | bytes 1048576
  25.8 18.0 %copy-start.2 = (bf16[2304,128]{1,0:T(8,128)(2,1)S(1)}, bf16[2304,128]{1,0:T(8,128)(2,1)}, u32[]{:S(2)}) copy-start(bf16[2304,128]{1,0:T(8,128)(2,1)} %refs_3_.2) | copy-start | bytes 1769476
  46.8 13.1 %all-to-all-start.1 = ((bf16[32,2,2304]{2,1,0:T(2,128)(2,1)}), bf16[32,2,2304]{2,1,0:T(2,128)(2,1)S(1)}, u32[]{:S(2)}, u32[]{:S(2)}) async-start(bf16[32,2,2304]{2,1,0:T(2,128)(2,1)} %bitcast.10), calls=%async_computation.1 | async-start | bytes 589824 | tf_op jit(solution)/shard_map/all_to_all | solution.py:310
  60.2 4.4 %collective-permute-start.14 = (bf16[2,2304]{1,0:T(2,128)(2,1)S(1)}, bf16[2,2304]{1,0:T(2,128)(2,1)S(1)}, u32[]{:S(2)}, u32[]{:S(2)}) collective-permute-start(bf16[2,2304]{1,0:T(2,128)(2,1)S(1)} %shard_map.142), channel_id=1, source_target_pairs={{0,97},{1,96},{2,99},{3,98},{4,101},{5,100},{6,103},{7,102},{8,105... | collective-permute-start | bytes 27656 | tf_op jit(solution)/shard_map/ppermute | solution.py:231
  61.9 4.7 %collective-permute-start.13 = (bf16[2,2304]{1,0:T(2,128)(2,1)S(1)}, bf16[2,2304]{1,0:T(2,128)(2,1)S(1)}, u32[]{:S(2)}, u32[]{:S(2)}) collective-permute-start(bf16[2,2304]{1,0:T(2,128)(2,1)S(1)} %shard_map.142), channel_id=1, source_target_pairs={{0,65},{1,64},{2,67},{3,66},{4,69},{5,68},{6,71},{7,70},{8,73},{9,... | collective-permute-start | bytes 27656 | tf_op jit(solution)/shard_map/ppermute | solution.py:231
  62.9 3.7 %collective-permute-start.12 = (bf16[2,2304]{1,0:T(2,128)(2,1)S(1)}, bf16[2,2304]{1,0:T(2,128)(2,1)S(1)}, u32[]{:S(2)}, u32[]{:S(2)}) collective-permute-start(bf16[2,2304]{1,0:T(2,128)(2,1)S(1)} %shard_map.142), channel_id=1, source_target_pairs={{0,33},{1,32},{2,35},{3,34},{4,37},{5,36},{6,39},{7,38},{8,41},{9,... | collective-permute-start | bytes 27656 | tf_op jit(solution)/shard_map/ppermute | solution.py:231
  64.0 2.6 %collective-permute-start.11 = (bf16[2,2304]{1,0:T(2,128)(2,1)S(1)}, bf16[2,2304]{1,0:T(2,128)(2,1)S(1)}, u32[]{:S(2)}, u32[]{:S(2)}) collective-permute-start(bf16[2,2304]{1,0:T(2,128)(2,1)S(1)} %shard_map.142), channel_id=1, source_target_pairs={{0,1},{1,0},{2,3},{3,2},{4,5},{5,4},{6,7},{7,6},{8,9},{9,8},{10,11... | collective-permute-start | bytes 27656 | tf_op jit(solution)/shard_map/ppermute | solution.py:231
  (7 other events, 41.7 us)

commit v6 on v5

--- a/solution.py
+++ b/solution.py
@@ -48,7 +48,15 @@
     return values[0]
 
 
-def picked_kernel(ids_ref, out_ref):
+def picked_kernel(ids_hbm, lengths_hbm, out_ref, lengths_ref, ids_ref, sems):
+    copies = [
+        pltpu.make_async_copy(ids_hbm, ids_ref, sems.at[0]),
+        pltpu.make_async_copy(lengths_hbm, lengths_ref, sems.at[1]),
+    ]
+    for copy in copies:
+        copy.start()
+    for copy in copies:
+        copy.wait()
     group, choices, count = ids_ref.shape
     total, experts = out_ref.shape
     expert = lax.broadcasted_iota(jnp.int32, (experts, count), 0)
@@ -116,7 +124,7 @@
 
 
 def project_kernel(up_ref, proj_ref, *refs):
-    part_refs, out_ref = refs[:-1], refs[-1]
+    part_refs, out_ref = refs[-2::-1], refs[-1]
     heads, width, _ = up_ref.shape
     rows = out_ref.shape[0]
     count = rows * heads
@@ -163,7 +171,19 @@
         copies_ref[b] = normed
 
 
-def expert_kernel(marks_ref, rows_ref, picked_ref, router_ref, gate_up_ref, down_ref, out_ref, act):
+def expert_kernel(
+    marks_ref,
+    rows_ref,
+    picked_ref,
+    router_ref,
+    gate_up_ref,
+    down_ref,
+    shared_gate_up_ref,
+    shared_down_ref,
+    out_ref,
+    shared_ref,
+    act,
+):
     count = act.shape[0]
     rows = rows_ref[...].astype(F32).reshape(count, rows_ref.shape[2]).astype(BF16)
     pairs, cores, group, _ = out_ref.shape
@@ -185,26 +205,16 @@
         answer = answer.reshape(pairs, cores, group, step).astype(BF16)
         for core in range(cores):
             out_ref[:, core, :, n : n + step] = answer[:, cores - 1 - core]
-
-
-def shared_kernel(marks_ref, rows_ref, gate_up_ref, down_ref, out_ref, gate_up, down, sems):
-    first = pltpu.make_async_copy(gate_up_ref, gate_up, sems.at[0])
-    second = pltpu.make_async_copy(down_ref, down, sems.at[1])
-    first.start()
-    second.start()
-    batches, rows, model = rows_ref.shape
-    every = rows_ref[...].astype(F32).reshape(batches * rows, model).astype(BF16)
-    row = lax.broadcasted_iota(jnp.int32, (8, batches * rows), 0)
-    column = lax.broadcasted_iota(jnp.int32, (8, batches * rows), 1)
-    first_row = marks_ref[:, rows + 1 : rows + 2]
-    chosen = jnp.where((row < rows) & (column == first_row + row), 1.0, 0.0).astype(BF16)
-    normed = jnp.dot(chosen, every, preferred_element_type=F32).astype(BF16)
-    first.wait()
-    gate = jnp.dot(normed, gate_up[0], preferred_element_type=F32)
-    up = jnp.dot(normed, gate_up[1], preferred_element_type=F32)
-    act = (jax.nn.silu(gate) * up).astype(BF16)
-    second.wait()
-    out_ref[...] = jnp.dot(act, down[...], preferred_element_type=F32)[:rows]
+    row = lax.broadcasted_iota(jnp.int32, (8, count), 0)
+    column = lax.broadcasted_iota(jnp.int32, (8, count), 1)
+    first_row = marks_ref[:, group + 1 : group + 2]
+    chosen = jnp.where((row < group) & (column == first_row + row), 1.0, 0.0).astype(BF16)
+    chosen = jnp.dot(chosen, rows, preferred_element_type=F32).astype(BF16)
+    gate = jnp.dot(chosen, shared_gate_up_ref[0], preferred_element_type=F32)
+    up = jnp.dot(chosen, shared_gate_up_ref[1], preferred_element_type=F32)
+    shared = (jax.nn.silu(gate) * up).astype(BF16)
+    shared = jnp.dot(shared, shared_down_ref[...], preferred_element_type=F32)
+    shared_ref[...] = shared[:group]
 
 
 def gather_sum_kernel(parts_ref, shared_ref, out_ref):
@@ -216,11 +226,15 @@
     refs[-1][...] = (hidden_ref[...] + tree_sum(refs[:-1])).astype(BF16)
 
 
-def swaps(arrays):
+def offsets():
+    return [m ^ (m >> 1) for m in range(lax.axis_size("ctx"))]
+
+
+def swaps(array):
     size = lax.axis_size("ctx")
     return [
         lax.ppermute(array, "ctx", [(place, place ^ m) for place in range(size)])
-        for m, array in enumerate(arrays, 1)
+        for m in offsets()[1:]
     ]
 
 
@@ -233,7 +247,7 @@
             ("ctx", "batch"),
             [(c * count + b, (c ^ m) * count + (b ^ 1)) for c, b in places],
         )
-        for m, array in enumerate(arrays)
+        for m, array in zip(offsets(), arrays, strict=True)
     ]
 
 
@@ -264,16 +278,22 @@
     shape = jax.ShapeDtypeStruct
 
     own_query = queries.reshape(rows * heads, width)
-    every_query = [own_query] + swaps([own_query] * (ctx_count - 1))
-    valid = lengths - (ctx_index * latent_cache.shape[2]).astype(jnp.int32)
+    every_query = [own_query] + swaps(own_query)
+    ids = expert_ids.transpose(1, 2, 0)
+    picked, own_lengths = call(
+        picked_kernel,
+        (shape((total_rows, experts), F32), shape(lengths.shape, jnp.int32)),
+        [
+            pltpu.with_memory_space_constraint(ids, pltpu.HBM),
+            pltpu.with_memory_space_constraint(lengths, pltpu.HBM),
+        ],
+        [HBM, HBM],
+        scratch=[pltpu.VMEM(ids.shape, jnp.int32), pltpu.SemaphoreType.DMA((2,))],
+        beside=[expert_gate_up],
+    )
+    valid = own_lengths - (ctx_index * latent_cache.shape[2]).astype(jnp.int32)
     places = jnp.stack([ctx_index * batch_count + batch_index, (batch_index ^ 1) * rows])
     marks = jnp.concatenate([valid, places.astype(jnp.int32)[None]], axis=1)
-    picked = call(
-        picked_kernel,
-        shape((total_rows, experts), F32),
-        [expert_ids.transpose(1, 2, 0)],
-        beside=[expert_gate_up],
-    )
     *parts, picked = call(
         attend_kernel,
         [shape((2 * rows * heads, width + 128), BF16)]
@@ -286,7 +306,7 @@
     terms = call(
         project_kernel,
         shape((rows, model), BF16),
-        [value_up_weight, out_proj, *parts],
+        [value_up_weight, out_proj, *parts[::-1]],
     )
     terms = crossings([terms] * ctx_count)
     hidden, copies = call(
@@ -300,30 +320,26 @@
     )
 
     every_rows = lax.all_to_all(copies, "batch", 0, 0)
-    weighted = call(
+    weighted, shared_part = call(
         expert_kernel,
-        shape((batch_count // 2, 2, rows, model), BF16),
-        [marks, every_rows, picked, router, expert_gate_up[0], expert_down[0]],
-        scratch=[pltpu.VMEM((total_rows, expert_down.shape[1]), BF16)],
-    )
-    weighted = weighted.reshape(batch_count, rows, model)
-    weighted = lax.all_to_all(weighted, "batch", 0, 0)
-    shared_part = call(
-        shared_kernel,
-        shape((rows, model), F32),
+        (
+            shape((batch_count // 2, 2, rows, model), BF16),
+            shape((rows, model), F32),
+        ),
         [
             marks,
             every_rows,
-            pltpu.with_memory_space_constraint(shared_gate_up, pltpu.HBM),
-            pltpu.with_memory_space_constraint(shared_down, pltpu.HBM),
+            picked,
+            router,
+            expert_gate_up[0],
+            expert_down[0],
+            shared_gate_up,
+            shared_down,
         ],
-        [VMEM, VMEM, HBM, HBM],
-        scratch=[
-            pltpu.VMEM(shared_gate_up.shape, BF16),
-            pltpu.VMEM(shared_down.shape, BF16),
-            pltpu.SemaphoreType.DMA((2,)),
-        ],
-    )
+        scratch=[pltpu.VMEM((total_rows, expert_down.shape[1]), BF16)],
+    )
+    weighted = weighted.reshape(batch_count, rows, model)
+    weighted = lax.all_to_all(weighted, "batch", 0, 0)
     totals = call(
         gather_sum_kernel, shape((rows, model), BF16), [weighted, shared_part]
     )

time: 67.5 us -> 64.8 us (0.960)
  blocking collectives: 17.8 us -> 30.5 us
  waiting for transfers between devices: 16.3 us -> 9.92 us
  starting transfers between devices: 22 us -> 16.3 us
  Pallas kernels: 9.33 us -> 7.41 us
  local copies, waits for them, and re-layouts: 0.77 us -> 0.09 us
    all_to_all x0 -> x1, blocking collectives: none -> 12.8 us  [local(): weighted = lax.all_to_all(weighted, 'batch', 0, 0)]
    all_to_all x1 -> x0, waiting for transfers between devices: 6.81 us -> none  [local(): weighted = lax.all_to_all(weighted, 'batch', 0, 0)]
    all_to_all x1 -> x0, starting transfers between devices: 3.79 us -> none  [local(): weighted = lax.all_to_all(weighted, 'batch', 0, 0)]
    ppermute x12, starting transfers between devices: 14.3 us -> 11.9 us  [crossings(): lax.ppermute(array, ('ctx', 'batch'), [(c * count + b, (c ^ m) * count +...]
    pallas_call x8 -> x7, Pallas kernels: 9.33 us -> 7.41 us  [call(): pl.pallas_call(body, out_shape=out_shape, in_specs=(specs or [VMEM] * cou...]
    unnamed x30 -> x32, local copies, waits for them, and re-layouts: 0.77 us -> 0.09 us
  transfers between devices with their start and end apart: 16 -> 15, of which waited for: 8 -> 7; matrix products, arithmetic and copies ran while one was open for 1% -> 0% of each run, Pallas kernels for 4% -> 2%
where the time goes in v6:
time: 64.8 us; the launch traced here: 64.7 us
  blocking collectives  30.5 us (47%)
  starting transfers between devices  16.3 us (25%)
  waiting for transfers between devices  9.92 us (15%)
  Pallas kernels  7.41 us (11%)
    all_to_all x1, blocking collectives, local(): every_rows = lax.all_to_all(copies, 'batch', 0, 0)  17.8 us
    all_to_all x1, blocking collectives, local(): weighted = lax.all_to_all(weighted, 'batch', 0, 0)  12.8 us
    ppermute x12, starting transfers between devices, crossings(): lax.ppermute(array, ('ctx', 'batch'), [(c * count + b, (c ^ m) * count +...  11.9 us
    ppermute x12, waiting for transfers between devices, crossings(): lax.ppermute(array, ('ctx', 'batch'), [(c * count + b, (c ^ m) * count +...  8.02 us
    pallas_call x7, Pallas kernels, call(): pl.pallas_call(body, out_shape=out_shape, in_specs=(specs or [VMEM] * cou...  7.41 us
    ppermute x3, starting transfers between devices, swaps(): lax.ppermute(array, 'ctx', [(place, place ^ m) for place in range(size)])  4.44 us
    ppermute x3, waiting for transfers between devices, swaps(): lax.ppermute(array, 'ctx', [(place, place ^ m) for place in range(size)])  1.9 us
  transfers between devices with their start and end apart: 15, of which 7 were waited for; matrix products, arithmetic and copies ran while one was open for 0% of the time, Pallas kernels for 2%

profile of v6, /device:TPU:1, one launch (start us, length us, event | category | flops | bytes accessed | tf_op | source)
XLA Modules:
  0.0 64.7 jit_solution(15644722192475267128)
XLA Ops:
  0.0 3.6 %collective-permute-start.2 = (bf16[16,512]{1,0:T(8,128)(2,1)}, bf16[16,512]{1,0:T(8,128)(2,1)S(1)}, u32[]{:S(2)}, u32[]{:S(2)}) collective-permute-start(bf16[16,512]{1,0:T(8,128)(2,1)} %bitcast.23), channel_id=1, source_target_pairs={{0,64},{32,96},{64,0},{96,32},{1,65},{33,97},{65,1},{97,33},{2,66}... | collective-permute-start | bytes 49160 | tf_op jit(solution)/shard_map/ppermute | solution.py:236
  3.6 0.9 %collective-permute-start.1 = (bf16[16,512]{1,0:T(8,128)(2,1)}, bf16[16,512]{1,0:T(8,128)(2,1)S(1)}, u32[]{:S(2)}, u32[]{:S(2)}) collective-permute-start(bf16[16,512]{1,0:T(8,128)(2,1)} %bitcast.24), channel_id=1, source_target_pairs={{0,96},{32,64},{64,32},{96,0},{1,97},{33,65},{65,33},{97,1},{2,98}... | collective-permute-start | bytes 49160 | tf_op jit(solution)/shard_map/ppermute | solution.py:236
  4.5 1.1 %shard_map.136 = (f32[64,128]{1,0:T(8,128)S(1)}, s32[1,2]{1,0:T(1,128)S(1)}) custom-call(s32[2,8,32]{2,1,0:T(8,128)} %bitcast.29, s32[1,2]{1,0:T(1,128)} %refs_1_.3, bf16[1,2304,2048]{2,1,0:T(8,128)(2,1)} %refs_9_.3), custom_call_target="tpu_custom_call" | custom-call | tf_op jit(solution)/shard_map/pallas_call | solution.py:28
  5.7 1.9 %collective-permute-done.1.refs_3_ = bf16[16,512]{1,0:T(8,128)(2,1)S(1)} collective-permute-done((bf16[16,512]{1,0:T(8,128)(2,1)}, bf16[16,512]{1,0:T(8,128)(2,1)S(1)}, u32[]{:S(2)}, u32[]{:S(2)}) %collective-permute-start.1) | collective-permute-done | bytes 16416 | tf_op jit(solution)/shard_map/ppermute | solution.py:236
  7.6 1.1 %shard_map.137 = (bf16[32,640]{1,0:T(8,128)(2,1)S(1)}, bf16[16,640]{1,0:T(8,128)(2,1)S(1)}, bf16[16,640]{1,0:T(8,128)(2,1)S(1)}, bf16[16,640]{1,0:T(8,128)(2,1)S(1)}, f32[64,128]{1,0:T(8,128)S(1)}) custom-call(s32[1,4]{1,0:T(1,128)S(1)} %pad_add_fusion.refs_0_, bf16[16,512]{1,0:T(8,128)(2,1)S(1)} %bitcast.26, ...), custom_call_target="tpu_custom_call" | custom-call | tf_op jit(solution)/shard_map/pallas_call | solution.py:28
  8.8 2.2 %collective-permute-start.6 = (bf16[32,640]{1,0:T(8,128)(2,1)S(1)}, bf16[32,640]{1,0:T(8,128)(2,1)S(1)}, u32[]{:S(2)}, u32[]{:S(2)}) collective-permute-start(bf16[32,640]{1,0:T(8,128)(2,1)S(1)} %get-tuple-element.21), channel_id=1, source_target_pairs={{0,1},{1,0},{2,3},{3,2},{4,5},{5,4},{6,7},{7,6},{8,9},{9,8},{10,11... | collective-permute-start | bytes 122888 | tf_op jit(solution)/shard_map/ppermute | solution.py:245
  11.0 1.2 %collective-permute-start.3 = (bf16[16,640]{1,0:T(8,128)(2,1)S(1)}, bf16[16,640]{1,0:T(8,128)(2,1)S(1)}, u32[]{:S(2)}, u32[]{:S(2)}) collective-permute-start(bf16[16,640]{1,0:T(8,128)(2,1)S(1)} %get-tuple-element.18), channel_id=1, source_target_pairs={{0,65},{1,64},{2,67},{3,66},{4,69},{5,68},{6,71},{7,70},{8,73},{9,... | collective-permute-start | bytes 61448 | tf_op jit(solution)/shard_map/ppermute | solution.py:245
  12.1 1.2 %collective-permute-start.4 = (bf16[16,640]{1,0:T(8,128)(2,1)S(1)}, bf16[16,640]{1,0:T(8,128)(2,1)S(1)}, u32[]{:S(2)}, u32[]{:S(2)}) collective-permute-start(bf16[16,640]{1,0:T(8,128)(2,1)S(1)} %get-tuple-element.19), channel_id=1, source_target_pairs={{0,97},{1,96},{2,99},{3,98},{4,101},{5,100},{6,103},{7,102},{8,105... | collective-permute-start | bytes 61448 | tf_op jit(solution)/shard_map/ppermute | solution.py:245
  13.9 1.8 %collective-permute-done.3.refs_2_ = bf16[16,640]{1,0:T(8,128)(2,1)S(1)} collective-permute-done((bf16[16,640]{1,0:T(8,128)(2,1)S(1)}, bf16[16,640]{1,0:T(8,128)(2,1)S(1)}, u32[]{:S(2)}, u32[]{:S(2)}) %collective-permute-start.3) | collective-permute-done | bytes 20512 | tf_op jit(solution)/shard_map/ppermute | solution.py:245
  15.7 0.9 %collective-permute-done.4.refs_3_ = bf16[16,640]{1,0:T(8,128)(2,1)S(1)} collective-permute-done((bf16[16,640]{1,0:T(8,128)(2,1)S(1)}, bf16[16,640]{1,0:T(8,128)(2,1)S(1)}, u32[]{:S(2)}, u32[]{:S(2)}) %collective-permute-start.4) | collective-permute-done | bytes 20512 | tf_op jit(solution)/shard_map/ppermute | solution.py:245
  16.7 1.4 %shard_map.138 = bf16[2,2304]{1,0:T(2,128)(2,1)S(1)} custom-call(bf16[8,512,128]{2,1,0:T(8,128)(2,1)S(1)} %copy-done.3, bf16[1024,2304]{1,0:T(8,128)(2,1)S(1)} %bitcast.17, bf16[16,640]{1,0:T(8,128)(2,1)S(1)} %collective-permute-done.3.refs_2_, bf16[16,640]{1,0:T(8,128)(2,1)S(1)} %collective-permute-done.4.refs_3_, ...), custom_call_target="tpu_custom_call" | custom-call | tf_op jit(solution)/shard_map/pallas_call | solution.py:28
  18.1 2.0 %collective-permute-start.10 = (bf16[2,2304]{1,0:T(2,128)(2,1)S(1)}, bf16[2,2304]{1,0:T(2,128)(2,1)S(1)}, u32[]{:S(2)}, u32[]{:S(2)}) collective-permute-start(bf16[2,2304]{1,0:T(2,128)(2,1)S(1)} %shard_map.138), channel_id=1, source_target_pairs={{0,65},{1,64},{2,67},{3,66},{4,69},{5,68},{6,71},{7,70},{8,73},{9,... | collective-permute-start | bytes 27656 | tf_op jit(solution)/shard_map/ppermute | solution.py:245
  20.1 1.3 %collective-permute-start.9 = (bf16[2,2304]{1,0:T(2,128)(2,1)S(1)}, bf16[2,2304]{1,0:T(2,128)(2,1)S(1)}, u32[]{:S(2)}, u32[]{:S(2)}) collective-permute-start(bf16[2,2304]{1,0:T(2,128)(2,1)S(1)} %shard_map.138), channel_id=1, source_target_pairs={{0,97},{1,96},{2,99},{3,98},{4,101},{5,100},{6,103},{7,102},{8,105... | collective-permute-start | bytes 27656 | tf_op jit(solution)/shard_map/ppermute | solution.py:245
  21.5 1.3 %collective-permute-done.10.refs_5_ = bf16[2,2304]{1,0:T(2,128)(2,1)S(1)} collective-permute-done((bf16[2,2304]{1,0:T(2,128)(2,1)S(1)}, bf16[2,2304]{1,0:T(2,128)(2,1)S(1)}, u32[]{:S(2)}, u32[]{:S(2)}) %collective-permute-start.10) | collective-permute-done | bytes 9248 | tf_op jit(solution)/shard_map/ppermute | solution.py:245
  22.8 1.7 %collective-permute-done.9.refs_4_ = bf16[2,2304]{1,0:T(2,128)(2,1)S(1)} collective-permute-done((bf16[2,2304]{1,0:T(2,128)(2,1)S(1)}, bf16[2,2304]{1,0:T(2,128)(2,1)S(1)}, u32[]{:S(2)}, u32[]{:S(2)}) %collective-permute-start.9) | collective-permute-done | bytes 9248 | tf_op jit(solution)/shard_map/ppermute | solution.py:245
  24.7 17.8 %all_to_all.10.refs_1_ = bf16[32,2,2304]{2,1,0:T(2,128)(2,1)S(1)} all-to-all(bf16[32,2,2304]{2,1,0:T(2,128)(2,1)S(1)} %get-tuple-element.23), channel_id=1, replica_groups=mesh['ctx'=4,'batch'=32] {'batch'}, dimensions={0} | all-to-all | bytes 589824 | tf_op jit(solution)/shard_map/all_to_all | solution.py:322
  42.5 2.7 %shard_map.140 = (bf16[16,2,2,2304]{3,2,1,0:T(2,128)(2,1)S(1)}, f32[2,2304]{1,0:T(2,128)S(1)}) custom-call(s32[1,4]{1,0:T(1,128)S(1)} %pad_add_fusion.refs_0_, bf16[32,2,2304]{2,1,0:T(2,128)(2,1)S(1)} %all_to_all.10.refs_1_, f32[64,128]{1,0:T(8,128)S(1)} %get-tuple-element.24.refs_2_, bf16[2304,128]{1,0:T(8,128)(2,1)S(1)} %copy-done.4, ...), custom_call_target="tpu_custom_call" | custom-call | tf_op jit(solution)/shard_map/pallas_call | solution.py:28
  45.3 12.8 %all_to_all.11.refs_0_ = bf16[32,2,2304]{2,1,0:T(2,128)(2,1)S(1)} all-to-all(bf16[32,2,2304]{2,1,0:T(2,128)(2,1)S(1)} %bitcast.22), channel_id=1, replica_groups=mesh['ctx'=4,'batch'=32] {'batch'}, dimensions={0} | all-to-all | bytes 589824 | tf_op jit(solution)/shard_map/all_to_all | solution.py:342
  58.3 1.4 %collective-permute-start.14 = (bf16[2,2304]{1,0:T(2,128)(2,1)S(1)}, bf16[2,2304]{1,0:T(2,128)(2,1)S(1)}, u32[]{:S(2)}, u32[]{:S(2)}) collective-permute-start(bf16[2,2304]{1,0:T(2,128)(2,1)S(1)} %shard_map.141), channel_id=1, source_target_pairs={{0,65},{1,64},{2,67},{3,66},{4,69},{5,68},{6,71},{7,70},{8,73},{9,... | collective-permute-start | bytes 27656 | tf_op jit(solution)/shard_map/ppermute | solution.py:245
  59.8 1.1 %collective-permute-start.13 = (bf16[2,2304]{1,0:T(2,128)(2,1)S(1)}, bf16[2,2304]{1,0:T(2,128)(2,1)S(1)}, u32[]{:S(2)}, u32[]{:S(2)}) collective-permute-start(bf16[2,2304]{1,0:T(2,128)(2,1)S(1)} %shard_map.141), channel_id=1, source_target_pairs={{0,97},{1,96},{2,99},{3,98},{4,101},{5,100},{6,103},{7,102},{8,105... | collective-permute-start | bytes 27656 | tf_op jit(solution)/shard_map/ppermute | solution.py:245
  60.9 0.6 collective-permute-start.12
  61.7 1.3 %collective-permute-done.14.refs_4_ = bf16[2,2304]{1,0:T(2,128)(2,1)S(1)} collective-permute-done((bf16[2,2304]{1,0:T(2,128)(2,1)S(1)}, bf16[2,2304]{1,0:T(2,128)(2,1)S(1)}, u32[]{:S(2)}, u32[]{:S(2)}) %collective-permute-start.14) | collective-permute-done | bytes 9248 | tf_op jit(solution)/shard_map/ppermute | solution.py:245
  63.0 1.1 %collective-permute-done.13.refs_3_ = bf16[2,2304]{1,0:T(2,128)(2,1)S(1)} collective-permute-done((bf16[2,2304]{1,0:T(2,128)(2,1)S(1)}, bf16[2,2304]{1,0:T(2,128)(2,1)S(1)}, u32[]{:S(2)}, u32[]{:S(2)}) %collective-permute-start.13) | collective-permute-done | bytes 9248 | tf_op jit(solution)/shard_map/ppermute | solution.py:245
  64.1 0.6 shard_map.142
  (53 shorter events, 1.6 us)
Async XLA Ops:
  0.0 5.7 %collective-permute-start.2 = (bf16[16,512]{1,0:T(8,128)(2,1)}, bf16[16,512]{1,0:T(8,128)(2,1)S(1)}, u32[]{:S(2)}, u32[]{:S(2)}) collective-permute-start(bf16[16,512]{1,0:T(8,128)(2,1)} %bitcast.23), channel_id=1, source_target_pairs={{0,64},{32,96},{64,0},{96,32},{1,65},{33,97},{65,1},{97,33},{2,66}... | collective-permute-start | bytes 49160 | tf_op jit(solution)/shard_map/ppermute | solution.py:236
  3.6 4.0 %collective-permute-start.1 = (bf16[16,512]{1,0:T(8,128)(2,1)}, bf16[16,512]{1,0:T(8,128)(2,1)S(1)}, u32[]{:S(2)}, u32[]{:S(2)}) collective-permute-start(bf16[16,512]{1,0:T(8,128)(2,1)} %bitcast.24), channel_id=1, source_target_pairs={{0,96},{32,64},{64,32},{96,0},{1,97},{33,65},{65,33},{97,1},{2,98}... | collective-permute-start | bytes 49160 | tf_op jit(solution)/shard_map/ppermute | solution.py:236
  4.4 3.2 %collective-permute-start = (bf16[16,512]{1,0:T(8,128)(2,1)}, bf16[16,512]{1,0:T(8,128)(2,1)S(1)}, u32[]{:S(2)}, u32[]{:S(2)}) collective-permute-start(bf16[16,512]{1,0:T(8,128)(2,1)} %bitcast.25), channel_id=1, source_target_pairs={{0,32},{32,0},{64,96},{96,64},{1,33},{33,1},{65,97},{97,65},{2,34}... | collective-permute-start | bytes 49160 | tf_op jit(solution)/shard_map/ppermute | solution.py:236
  8.8 15.7 %copy-start.6 = (bf16[1,2,2304]{2,1,0:T(2,128)(2,1)S(1)}, bf16[1,2,2304]{2,1,0:T(2,128)(2,1)}, u32[]{:S(2)}) copy-start(bf16[1,2,2304]{2,1,0:T(2,128)(2,1)} %param.20) | copy-start | bytes 27652
  8.8 7.8 %collective-permute-start.6 = (bf16[32,640]{1,0:T(8,128)(2,1)S(1)}, bf16[32,640]{1,0:T(8,128)(2,1)S(1)}, u32[]{:S(2)}, u32[]{:S(2)}) collective-permute-start(bf16[32,640]{1,0:T(8,128)(2,1)S(1)} %get-tuple-element.21), channel_id=1, source_target_pairs={{0,1},{1,0},{2,3},{3,2},{4,5},{5,4},{6,7},{7,6},{8,9},{9,8},{10,11... | collective-permute-start | bytes 122888 | tf_op jit(solution)/shard_map/ppermute | solution.py:245
  11.0 4.7 %collective-permute-start.3 = (bf16[16,640]{1,0:T(8,128)(2,1)S(1)}, bf16[16,640]{1,0:T(8,128)(2,1)S(1)}, u32[]{:S(2)}, u32[]{:S(2)}) collective-permute-start(bf16[16,640]{1,0:T(8,128)(2,1)S(1)} %get-tuple-element.18), channel_id=1, source_target_pairs={{0,65},{1,64},{2,67},{3,66},{4,69},{5,68},{6,71},{7,70},{8,73},{9,... | collective-permute-start | bytes 61448 | tf_op jit(solution)/shard_map/ppermute | solution.py:245
  12.1 4.5 %collective-permute-start.4 = (bf16[16,640]{1,0:T(8,128)(2,1)S(1)}, bf16[16,640]{1,0:T(8,128)(2,1)S(1)}, u32[]{:S(2)}, u32[]{:S(2)}) collective-permute-start(bf16[16,640]{1,0:T(8,128)(2,1)S(1)} %get-tuple-element.19), channel_id=1, source_target_pairs={{0,97},{1,96},{2,99},{3,98},{4,101},{5,100},{6,103},{7,102},{8,105... | collective-permute-start | bytes 61448 | tf_op jit(solution)/shard_map/ppermute | solution.py:245
  13.3 3.3 %collective-permute-start.5 = (bf16[16,640]{1,0:T(8,128)(2,1)S(1)}, bf16[16,640]{1,0:T(8,128)(2,1)S(1)}, u32[]{:S(2)}, u32[]{:S(2)}) collective-permute-start(bf16[16,640]{1,0:T(8,128)(2,1)S(1)} %get-tuple-element.20), channel_id=1, source_target_pairs={{0,33},{1,32},{2,35},{3,34},{4,37},{5,36},{6,39},{7,38},{8,41},{9,... | collective-permute-start | bytes 61448 | tf_op jit(solution)/shard_map/ppermute | solution.py:245
  16.6 25.8 %slice-start.5 = ((s8[4718592]{0:T(1024)(128)(4,1)}), s8[524288]{0:T(1024)(128)(4,1)S(1)}, s32[]{:S(2)}) async-start(s8[4718592]{0:T(1024)(128)(4,1)} %bitcast.18), calls=%async_computation.7 | async-start | bytes 1048576
  18.1 4.7 %collective-permute-start.10 = (bf16[2,2304]{1,0:T(2,128)(2,1)S(1)}, bf16[2,2304]{1,0:T(2,128)(2,1)S(1)}, u32[]{:S(2)}, u32[]{:S(2)}) collective-permute-start(bf16[2,2304]{1,0:T(2,128)(2,1)S(1)} %shard_map.138), channel_id=1, source_target_pairs={{0,65},{1,64},{2,67},{3,66},{4,69},{5,68},{6,71},{7,70},{8,73},{9,... | collective-permute-start | bytes 27656 | tf_op jit(solution)/shard_map/ppermute | solution.py:245
  20.1 4.3 %collective-permute-start.9 = (bf16[2,2304]{1,0:T(2,128)(2,1)S(1)}, bf16[2,2304]{1,0:T(2,128)(2,1)S(1)}, u32[]{:S(2)}, u32[]{:S(2)}) collective-permute-start(bf16[2,2304]{1,0:T(2,128)(2,1)S(1)} %shard_map.138), channel_id=1, source_target_pairs={{0,97},{1,96},{2,99},{3,98},{4,101},{5,100},{6,103},{7,102},{8,105... | collective-permute-start | bytes 27656 | tf_op jit(solution)/shard_map/ppermute | solution.py:245
  21.3 3.1 %collective-permute-start.8 = (bf16[2,2304]{1,0:T(2,128)(2,1)S(1)}, bf16[2,2304]{1,0:T(2,128)(2,1)S(1)}, u32[]{:S(2)}, u32[]{:S(2)}) collective-permute-start(bf16[2,2304]{1,0:T(2,128)(2,1)S(1)} %shard_map.138), channel_id=1, source_target_pairs={{0,33},{1,32},{2,35},{3,34},{4,37},{5,36},{6,39},{7,38},{8,41},{9,... | collective-permute-start | bytes 27656 | tf_op jit(solution)/shard_map/ppermute | solution.py:245
  21.4 3.0 %collective-permute-start.7 = (bf16[2,2304]{1,0:T(2,128)(2,1)S(1)}, bf16[2,2304]{1,0:T(2,128)(2,1)S(1)}, u32[]{:S(2)}, u32[]{:S(2)}) collective-permute-start(bf16[2,2304]{1,0:T(2,128)(2,1)S(1)} %shard_map.138), channel_id=1, source_target_pairs={{0,1},{1,0},{2,3},{3,2},{4,5},{5,4},{6,7},{7,6},{8,9},{9,8},{10,11... | collective-permute-start | bytes 27656 | tf_op jit(solution)/shard_map/ppermute | solution.py:245
  24.4 18.0 %slice-start = ((s8[9437184]{0:T(1024)(128)(4,1)}), s8[4194304]{0:T(1024)(128)(4,1)S(1)}, s32[]{:S(2)}) async-start(s8[9437184]{0:T(1024)(128)(4,1)} %bitcast.13), calls=%async_computation.2 | async-start | bytes 8388608
  24.5 18.0 %slice-start.1 = ((s8[9437184]{0:T(1024)(128)(4,1)}), s8[4194304]{0:T(1024)(128)(4,1)S(1)}, s32[]{:S(2)}) async-start(s8[9437184]{0:T(1024)(128)(4,1)} %bitcast.13), calls=%async_computation.3 | async-start | bytes 8388608
  24.5 18.0 %slice-start.2 = ((s8[9437184]{0:T(1024)(128)(4,1)}), s8[1048576]{0:T(1024)(128)(4,1)S(1)}, s32[]{:S(2)}) async-start(s8[9437184]{0:T(1024)(128)(4,1)} %bitcast.13), calls=%async_computation.4 | async-start | bytes 2097152
  24.5 18.0 %slice-start.6 = ((s8[4718592]{0:T(1024)(128)(4,1)}), s8[4194304]{0:T(1024)(128)(4,1)S(1)}, s32[]{:S(2)}) async-start(s8[4718592]{0:T(1024)(128)(4,1)} %bitcast.18), calls=%async_computation.8 | async-start | bytes 8388608
  24.5 18.0 %copy-start = (bf16[2,2304,256]{2,1,0:T(8,128)(2,1)S(1)}, bf16[2,2304,256]{2,1,0:T(8,128)(2,1)}, u32[]{:S(2)}) copy-start(bf16[2,2304,256]{2,1,0:T(8,128)(2,1)} %refs_6_.3) | copy-start | bytes 7077892
  24.5 18.0 %copy-start.2 = (bf16[256,2304]{1,0:T(8,128)(2,1)S(1)}, bf16[256,2304]{1,0:T(8,128)(2,1)}, u32[]{:S(2)}) copy-start(bf16[256,2304]{1,0:T(8,128)(2,1)} %refs_7_.3) | copy-start | bytes 3538948
  24.5 18.0 %copy-start.4 = (bf16[2304,128]{1,0:T(8,128)(2,1)S(1)}, bf16[2304,128]{1,0:T(8,128)(2,1)}, u32[]{:S(2)}) copy-start(bf16[2304,128]{1,0:T(8,128)(2,1)} %refs_3_.1) | copy-start | bytes 1769476
  58.3 4.7 %collective-permute-start.14 = (bf16[2,2304]{1,0:T(2,128)(2,1)S(1)}, bf16[2,2304]{1,0:T(2,128)(2,1)S(1)}, u32[]{:S(2)}, u32[]{:S(2)}) collective-permute-start(bf16[2,2304]{1,0:T(2,128)(2,1)S(1)} %shard_map.141), channel_id=1, source_target_pairs={{0,65},{1,64},{2,67},{3,66},{4,69},{5,68},{6,71},{7,70},{8,73},{9,... | collective-permute-start | bytes 27656 | tf_op jit(solution)/shard_map/ppermute | solution.py:245
  59.8 4.3 %collective-permute-start.13 = (bf16[2,2304]{1,0:T(2,128)(2,1)S(1)}, bf16[2,2304]{1,0:T(2,128)(2,1)S(1)}, u32[]{:S(2)}, u32[]{:S(2)}) collective-permute-start(bf16[2,2304]{1,0:T(2,128)(2,1)S(1)} %shard_map.141), channel_id=1, source_target_pairs={{0,97},{1,96},{2,99},{3,98},{4,101},{5,100},{6,103},{7,102},{8,105... | collective-permute-start | bytes 27656 | tf_op jit(solution)/shard_map/ppermute | solution.py:245
  60.9 3.2 %collective-permute-start.12 = (bf16[2,2304]{1,0:T(2,128)(2,1)S(1)}, bf16[2,2304]{1,0:T(2,128)(2,1)S(1)}, u32[]{:S(2)}, u32[]{:S(2)}) collective-permute-start(bf16[2,2304]{1,0:T(2,128)(2,1)S(1)} %shard_map.141), channel_id=1, source_target_pairs={{0,33},{1,32},{2,35},{3,34},{4,37},{5,36},{6,39},{7,38},{8,41},{9,... | collective-permute-start | bytes 27656 | tf_op jit(solution)/shard_map/ppermute | solution.py:245
  61.5 2.6 %collective-permute-start.11 = (bf16[2,2304]{1,0:T(2,128)(2,1)S(1)}, bf16[2,2304]{1,0:T(2,128)(2,1)S(1)}, u32[]{:S(2)}, u32[]{:S(2)}) collective-permute-start(bf16[2,2304]{1,0:T(2,128)(2,1)S(1)} %shard_map.141), channel_id=1, source_target_pairs={{0,1},{1,0},{2,3},{3,2},{4,5},{5,4},{6,7},{7,6},{8,9},{9,8},{10,11... | collective-permute-start | bytes 27656 | tf_op jit(solution)/shard_map/ppermute | solution.py:245
  (7 other events, 55.0 us)

commit v7 on v6

--- a/solution.py
+++ b/solution.py
@@ -46,6 +46,13 @@
     while len(values) > 1:
         values = [a + b for a, b in zip(values[::2], values[1::2])]
     return values[0]
+
+
+def by_heads(token, heads):
+    token = token.astype(F32)
+    rows, width = token.shape
+    token = [jnp.broadcast_to(token[r : r + 1], (heads, width)) for r in range(rows)]
+    return jnp.concatenate(token, axis=0)
 
 
 def picked_kernel(ids_hbm, lengths_hbm, out_ref, lengths_ref, ids_ref, sems):
@@ -111,25 +118,20 @@
         part = jnp.concatenate([blend[there] for blend in blends])
         tail = jnp.concatenate([tail[there] for tail in tails])
         if m == 0:
-            token = token_ref[...].astype(F32)
-            token = [jnp.broadcast_to(token[r : r + 1], (heads, width)) for r in range(rows)]
-            token = jnp.concatenate(token, axis=0)
+            token = by_heads(token_ref[...], heads)
             fresh = jnp.sum(every[0] * token, axis=-1, keepdims=True) * SCALE
             for place, piece in enumerate(split(fresh), 6):
                 tail = jnp.where(lane[: rows * heads] == place, piece, tail)
-            part_ref[rows * heads :, :width] = token.astype(BF16)
-            part_ref[rows * heads :, width:] = jnp.zeros((rows * heads, 128), BF16)
-        part_ref[: rows * heads, :width] = part.astype(BF16)
-        part_ref[: rows * heads, width:] = tail.astype(BF16)
-
-
-def project_kernel(up_ref, proj_ref, *refs):
+        part_ref[:, :width] = part.astype(BF16)
+        part_ref[:, width:] = tail.astype(BF16)
+
+
+def project_kernel(up_ref, proj_ref, token_ref, *refs):
     part_refs, out_ref = refs[-2::-1], refs[-1]
     heads, width, _ = up_ref.shape
     rows = out_ref.shape[0]
-    count = rows * heads
-    token = part_refs[0][count:, :width].astype(F32)
-    tails = [part_ref[:count, width:].astype(F32) for part_ref in part_refs]
+    token = by_heads(token_ref[...], heads)
+    tails = [part_ref[:, width:].astype(F32) for part_ref in part_refs]
     peaks = [tail[:, 0:1] + (tail[:, 1:2] + tail[:, 2:3]) for tail in tails]
     masses = [tail[:, 3:4] + (tail[:, 4:5] + tail[:, 5:6]) for tail in tails]
     fresh = tails[0][:, 6:7] + (tails[0][:, 7:8] + tails[0][:, 8:9])
@@ -139,7 +141,7 @@
     for there, peak, part_ref in zip(masses, peaks, part_refs):
         factor = jnp.exp(peak - top)
         mass = mass + there * factor
-        blend = blend + part_ref[:count, :width].astype(F32) * factor
+        blend = blend + part_ref[:, :width].astype(F32) * factor
     latent = (blend / mass).astype(BF16)
     head = lax.rem(
         lax.broadcasted_iota(jnp.int32, (rows * heads, up_ref.shape[2]), 0), jnp.int32(heads)
@@ -247,7 +249,7 @@
             ("ctx", "batch"),
             [(c * count + b, (c ^ m) * count + (b ^ 1)) for c, b in places],
         )
-        for m, array in zip(offsets(), arrays, strict=True)
+        for m, array in zip(offsets(), arrays)
     ]
 
 
@@ -279,6 +281,7 @@
 
     own_query = queries.reshape(rows * heads, width)
     every_query = [own_query] + swaps(own_query)
+    other_token = crossings([token_latent[0]])[0]
     ids = expert_ids.transpose(1, 2, 0)
     picked, own_lengths = call(
         picked_kernel,
@@ -296,8 +299,7 @@
     marks = jnp.concatenate([valid, places.astype(jnp.int32)[None]], axis=1)
     *parts, picked = call(
         attend_kernel,
-        [shape((2 * rows * heads, width + 128), BF16)]
-        + [shape((rows * heads, width + 128), BF16)] * (ctx_count - 1)
+        [shape((rows * heads, width + 128), BF16)] * ctx_count
         + [shape((total_rows, experts), F32)],
         [marks, *every_query, latent_cache[0], token_latent[0], picked],
         beside=[expert_gate_up] * 3,
@@ -306,7 +308,7 @@
     terms = call(
         project_kernel,
         shape((rows, model), BF16),
-        [value_up_weight, out_proj, *parts[::-1]],
+        [value_up_weight, out_proj, other_token, *parts[::-1]],
     )
     terms = crossings([terms] * ctx_count)
     hidden, copies = call(

time: 64.8 us -> 64.4 us (level)
  waiting for transfers between devices: 9.92 us -> 9.06 us
    ppermute x12 -> x13, waiting for transfers between devices: 8.02 us -> 7.16 us  [crossings(): lax.ppermute(array, ('ctx', 'batch'), [(c * count + b, (c ^ m) * count +...]
    ppermute x12 -> x13, starting transfers between devices: 11.9 us -> 12.5 us  [crossings(): lax.ppermute(array, ('ctx', 'batch'), [(c * count + b, (c ^ m) * count +...]
  transfers between devices with their start and end apart: 15 -> 16, of which waited for: 7 -> 7; matrix products, arithmetic and copies ran while one was open for 0% -> 0% of each run, Pallas kernels for 2% -> 2%
where the time goes in v7:
time: 64.4 us; the launch traced here: 64.3 us
  blocking collectives  30.4 us (47%)
  starting transfers between devices  16.9 us (26%)
  waiting for transfers between devices  9.06 us (14%)
  Pallas kernels  7.41 us (12%)
    all_to_all x1, blocking collectives, local(): every_rows = lax.all_to_all(copies, 'batch', 0, 0)  17.7 us
    all_to_all x1, blocking collectives, local(): weighted = lax.all_to_all(weighted, 'batch', 0, 0)  12.8 us
    ppermute x13, starting transfers between devices, crossings(): lax.ppermute(array, ('ctx', 'batch'), [(c * count + b, (c ^ m) * count +...  12.5 us
    pallas_call x7, Pallas kernels, call(): pl.pallas_call(body, out_shape=out_shape, in_specs=(specs or [VMEM] * cou...  7.41 us
    ppermute x13, waiting for transfers between devices, crossings(): lax.ppermute(array, ('ctx', 'batch'), [(c * count + b, (c ^ m) * count +...  7.16 us
    ppermute x3, starting transfers between devices, swaps(): lax.ppermute(array, 'ctx', [(place, place ^ m) for place in range(size)])  4.44 us
    ppermute x3, waiting for transfers between devices, swaps(): lax.ppermute(array, 'ctx', [(place, place ^ m) for place in range(size)])  1.9 us
  transfers between devices with their start and end apart: 16, of which 7 were waited for; matrix products, arithmetic and copies ran while one was open for 0% of the time, Pallas kernels for 2%

profile of v7, /device:TPU:1, one launch (start us, length us, event | category | flops | bytes accessed | tf_op | source)
XLA Modules:
  0.0 64.3 jit_solution(7305252359525009251)
XLA Ops:
  0.0 3.6 %collective-permute-start.3 = (bf16[16,512]{1,0:T(8,128)(2,1)}, bf16[16,512]{1,0:T(8,128)(2,1)S(1)}, u32[]{:S(2)}, u32[]{:S(2)}) collective-permute-start(bf16[16,512]{1,0:T(8,128)(2,1)} %bitcast.23), channel_id=1, source_target_pairs={{0,64},{32,96},{64,0},{96,32},{1,65},{33,97},{65,1},{97,33},{2,66}... | collective-permute-start | bytes 49160 | tf_op jit(solution)/shard_map/ppermute | solution.py:238
  3.6 0.9 %collective-permute-start.2 = (bf16[16,512]{1,0:T(8,128)(2,1)}, bf16[16,512]{1,0:T(8,128)(2,1)S(1)}, u32[]{:S(2)}, u32[]{:S(2)}) collective-permute-start(bf16[16,512]{1,0:T(8,128)(2,1)} %bitcast.24), channel_id=1, source_target_pairs={{0,96},{32,64},{64,32},{96,0},{1,97},{33,65},{65,33},{97,1},{2,98}... | collective-permute-start | bytes 49160 | tf_op jit(solution)/shard_map/ppermute | solution.py:238
  4.5 1.1 %shard_map.136 = (f32[64,128]{1,0:T(8,128)S(1)}, s32[1,2]{1,0:T(1,128)S(1)}) custom-call(s32[2,8,32]{2,1,0:T(8,128)} %bitcast.30, s32[1,2]{1,0:T(1,128)} %refs_1_.3, bf16[1,2304,2048]{2,1,0:T(8,128)(2,1)} %refs_9_.3), custom_call_target="tpu_custom_call" | custom-call | tf_op jit(solution)/shard_map/pallas_call | solution.py:28
  5.7 1.9 %collective-permute-done.2.refs_3_ = bf16[16,512]{1,0:T(8,128)(2,1)S(1)} collective-permute-done((bf16[16,512]{1,0:T(8,128)(2,1)}, bf16[16,512]{1,0:T(8,128)(2,1)S(1)}, u32[]{:S(2)}, u32[]{:S(2)}) %collective-permute-start.2) | collective-permute-done | bytes 16416 | tf_op jit(solution)/shard_map/ppermute | solution.py:238
  7.6 1.1 %shard_map.137 = (bf16[16,640]{1,0:T(8,128)(2,1)S(1)}, bf16[16,640]{1,0:T(8,128)(2,1)S(1)}, bf16[16,640]{1,0:T(8,128)(2,1)S(1)}, bf16[16,640]{1,0:T(8,128)(2,1)S(1)}, f32[64,128]{1,0:T(8,128)S(1)}) custom-call(s32[1,4]{1,0:T(1,128)S(1)} %pad_add_fusion.refs_0_, bf16[16,512]{1,0:T(8,128)(2,1)S(1)} %bitcast.26, ...), custom_call_target="tpu_custom_call" | custom-call | tf_op jit(solution)/shard_map/pallas_call | solution.py:28
  8.8 3.3 %collective-permute-start.4 = (bf16[16,640]{1,0:T(8,128)(2,1)S(1)}, bf16[16,640]{1,0:T(8,128)(2,1)S(1)}, u32[]{:S(2)}, u32[]{:S(2)}) collective-permute-start(bf16[16,640]{1,0:T(8,128)(2,1)S(1)} %get-tuple-element.18), channel_id=1, source_target_pairs={{0,65},{1,64},{2,67},{3,66},{4,69},{5,68},{6,71},{7,70},{8,73},{9,... | collective-permute-start | bytes 61448 | tf_op jit(solution)/shard_map/ppermute | solution.py:247
  12.1 0.6 collective-permute-start.5
  12.7 1.1 %collective-permute-start.6 = (bf16[16,640]{1,0:T(8,128)(2,1)S(1)}, bf16[16,640]{1,0:T(8,128)(2,1)S(1)}, u32[]{:S(2)}, u32[]{:S(2)}) collective-permute-start(bf16[16,640]{1,0:T(8,128)(2,1)S(1)} %get-tuple-element.20), channel_id=1, source_target_pairs={{0,33},{1,32},{2,35},{3,34},{4,37},{5,36},{6,39},{7,38},{8,41},{9,... | collective-permute-start | bytes 61448 | tf_op jit(solution)/shard_map/ppermute | solution.py:247
  14.3 0.8 %collective-permute-done.refs_2_ = bf16[2,512]{1,0:T(2,128)(2,1)S(1)} collective-permute-done((bf16[2,512]{1,0:T(2,128)(2,1)S(1)}, bf16[2,512]{1,0:T(2,128)(2,1)S(1)}, u32[]{:S(2)}, u32[]{:S(2)}) %collective-permute-start) | collective-permute-done | bytes 2080 | tf_op jit(solution)/shard_map/ppermute | solution.py:247
  15.1 1.4 %collective-permute-done.5.refs_4_ = bf16[16,640]{1,0:T(8,128)(2,1)S(1)} collective-permute-done((bf16[16,640]{1,0:T(8,128)(2,1)S(1)}, bf16[16,640]{1,0:T(8,128)(2,1)S(1)}, u32[]{:S(2)}, u32[]{:S(2)}) %collective-permute-start.5) | collective-permute-done | bytes 20512 | tf_op jit(solution)/shard_map/ppermute | solution.py:247
  16.5 1.4 %shard_map.138 = bf16[2,2304]{1,0:T(2,128)(2,1)S(1)} custom-call(bf16[8,512,128]{2,1,0:T(8,128)(2,1)S(1)} %copy-done.3, bf16[1024,2304]{1,0:T(8,128)(2,1)S(1)} %bitcast.17, bf16[2,512]{1,0:T(2,128)(2,1)S(1)} %collective-permute-done.refs_2_, bf16[16,640]{1,0:T(8,128)(2,1)S(1)} %collective-permute-done.4.refs_3_, ...), custom_call_target="tpu_custom_call" | custom-call | tf_op jit(solution)/shard_map/pallas_call | solution.py:28
  18.0 2.0 %collective-permute-start.11 = (bf16[2,2304]{1,0:T(2,128)(2,1)S(1)}, bf16[2,2304]{1,0:T(2,128)(2,1)S(1)}, u32[]{:S(2)}, u32[]{:S(2)}) collective-permute-start(bf16[2,2304]{1,0:T(2,128)(2,1)S(1)} %shard_map.138), channel_id=1, source_target_pairs={{0,65},{1,64},{2,67},{3,66},{4,69},{5,68},{6,71},{7,70},{8,73},{9,... | collective-permute-start | bytes 27656 | tf_op jit(solution)/shard_map/ppermute | solution.py:247
  20.0 1.1 %collective-permute-start.10 = (bf16[2,2304]{1,0:T(2,128)(2,1)S(1)}, bf16[2,2304]{1,0:T(2,128)(2,1)S(1)}, u32[]{:S(2)}, u32[]{:S(2)}) collective-permute-start(bf16[2,2304]{1,0:T(2,128)(2,1)S(1)} %shard_map.138), channel_id=1, source_target_pairs={{0,97},{1,96},{2,99},{3,98},{4,101},{5,100},{6,103},{7,102},{8,105... | collective-permute-start | bytes 27656 | tf_op jit(solution)/shard_map/ppermute | solution.py:247
  21.5 1.1 %collective-permute-done.11.refs_5_ = bf16[2,2304]{1,0:T(2,128)(2,1)S(1)} collective-permute-done((bf16[2,2304]{1,0:T(2,128)(2,1)S(1)}, bf16[2,2304]{1,0:T(2,128)(2,1)S(1)}, u32[]{:S(2)}, u32[]{:S(2)}) %collective-permute-start.11) | collective-permute-done | bytes 9248 | tf_op jit(solution)/shard_map/ppermute | solution.py:247
  22.6 1.7 %collective-permute-done.10.refs_4_ = bf16[2,2304]{1,0:T(2,128)(2,1)S(1)} collective-permute-done((bf16[2,2304]{1,0:T(2,128)(2,1)S(1)}, bf16[2,2304]{1,0:T(2,128)(2,1)S(1)}, u32[]{:S(2)}, u32[]{:S(2)}) %collective-permute-start.10) | collective-permute-done | bytes 9248 | tf_op jit(solution)/shard_map/ppermute | solution.py:247
  24.6 17.7 %all_to_all.10.refs_1_ = bf16[32,2,2304]{2,1,0:T(2,128)(2,1)S(1)} all-to-all(bf16[32,2,2304]{2,1,0:T(2,128)(2,1)S(1)} %get-tuple-element.23), channel_id=1, replica_groups=mesh['ctx'=4,'batch'=32] {'batch'}, dimensions={0} | all-to-all | bytes 589824 | tf_op jit(solution)/shard_map/all_to_all | solution.py:324
  42.3 2.7 %shard_map.140 = (bf16[16,2,2,2304]{3,2,1,0:T(2,128)(2,1)S(1)}, f32[2,2304]{1,0:T(2,128)S(1)}) custom-call(s32[1,4]{1,0:T(1,128)S(1)} %pad_add_fusion.refs_0_, bf16[32,2,2304]{2,1,0:T(2,128)(2,1)S(1)} %all_to_all.10.refs_1_, f32[64,128]{1,0:T(8,128)S(1)} %get-tuple-element.24.refs_2_, bf16[2304,128]{1,0:T(8,128)(2,1)S(1)} %copy-done.4, ...), custom_call_target="tpu_custom_call" | custom-call | tf_op jit(solution)/shard_map/pallas_call | solution.py:28
  45.0 12.8 %all_to_all.11.refs_0_ = bf16[32,2,2304]{2,1,0:T(2,128)(2,1)S(1)} all-to-all(bf16[32,2,2304]{2,1,0:T(2,128)(2,1)S(1)} %bitcast.22), channel_id=1, replica_groups=mesh['ctx'=4,'batch'=32] {'batch'}, dimensions={0} | all-to-all | bytes 589824 | tf_op jit(solution)/shard_map/all_to_all | solution.py:344
  58.1 1.3 %collective-permute-start.15 = (bf16[2,2304]{1,0:T(2,128)(2,1)S(1)}, bf16[2,2304]{1,0:T(2,128)(2,1)S(1)}, u32[]{:S(2)}, u32[]{:S(2)}) collective-permute-start(bf16[2,2304]{1,0:T(2,128)(2,1)S(1)} %shard_map.141), channel_id=1, source_target_pairs={{0,65},{1,64},{2,67},{3,66},{4,69},{5,68},{6,71},{7,70},{8,73},{9,... | collective-permute-start | bytes 27656 | tf_op jit(solution)/shard_map/ppermute | solution.py:247
  59.4 1.2 %collective-permute-start.14 = (bf16[2,2304]{1,0:T(2,128)(2,1)S(1)}, bf16[2,2304]{1,0:T(2,128)(2,1)S(1)}, u32[]{:S(2)}, u32[]{:S(2)}) collective-permute-start(bf16[2,2304]{1,0:T(2,128)(2,1)S(1)} %shard_map.141), channel_id=1, source_target_pairs={{0,97},{1,96},{2,99},{3,98},{4,101},{5,100},{6,103},{7,102},{8,105... | collective-permute-start | bytes 27656 | tf_op jit(solution)/shard_map/ppermute | solution.py:247
  60.6 0.7 %collective-permute-start.13 = (bf16[2,2304]{1,0:T(2,128)(2,1)S(1)}, bf16[2,2304]{1,0:T(2,128)(2,1)S(1)}, u32[]{:S(2)}, u32[]{:S(2)}) collective-permute-start(bf16[2,2304]{1,0:T(2,128)(2,1)S(1)} %shard_map.141), channel_id=1, source_target_pairs={{0,33},{1,32},{2,35},{3,34},{4,37},{5,36},{6,39},{7,38},{8,41},{9,... | collective-permute-start | bytes 27656 | tf_op jit(solution)/shard_map/ppermute | solution.py:247
  61.5 1.3 %collective-permute-done.15.refs_4_ = bf16[2,2304]{1,0:T(2,128)(2,1)S(1)} collective-permute-done((bf16[2,2304]{1,0:T(2,128)(2,1)S(1)}, bf16[2,2304]{1,0:T(2,128)(2,1)S(1)}, u32[]{:S(2)}, u32[]{:S(2)}) %collective-permute-start.15) | collective-permute-done | bytes 9248 | tf_op jit(solution)/shard_map/ppermute | solution.py:247
  62.8 0.9 %collective-permute-done.14.refs_3_ = bf16[2,2304]{1,0:T(2,128)(2,1)S(1)} collective-permute-done((bf16[2,2304]{1,0:T(2,128)(2,1)S(1)}, bf16[2,2304]{1,0:T(2,128)(2,1)S(1)}, u32[]{:S(2)}, u32[]{:S(2)}) %collective-permute-start.14) | collective-permute-done | bytes 9248 | tf_op jit(solution)/shard_map/ppermute | solution.py:247
  63.7 0.6 shard_map.142
  (55 shorter events, 1.9 us)
Async XLA Ops:
  0.0 5.7 %collective-permute-start.3 = (bf16[16,512]{1,0:T(8,128)(2,1)}, bf16[16,512]{1,0:T(8,128)(2,1)S(1)}, u32[]{:S(2)}, u32[]{:S(2)}) collective-permute-start(bf16[16,512]{1,0:T(8,128)(2,1)} %bitcast.23), channel_id=1, source_target_pairs={{0,64},{32,96},{64,0},{96,32},{1,65},{33,97},{65,1},{97,33},{2,66}... | collective-permute-start | bytes 49160 | tf_op jit(solution)/shard_map/ppermute | solution.py:238
  3.6 4.0 %collective-permute-start.2 = (bf16[16,512]{1,0:T(8,128)(2,1)}, bf16[16,512]{1,0:T(8,128)(2,1)S(1)}, u32[]{:S(2)}, u32[]{:S(2)}) collective-permute-start(bf16[16,512]{1,0:T(8,128)(2,1)} %bitcast.24), channel_id=1, source_target_pairs={{0,96},{32,64},{64,32},{96,0},{1,97},{33,65},{65,33},{97,1},{2,98}... | collective-permute-start | bytes 49160 | tf_op jit(solution)/shard_map/ppermute | solution.py:238
  4.4 3.2 %collective-permute-start.1 = (bf16[16,512]{1,0:T(8,128)(2,1)}, bf16[16,512]{1,0:T(8,128)(2,1)S(1)}, u32[]{:S(2)}, u32[]{:S(2)}) collective-permute-start(bf16[16,512]{1,0:T(8,128)(2,1)} %bitcast.25), channel_id=1, source_target_pairs={{0,32},{32,0},{64,96},{96,64},{1,33},{33,1},{65,97},{97,65},{2,34}... | collective-permute-start | bytes 49160 | tf_op jit(solution)/shard_map/ppermute | solution.py:238
  8.8 6.3 %collective-permute-start.4 = (bf16[16,640]{1,0:T(8,128)(2,1)S(1)}, bf16[16,640]{1,0:T(8,128)(2,1)S(1)}, u32[]{:S(2)}, u32[]{:S(2)}) collective-permute-start(bf16[16,640]{1,0:T(8,128)(2,1)S(1)} %get-tuple-element.18), channel_id=1, source_target_pairs={{0,65},{1,64},{2,67},{3,66},{4,69},{5,68},{6,71},{7,70},{8,73},{9,... | collective-permute-start | bytes 61448 | tf_op jit(solution)/shard_map/ppermute | solution.py:247
  12.1 4.4 %collective-permute-start.5 = (bf16[16,640]{1,0:T(8,128)(2,1)S(1)}, bf16[16,640]{1,0:T(8,128)(2,1)S(1)}, u32[]{:S(2)}, u32[]{:S(2)}) collective-permute-start(bf16[16,640]{1,0:T(8,128)(2,1)S(1)} %get-tuple-element.19), channel_id=1, source_target_pairs={{0,97},{1,96},{2,99},{3,98},{4,101},{5,100},{6,103},{7,102},{8,105... | collective-permute-start | bytes 61448 | tf_op jit(solution)/shard_map/ppermute | solution.py:247
  12.7 3.8 %collective-permute-start.6 = (bf16[16,640]{1,0:T(8,128)(2,1)S(1)}, bf16[16,640]{1,0:T(8,128)(2,1)S(1)}, u32[]{:S(2)}, u32[]{:S(2)}) collective-permute-start(bf16[16,640]{1,0:T(8,128)(2,1)S(1)} %get-tuple-element.20), channel_id=1, source_target_pairs={{0,33},{1,32},{2,35},{3,34},{4,37},{5,36},{6,39},{7,38},{8,41},{9,... | collective-permute-start | bytes 61448 | tf_op jit(solution)/shard_map/ppermute | solution.py:247
  13.8 2.7 %collective-permute-start.7 = (bf16[16,640]{1,0:T(8,128)(2,1)S(1)}, bf16[16,640]{1,0:T(8,128)(2,1)S(1)}, u32[]{:S(2)}, u32[]{:S(2)}) collective-permute-start(bf16[16,640]{1,0:T(8,128)(2,1)S(1)} %get-tuple-element.21), channel_id=1, source_target_pairs={{0,1},{1,0},{2,3},{3,2},{4,5},{5,4},{6,7},{7,6},{8,9},{9,8},{10,11... | collective-permute-start | bytes 61448 | tf_op jit(solution)/shard_map/ppermute | solution.py:247
  13.8 1.3 %collective-permute-start = (bf16[2,512]{1,0:T(2,128)(2,1)S(1)}, bf16[2,512]{1,0:T(2,128)(2,1)S(1)}, u32[]{:S(2)}, u32[]{:S(2)}) collective-permute-start(bf16[2,512]{1,0:T(2,128)(2,1)S(1)} %bitcast.29), channel_id=1, source_target_pairs={{0,1},{1,0},{2,3},{3,2},{4,5},{5,4},{6,7},{7,6},{8,9},{9,8},{10,11... | collective-permute-start | bytes 6152 | tf_op jit(solution)/shard_map/ppermute | solution.py:247
  16.5 25.7 %slice-start.5 = ((s8[4718592]{0:T(1024)(128)(4,1)}), s8[524288]{0:T(1024)(128)(4,1)S(1)}, s32[]{:S(2)}) async-start(s8[4718592]{0:T(1024)(128)(4,1)} %bitcast.18), calls=%async_computation.7 | async-start | bytes 1048576
  18.0 4.7 %collective-permute-start.11 = (bf16[2,2304]{1,0:T(2,128)(2,1)S(1)}, bf16[2,2304]{1,0:T(2,128)(2,1)S(1)}, u32[]{:S(2)}, u32[]{:S(2)}) collective-permute-start(bf16[2,2304]{1,0:T(2,128)(2,1)S(1)} %shard_map.138), channel_id=1, source_target_pairs={{0,65},{1,64},{2,67},{3,66},{4,69},{5,68},{6,71},{7,70},{8,73},{9,... | collective-permute-start | bytes 27656 | tf_op jit(solution)/shard_map/ppermute | solution.py:247
  20.0 4.3 %collective-permute-start.10 = (bf16[2,2304]{1,0:T(2,128)(2,1)S(1)}, bf16[2,2304]{1,0:T(2,128)(2,1)S(1)}, u32[]{:S(2)}, u32[]{:S(2)}) collective-permute-start(bf16[2,2304]{1,0:T(2,128)(2,1)S(1)} %shard_map.138), channel_id=1, source_target_pairs={{0,97},{1,96},{2,99},{3,98},{4,101},{5,100},{6,103},{7,102},{8,105... | collective-permute-start | bytes 27656 | tf_op jit(solution)/shard_map/ppermute | solution.py:247
  21.1 3.2 %collective-permute-start.9 = (bf16[2,2304]{1,0:T(2,128)(2,1)S(1)}, bf16[2,2304]{1,0:T(2,128)(2,1)S(1)}, u32[]{:S(2)}, u32[]{:S(2)}) collective-permute-start(bf16[2,2304]{1,0:T(2,128)(2,1)S(1)} %shard_map.138), channel_id=1, source_target_pairs={{0,33},{1,32},{2,35},{3,34},{4,37},{5,36},{6,39},{7,38},{8,41},{9,... | collective-permute-start | bytes 27656 | tf_op jit(solution)/shard_map/ppermute | solution.py:247
  21.1 3.2 %collective-permute-start.8 = (bf16[2,2304]{1,0:T(2,128)(2,1)S(1)}, bf16[2,2304]{1,0:T(2,128)(2,1)S(1)}, u32[]{:S(2)}, u32[]{:S(2)}) collective-permute-start(bf16[2,2304]{1,0:T(2,128)(2,1)S(1)} %shard_map.138), channel_id=1, source_target_pairs={{0,1},{1,0},{2,3},{3,2},{4,5},{5,4},{6,7},{7,6},{8,9},{9,8},{10,11... | collective-permute-start | bytes 27656 | tf_op jit(solution)/shard_map/ppermute | solution.py:247
  24.3 17.9 %slice-start = ((s8[9437184]{0:T(1024)(128)(4,1)}), s8[4194304]{0:T(1024)(128)(4,1)S(1)}, s32[]{:S(2)}) async-start(s8[9437184]{0:T(1024)(128)(4,1)} %bitcast.13), calls=%async_computation.2 | async-start | bytes 8388608
  24.3 17.9 %slice-start.1 = ((s8[9437184]{0:T(1024)(128)(4,1)}), s8[4194304]{0:T(1024)(128)(4,1)S(1)}, s32[]{:S(2)}) async-start(s8[9437184]{0:T(1024)(128)(4,1)} %bitcast.13), calls=%async_computation.3 | async-start | bytes 8388608
  24.3 17.9 %slice-start.2 = ((s8[9437184]{0:T(1024)(128)(4,1)}), s8[1048576]{0:T(1024)(128)(4,1)S(1)}, s32[]{:S(2)}) async-start(s8[9437184]{0:T(1024)(128)(4,1)} %bitcast.13), calls=%async_computation.4 | async-start | bytes 2097152
  24.4 17.9 %slice-start.6 = ((s8[4718592]{0:T(1024)(128)(4,1)}), s8[4194304]{0:T(1024)(128)(4,1)S(1)}, s32[]{:S(2)}) async-start(s8[4718592]{0:T(1024)(128)(4,1)} %bitcast.18), calls=%async_computation.8 | async-start | bytes 8388608
  24.4 17.9 %copy-start = (bf16[2,2304,256]{2,1,0:T(8,128)(2,1)S(1)}, bf16[2,2304,256]{2,1,0:T(8,128)(2,1)}, u32[]{:S(2)}) copy-start(bf16[2,2304,256]{2,1,0:T(8,128)(2,1)} %refs_6_.3) | copy-start | bytes 7077892
  24.4 17.9 %copy-start.2 = (bf16[256,2304]{1,0:T(8,128)(2,1)S(1)}, bf16[256,2304]{1,0:T(8,128)(2,1)}, u32[]{:S(2)}) copy-start(bf16[256,2304]{1,0:T(8,128)(2,1)} %refs_7_.3) | copy-start | bytes 3538948
  24.4 17.9 %copy-start.4 = (bf16[2304,128]{1,0:T(8,128)(2,1)S(1)}, bf16[2304,128]{1,0:T(8,128)(2,1)}, u32[]{:S(2)}) copy-start(bf16[2304,128]{1,0:T(8,128)(2,1)} %refs_3_.1) | copy-start | bytes 1769476
  58.1 4.7 %collective-permute-start.15 = (bf16[2,2304]{1,0:T(2,128)(2,1)S(1)}, bf16[2,2304]{1,0:T(2,128)(2,1)S(1)}, u32[]{:S(2)}, u32[]{:S(2)}) collective-permute-start(bf16[2,2304]{1,0:T(2,128)(2,1)S(1)} %shard_map.141), channel_id=1, source_target_pairs={{0,65},{1,64},{2,67},{3,66},{4,69},{5,68},{6,71},{7,70},{8,73},{9,... | collective-permute-start | bytes 27656 | tf_op jit(solution)/shard_map/ppermute | solution.py:247
  59.4 4.3 %collective-permute-start.14 = (bf16[2,2304]{1,0:T(2,128)(2,1)S(1)}, bf16[2,2304]{1,0:T(2,128)(2,1)S(1)}, u32[]{:S(2)}, u32[]{:S(2)}) collective-permute-start(bf16[2,2304]{1,0:T(2,128)(2,1)S(1)} %shard_map.141), channel_id=1, source_target_pairs={{0,97},{1,96},{2,99},{3,98},{4,101},{5,100},{6,103},{7,102},{8,105... | collective-permute-start | bytes 27656 | tf_op jit(solution)/shard_map/ppermute | solution.py:247
  60.6 3.1 %collective-permute-start.13 = (bf16[2,2304]{1,0:T(2,128)(2,1)S(1)}, bf16[2,2304]{1,0:T(2,128)(2,1)S(1)}, u32[]{:S(2)}, u32[]{:S(2)}) collective-permute-start(bf16[2,2304]{1,0:T(2,128)(2,1)S(1)} %shard_map.141), channel_id=1, source_target_pairs={{0,33},{1,32},{2,35},{3,34},{4,37},{5,36},{6,39},{7,38},{8,41},{9,... | collective-permute-start | bytes 27656 | tf_op jit(solution)/shard_map/ppermute | solution.py:247
  61.3 2.4 %collective-permute-start.12 = (bf16[2,2304]{1,0:T(2,128)(2,1)S(1)}, bf16[2,2304]{1,0:T(2,128)(2,1)S(1)}, u32[]{:S(2)}, u32[]{:S(2)}) collective-permute-start(bf16[2,2304]{1,0:T(2,128)(2,1)S(1)} %shard_map.141), channel_id=1, source_target_pairs={{0,1},{1,0},{2,3},{3,2},{4,5},{5,4},{6,7},{7,6},{8,9},{9,8},{10,11... | collective-permute-start | bytes 27656 | tf_op jit(solution)/shard_map/ppermute | solution.py:247
  (8 other events, 70.1 us)

commit v8 on v7

--- a/solution.py
+++ b/solution.py
@@ -74,7 +74,8 @@
         named = jnp.zeros((experts, count), F32)
         for k in range(choices):
             named = jnp.where(ids_ref[r, k : k + 1, :] == expert, 1.0, named)
-        place = jnp.where(row == batch * group + r, 1.0, 0.0).astype(BF16)
+        place = (batch & 1) * (total // 2) + (batch >> 1) * group + r
+        place = jnp.where(row == place, 1.0, 0.0).astype(BF16)
         picked = picked + lax.dot_general(
             place, named.astype(BF16), (((1,), (1,)), ((), ())), preferred_element_type=F32
         )
@@ -175,7 +176,8 @@
 
 def expert_kernel(
     marks_ref,
-    rows_ref,
+    own_rows_ref,
+    other_rows_ref,
     picked_ref,
     router_ref,
     gate_up_ref,
@@ -187,11 +189,21 @@
     act,
 ):
     count = act.shape[0]
-    rows = rows_ref[...].astype(F32).reshape(count, rows_ref.shape[2]).astype(BF16)
-    pairs, cores, group, _ = out_ref.shape
+    pairs, _, group, _ = out_ref.shape
+    half = count // 2
+    rows = jnp.concatenate(
+        [
+            rows_ref[...].astype(F32).reshape(half, rows_ref.shape[2])
+            for rows_ref in (own_rows_ref, other_rows_ref)
+        ]
+    )
+    rows = rows.astype(BF16)
+    first = marks_ref[:, group + 1 : group + 2] == 0
+    picked = picked_ref[...]
+    picked = jnp.where(first, picked, jnp.concatenate([picked[half:], picked[:half]]))
     width, model = down_ref.shape
     logits = jnp.dot(rows, router_ref[...], preferred_element_type=F32)
-    score = jnp.where(picked_ref[...] > 0, jax.nn.sigmoid(logits), 0.0)
+    score = jnp.where(picked > 0, jax.nn.sigmoid(logits), 0.0)
     expert = lax.broadcasted_iota(jnp.int32, score.shape, 1)
     own = jnp.where(expert == marks_ref[:, group : group + 1], score, 0.0)
     own = jnp.sum(own, axis=-1, keepdims=True)
@@ -204,12 +216,14 @@
     for n in range(0, model, step):
         answer = jnp.dot(act[...], down_ref[:, n : n + step], preferred_element_type=F32)
         answer = weight * answer.astype(BF16).astype(F32)
-        answer = answer.reshape(pairs, cores, group, step).astype(BF16)
-        for core in range(cores):
-            out_ref[:, core, :, n : n + step] = answer[:, cores - 1 - core]
+        mine, other = answer[:half], answer[half:]
+        for core, part in enumerate(
+            (jnp.where(first, other, mine), jnp.where(first, mine, other))
+        ):
+            out_ref[:, core, :, n : n + step] = part.reshape(pairs, group, step).astype(BF16)
     row = lax.broadcasted_iota(jnp.int32, (8, count), 0)
     column = lax.broadcasted_iota(jnp.int32, (8, count), 1)
-    first_row = marks_ref[:, group + 1 : group + 2]
+    first_row = half + marks_ref[:, group + 2 : group + 3]
     chosen = jnp.where((row < group) & (column == first_row + row), 1.0, 0.0).astype(BF16)
     chosen = jnp.dot(chosen, rows, preferred_element_type=F32).astype(BF16)
     gate = jnp.dot(chosen, shared_gate_up_ref[0], preferred_element_type=F32)
@@ -295,7 +309,8 @@
         beside=[expert_gate_up],
     )
     valid = own_lengths - (ctx_index * latent_cache.shape[2]).astype(jnp.int32)
-    places = jnp.stack([ctx_index * batch_count + batch_index, (batch_index ^ 1) * rows])
+    places = [ctx_index * batch_count + batch_index, batch_index & 1, (batch_index >> 1) * rows]
+    places = jnp.stack(places)
     marks = jnp.concatenate([valid, places.astype(jnp.int32)[None]], axis=1)
     *parts, picked = call(
         attend_kernel,
@@ -315,13 +330,19 @@
         norm_kernel,
         (
             shape((rows, model), F32),
-            shape((batch_count, rows, model), BF16),
+            shape((batch_count // 2, rows, model), BF16),
         ),
         [residual[0], norm_gain, *terms],
         beside=[expert_gate_up] * 4,
     )
 
-    every_rows = lax.all_to_all(copies, "batch", 0, 0)
+    groups = [
+        [c * batch_count + b for b in range(core, batch_count, 2)]
+        for c in range(ctx_count)
+        for core in range(2)
+    ]
+    own_rows = lax.all_to_all(copies, ("ctx", "batch"), 0, 0, axis_index_groups=groups)
+    other_rows = crossings([own_rows])[0]
     weighted, shared_part = call(
         expert_kernel,
         (
@@ -330,7 +351,8 @@
         ),
         [
             marks,
-            every_rows,
+            own_rows,
+            other_rows,
             picked,
             router,
             expert_gate_up[0],

time: 64.4 us -> 64.2 us (level)
  blocking collectives: 30.4 us -> 27.5 us
  starting transfers between devices: 16.9 us -> 18.6 us
  waiting for transfers between devices: 9.06 us -> 10.1 us
    all_to_all x1, blocking collectives: 17.7 us -> 14.8 us  [local(): lax.all_to_all(copies, ('ctx', 'batch'), 0, 0, axis_index_groups=groups)]
    ppermute x13 -> x14, starting transfers between devices: 12.5 us -> 14.2 us  [crossings(): lax.ppermute(array, ('ctx', 'batch'), [(c * count + b, (c ^ m) * count +...]
    ppermute x13 -> x14, waiting for transfers between devices: 7.16 us -> 8.17 us  [crossings(): lax.ppermute(array, ('ctx', 'batch'), [(c * count + b, (c ^ m) * count +...]
  transfers between devices with their start and end apart: 16 -> 17, of which waited for: 7 -> 8; matrix products, arithmetic and copies ran while one was open for 0% -> 0% of each run, Pallas kernels for 2% -> 2%
where the time goes in v8:
time: 64.2 us; the launch traced here: 64.1 us
  blocking collectives  27.5 us (43%)
  starting transfers between devices  18.6 us (29%)
  waiting for transfers between devices  10.1 us (16%)
  Pallas kernels  7.43 us (12%)
    all_to_all x1, blocking collectives, local(): lax.all_to_all(copies, ('ctx', 'batch'), 0, 0, axis_index_groups=groups)  14.8 us
    ppermute x14, starting transfers between devices, crossings(): lax.ppermute(array, ('ctx', 'batch'), [(c * count + b, (c ^ m) * count +...  14.2 us
    all_to_all x1, blocking collectives, local(): weighted = lax.all_to_all(weighted, 'batch', 0, 0)  12.7 us
    ppermute x14, waiting for transfers between devices, crossings(): lax.ppermute(array, ('ctx', 'batch'), [(c * count + b, (c ^ m) * count +...  8.17 us
    pallas_call x7, Pallas kernels, call(): pl.pallas_call(body, out_shape=out_shape, in_specs=(specs or [VMEM] * cou...  7.43 us
    ppermute x3, starting transfers between devices, swaps(): lax.ppermute(array, 'ctx', [(place, place ^ m) for place in range(size)])  4.44 us
    ppermute x3, waiting for transfers between devices, swaps(): lax.ppermute(array, 'ctx', [(place, place ^ m) for place in range(size)])  1.88 us
  transfers between devices with their start and end apart: 17, of which 8 were waited for; matrix products, arithmetic and copies ran while one was open for 0% of the time, Pallas kernels for 2%

profile of v8, /device:TPU:1, one launch (start us, length us, event | category | flops | bytes accessed | tf_op | source)
XLA Modules:
  0.0 64.1 jit_solution(16869100667021529563)
XLA Ops:
  0.0 3.6 %collective-permute-start.3 = (bf16[16,512]{1,0:T(8,128)(2,1)}, bf16[16,512]{1,0:T(8,128)(2,1)S(1)}, u32[]{:S(2)}, u32[]{:S(2)}) collective-permute-start(bf16[16,512]{1,0:T(8,128)(2,1)} %bitcast.24), channel_id=1, source_target_pairs={{0,64},{32,96},{64,0},{96,32},{1,65},{33,97},{65,1},{97,33},{2,66}... | collective-permute-start | bytes 49160 | tf_op jit(solution)/shard_map/ppermute | solution.py:252
  3.6 0.9 %collective-permute-start.2 = (bf16[16,512]{1,0:T(8,128)(2,1)}, bf16[16,512]{1,0:T(8,128)(2,1)S(1)}, u32[]{:S(2)}, u32[]{:S(2)}) collective-permute-start(bf16[16,512]{1,0:T(8,128)(2,1)} %bitcast.25), channel_id=1, source_target_pairs={{0,96},{32,64},{64,32},{96,0},{1,97},{33,65},{65,33},{97,1},{2,98}... | collective-permute-start | bytes 49160 | tf_op jit(solution)/shard_map/ppermute | solution.py:252
  4.5 1.1 %shard_map.136 = (f32[64,128]{1,0:T(8,128)S(1)}, s32[1,2]{1,0:T(1,128)S(1)}) custom-call(s32[2,8,32]{2,1,0:T(8,128)} %bitcast.31, s32[1,2]{1,0:T(1,128)} %refs_1_.3, bf16[1,2304,2048]{2,1,0:T(8,128)(2,1)} %refs_9_.3), custom_call_target="tpu_custom_call" | custom-call | tf_op jit(solution)/shard_map/pallas_call | solution.py:28
  5.7 1.9 %collective-permute-done.2.refs_3_ = bf16[16,512]{1,0:T(8,128)(2,1)S(1)} collective-permute-done((bf16[16,512]{1,0:T(8,128)(2,1)}, bf16[16,512]{1,0:T(8,128)(2,1)S(1)}, u32[]{:S(2)}, u32[]{:S(2)}) %collective-permute-start.2) | collective-permute-done | bytes 16416 | tf_op jit(solution)/shard_map/ppermute | solution.py:252
  7.6 1.1 %shard_map.137 = (bf16[16,640]{1,0:T(8,128)(2,1)S(1)}, bf16[16,640]{1,0:T(8,128)(2,1)S(1)}, bf16[16,640]{1,0:T(8,128)(2,1)S(1)}, bf16[16,640]{1,0:T(8,128)(2,1)S(1)}, f32[64,128]{1,0:T(8,128)S(1)}) custom-call(s32[1,5]{1,0:T(1,128)S(1)} %pad_add_fusion.refs_0_, bf16[16,512]{1,0:T(8,128)(2,1)S(1)} %bitcast.27, ...), custom_call_target="tpu_custom_call" | custom-call | tf_op jit(solution)/shard_map/pallas_call | solution.py:28
  8.8 3.3 %collective-permute-start.4 = (bf16[16,640]{1,0:T(8,128)(2,1)S(1)}, bf16[16,640]{1,0:T(8,128)(2,1)S(1)}, u32[]{:S(2)}, u32[]{:S(2)}) collective-permute-start(bf16[16,640]{1,0:T(8,128)(2,1)S(1)} %get-tuple-element.18), channel_id=1, source_target_pairs={{0,65},{1,64},{2,67},{3,66},{4,69},{5,68},{6,71},{7,70},{8,73},{9,... | collective-permute-start | bytes 61448 | tf_op jit(solution)/shard_map/ppermute | solution.py:261
  12.7 1.1 %collective-permute-start.6 = (bf16[16,640]{1,0:T(8,128)(2,1)S(1)}, bf16[16,640]{1,0:T(8,128)(2,1)S(1)}, u32[]{:S(2)}, u32[]{:S(2)}) collective-permute-start(bf16[16,640]{1,0:T(8,128)(2,1)S(1)} %get-tuple-element.20), channel_id=1, source_target_pairs={{0,33},{1,32},{2,35},{3,34},{4,37},{5,36},{6,39},{7,38},{8,41},{9,... | collective-permute-start | bytes 61448 | tf_op jit(solution)/shard_map/ppermute | solution.py:261
  14.3 0.8 %collective-permute-done.refs_2_ = bf16[2,512]{1,0:T(2,128)(2,1)S(1)} collective-permute-done((bf16[2,512]{1,0:T(2,128)(2,1)S(1)}, bf16[2,512]{1,0:T(2,128)(2,1)S(1)}, u32[]{:S(2)}, u32[]{:S(2)}) %collective-permute-start) | collective-permute-done | bytes 2080 | tf_op jit(solution)/shard_map/ppermute | solution.py:261
  15.1 1.4 %collective-permute-done.5.refs_4_ = bf16[16,640]{1,0:T(8,128)(2,1)S(1)} collective-permute-done((bf16[16,640]{1,0:T(8,128)(2,1)S(1)}, bf16[16,640]{1,0:T(8,128)(2,1)S(1)}, u32[]{:S(2)}, u32[]{:S(2)}) %collective-permute-start.5) | collective-permute-done | bytes 20512 | tf_op jit(solution)/shard_map/ppermute | solution.py:261
  16.5 1.4 %shard_map.138 = bf16[2,2304]{1,0:T(2,128)(2,1)S(1)} custom-call(bf16[8,512,128]{2,1,0:T(8,128)(2,1)S(1)} %copy-done.3, bf16[1024,2304]{1,0:T(8,128)(2,1)S(1)} %bitcast.18, bf16[2,512]{1,0:T(2,128)(2,1)S(1)} %collective-permute-done.refs_2_, bf16[16,640]{1,0:T(8,128)(2,1)S(1)} %collective-permute-done.4.refs_3_, ...), custom_call_target="tpu_custom_call" | custom-call | tf_op jit(solution)/shard_map/pallas_call | solution.py:28
  18.0 2.0 %collective-permute-start.11 = (bf16[2,2304]{1,0:T(2,128)(2,1)S(1)}, bf16[2,2304]{1,0:T(2,128)(2,1)S(1)}, u32[]{:S(2)}, u32[]{:S(2)}) collective-permute-start(bf16[2,2304]{1,0:T(2,128)(2,1)S(1)} %shard_map.138), channel_id=1, source_target_pairs={{0,65},{1,64},{2,67},{3,66},{4,69},{5,68},{6,71},{7,70},{8,73},{9,... | collective-permute-start | bytes 27656 | tf_op jit(solution)/shard_map/ppermute | solution.py:261
  20.0 1.1 %collective-permute-start.10 = (bf16[2,2304]{1,0:T(2,128)(2,1)S(1)}, bf16[2,2304]{1,0:T(2,128)(2,1)S(1)}, u32[]{:S(2)}, u32[]{:S(2)}) collective-permute-start(bf16[2,2304]{1,0:T(2,128)(2,1)S(1)} %shard_map.138), channel_id=1, source_target_pairs={{0,97},{1,96},{2,99},{3,98},{4,101},{5,100},{6,103},{7,102},{8,105... | collective-permute-start | bytes 27656 | tf_op jit(solution)/shard_map/ppermute | solution.py:261
  21.5 1.1 %collective-permute-done.11.refs_5_ = bf16[2,2304]{1,0:T(2,128)(2,1)S(1)} collective-permute-done((bf16[2,2304]{1,0:T(2,128)(2,1)S(1)}, bf16[2,2304]{1,0:T(2,128)(2,1)S(1)}, u32[]{:S(2)}, u32[]{:S(2)}) %collective-permute-start.11) | collective-permute-done | bytes 9248 | tf_op jit(solution)/shard_map/ppermute | solution.py:261
  22.6 1.7 %collective-permute-done.10.refs_4_ = bf16[2,2304]{1,0:T(2,128)(2,1)S(1)} collective-permute-done((bf16[2,2304]{1,0:T(2,128)(2,1)S(1)}, bf16[2,2304]{1,0:T(2,128)(2,1)S(1)}, u32[]{:S(2)}, u32[]{:S(2)}) %collective-permute-start.10) | collective-permute-done | bytes 9248 | tf_op jit(solution)/shard_map/ppermute | solution.py:261
  24.5 14.8 %all_to_all.10.refs_1_ = bf16[16,2,2304]{2,1,0:T(2,128)(2,1)S(1)} all-to-all(bf16[16,2,2304]{2,1,0:T(2,128)(2,1)S(1)} %get-tuple-element.23), channel_id=1, replica_groups={{0,2,4,6,8,10,12,14,16,18,20,22,24,26,28,30},{1,3,5,7,9,11,13,15,17,19,..., dimensions={0} | all-to-all | bytes 294912 | tf_op jit(solution)/shard_map/all_to_all | solution.py:344
  39.3 1.7 %collective-permute-start.12 = (bf16[16,2,2304]{2,1,0:T(2,128)(2,1)S(1)}, bf16[16,2,2304]{2,1,0:T(2,128)(2,1)S(1)}, u32[]{:S(2)}, u32[]{:S(2)}) collective-permute-start(bf16[16,2,2304]{2,1,0:T(2,128)(2,1)S(1)} %all_to_all.10.refs_1_), channel_id=1, source_target_pairs={{0,1},{1,0},{2,3},{3,2},{4,5},{5,4},{6,7},{7,6},{8,9},{9,8},{10,11... | collective-permute-start | bytes 442376 | tf_op jit(solution)/shard_map/ppermute | solution.py:261
  41.0 1.0 %collective-permute-done.12.refs_2_ = bf16[16,2,2304]{2,1,0:T(2,128)(2,1)S(1)} collective-permute-done((bf16[16,2,2304]{2,1,0:T(2,128)(2,1)S(1)}, bf16[16,2,2304]{2,1,0:T(2,128)(2,1)S(1)}, u32[]{:S(2)}, u32[]{:S(2)}) %collective-permute-start.12) | collective-permute-done | bytes 147488 | tf_op jit(solution)/shard_map/ppermute | solution.py:261
  42.1 2.8 %shard_map.140 = (bf16[16,2,2,2304]{3,2,1,0:T(2,128)(2,1)S(1)}, f32[2,2304]{1,0:T(2,128)S(1)}) custom-call(s32[1,5]{1,0:T(1,128)S(1)} %pad_add_fusion.refs_0_, bf16[16,2,2304]{2,1,0:T(2,128)(2,1)S(1)} %all_to_all.10.refs_1_, bf16[16,2,2304]{2,1,0:T(2,128)(2,1)S(1)} %collective-permute-done.12.refs_2_, f32[64,128]{1,0:T(8,128)S(1)} %get-tuple-element.24.refs_3_, ...), custom_call_target="tpu_custom_call" | custom-call | tf_op jit(solution)/shard_map/pallas_call | solution.py:28
  44.9 12.7 %all_to_all.11.refs_0_ = bf16[32,2,2304]{2,1,0:T(2,128)(2,1)S(1)} all-to-all(bf16[32,2,2304]{2,1,0:T(2,128)(2,1)S(1)} %bitcast.23), channel_id=1, replica_groups=mesh['ctx'=4,'batch'=32] {'batch'}, dimensions={0} | all-to-all | bytes 589824 | tf_op jit(solution)/shard_map/all_to_all | solution.py:366
  57.9 1.3 %collective-permute-start.16 = (bf16[2,2304]{1,0:T(2,128)(2,1)S(1)}, bf16[2,2304]{1,0:T(2,128)(2,1)S(1)}, u32[]{:S(2)}, u32[]{:S(2)}) collective-permute-start(bf16[2,2304]{1,0:T(2,128)(2,1)S(1)} %shard_map.141), channel_id=1, source_target_pairs={{0,65},{1,64},{2,67},{3,66},{4,69},{5,68},{6,71},{7,70},{8,73},{9,... | collective-permute-start | bytes 27656 | tf_op jit(solution)/shard_map/ppermute | solution.py:261
  59.1 1.2 %collective-permute-start.15 = (bf16[2,2304]{1,0:T(2,128)(2,1)S(1)}, bf16[2,2304]{1,0:T(2,128)(2,1)S(1)}, u32[]{:S(2)}, u32[]{:S(2)}) collective-permute-start(bf16[2,2304]{1,0:T(2,128)(2,1)S(1)} %shard_map.141), channel_id=1, source_target_pairs={{0,97},{1,96},{2,99},{3,98},{4,101},{5,100},{6,103},{7,102},{8,105... | collective-permute-start | bytes 27656 | tf_op jit(solution)/shard_map/ppermute | solution.py:261
  60.3 0.7 %collective-permute-start.14 = (bf16[2,2304]{1,0:T(2,128)(2,1)S(1)}, bf16[2,2304]{1,0:T(2,128)(2,1)S(1)}, u32[]{:S(2)}, u32[]{:S(2)}) collective-permute-start(bf16[2,2304]{1,0:T(2,128)(2,1)S(1)} %shard_map.141), channel_id=1, source_target_pairs={{0,33},{1,32},{2,35},{3,34},{4,37},{5,36},{6,39},{7,38},{8,41},{9,... | collective-permute-start | bytes 27656 | tf_op jit(solution)/shard_map/ppermute | solution.py:261
  61.3 1.3 %collective-permute-done.16.refs_4_ = bf16[2,2304]{1,0:T(2,128)(2,1)S(1)} collective-permute-done((bf16[2,2304]{1,0:T(2,128)(2,1)S(1)}, bf16[2,2304]{1,0:T(2,128)(2,1)S(1)}, u32[]{:S(2)}, u32[]{:S(2)}) %collective-permute-start.16) | collective-permute-done | bytes 9248 | tf_op jit(solution)/shard_map/ppermute | solution.py:261
  62.5 0.9 %collective-permute-done.15.refs_3_ = bf16[2,2304]{1,0:T(2,128)(2,1)S(1)} collective-permute-done((bf16[2,2304]{1,0:T(2,128)(2,1)S(1)}, bf16[2,2304]{1,0:T(2,128)(2,1)S(1)}, u32[]{:S(2)}, u32[]{:S(2)}) %collective-permute-start.15) | collective-permute-done | bytes 9248 | tf_op jit(solution)/shard_map/ppermute | solution.py:261
  (57 shorter events, 3.1 us)
Async XLA Ops:
  0.0 5.7 %collective-permute-start.3 = (bf16[16,512]{1,0:T(8,128)(2,1)}, bf16[16,512]{1,0:T(8,128)(2,1)S(1)}, u32[]{:S(2)}, u32[]{:S(2)}) collective-permute-start(bf16[16,512]{1,0:T(8,128)(2,1)} %bitcast.24), channel_id=1, source_target_pairs={{0,64},{32,96},{64,0},{96,32},{1,65},{33,97},{65,1},{97,33},{2,66}... | collective-permute-start | bytes 49160 | tf_op jit(solution)/shard_map/ppermute | solution.py:252
  3.6 4.0 %collective-permute-start.2 = (bf16[16,512]{1,0:T(8,128)(2,1)}, bf16[16,512]{1,0:T(8,128)(2,1)S(1)}, u32[]{:S(2)}, u32[]{:S(2)}) collective-permute-start(bf16[16,512]{1,0:T(8,128)(2,1)} %bitcast.25), channel_id=1, source_target_pairs={{0,96},{32,64},{64,32},{96,0},{1,97},{33,65},{65,33},{97,1},{2,98}... | collective-permute-start | bytes 49160 | tf_op jit(solution)/shard_map/ppermute | solution.py:252
  4.4 3.2 %collective-permute-start.1 = (bf16[16,512]{1,0:T(8,128)(2,1)}, bf16[16,512]{1,0:T(8,128)(2,1)S(1)}, u32[]{:S(2)}, u32[]{:S(2)}) collective-permute-start(bf16[16,512]{1,0:T(8,128)(2,1)} %bitcast.26), channel_id=1, source_target_pairs={{0,32},{32,0},{64,96},{96,64},{1,33},{33,1},{65,97},{97,65},{2,34}... | collective-permute-start | bytes 49160 | tf_op jit(solution)/shard_map/ppermute | solution.py:252
  8.8 6.3 %collective-permute-start.4 = (bf16[16,640]{1,0:T(8,128)(2,1)S(1)}, bf16[16,640]{1,0:T(8,128)(2,1)S(1)}, u32[]{:S(2)}, u32[]{:S(2)}) collective-permute-start(bf16[16,640]{1,0:T(8,128)(2,1)S(1)} %get-tuple-element.18), channel_id=1, source_target_pairs={{0,65},{1,64},{2,67},{3,66},{4,69},{5,68},{6,71},{7,70},{8,73},{9,... | collective-permute-start | bytes 61448 | tf_op jit(solution)/shard_map/ppermute | solution.py:261
  12.1 4.4 %collective-permute-start.5 = (bf16[16,640]{1,0:T(8,128)(2,1)S(1)}, bf16[16,640]{1,0:T(8,128)(2,1)S(1)}, u32[]{:S(2)}, u32[]{:S(2)}) collective-permute-start(bf16[16,640]{1,0:T(8,128)(2,1)S(1)} %get-tuple-element.19), channel_id=1, source_target_pairs={{0,97},{1,96},{2,99},{3,98},{4,101},{5,100},{6,103},{7,102},{8,105... | collective-permute-start | bytes 61448 | tf_op jit(solution)/shard_map/ppermute | solution.py:261
  12.7 3.8 %collective-permute-start.6 = (bf16[16,640]{1,0:T(8,128)(2,1)S(1)}, bf16[16,640]{1,0:T(8,128)(2,1)S(1)}, u32[]{:S(2)}, u32[]{:S(2)}) collective-permute-start(bf16[16,640]{1,0:T(8,128)(2,1)S(1)} %get-tuple-element.20), channel_id=1, source_target_pairs={{0,33},{1,32},{2,35},{3,34},{4,37},{5,36},{6,39},{7,38},{8,41},{9,... | collective-permute-start | bytes 61448 | tf_op jit(solution)/shard_map/ppermute | solution.py:261
  13.8 2.7 %collective-permute-start.7 = (bf16[16,640]{1,0:T(8,128)(2,1)S(1)}, bf16[16,640]{1,0:T(8,128)(2,1)S(1)}, u32[]{:S(2)}, u32[]{:S(2)}) collective-permute-start(bf16[16,640]{1,0:T(8,128)(2,1)S(1)} %get-tuple-element.21), channel_id=1, source_target_pairs={{0,1},{1,0},{2,3},{3,2},{4,5},{5,4},{6,7},{7,6},{8,9},{9,8},{10,11... | collective-permute-start | bytes 61448 | tf_op jit(solution)/shard_map/ppermute | solution.py:261
  13.8 1.3 %collective-permute-start = (bf16[2,512]{1,0:T(2,128)(2,1)S(1)}, bf16[2,512]{1,0:T(2,128)(2,1)S(1)}, u32[]{:S(2)}, u32[]{:S(2)}) collective-permute-start(bf16[2,512]{1,0:T(2,128)(2,1)S(1)} %bitcast.30), channel_id=1, source_target_pairs={{0,1},{1,0},{2,3},{3,2},{4,5},{5,4},{6,7},{7,6},{8,9},{9,8},{10,11... | collective-permute-start | bytes 6152 | tf_op jit(solution)/shard_map/ppermute | solution.py:261
  16.5 25.5 %slice-start.5 = ((s8[4718592]{0:T(1024)(128)(4,1)}), s8[524288]{0:T(1024)(128)(4,1)S(1)}, s32[]{:S(2)}) async-start(s8[4718592]{0:T(1024)(128)(4,1)} %bitcast.19), calls=%async_computation.7 | async-start | bytes 1048576
  18.0 4.7 %collective-permute-start.11 = (bf16[2,2304]{1,0:T(2,128)(2,1)S(1)}, bf16[2,2304]{1,0:T(2,128)(2,1)S(1)}, u32[]{:S(2)}, u32[]{:S(2)}) collective-permute-start(bf16[2,2304]{1,0:T(2,128)(2,1)S(1)} %shard_map.138), channel_id=1, source_target_pairs={{0,65},{1,64},{2,67},{3,66},{4,69},{5,68},{6,71},{7,70},{8,73},{9,... | collective-permute-start | bytes 27656 | tf_op jit(solution)/shard_map/ppermute | solution.py:261
  20.0 4.3 %collective-permute-start.10 = (bf16[2,2304]{1,0:T(2,128)(2,1)S(1)}, bf16[2,2304]{1,0:T(2,128)(2,1)S(1)}, u32[]{:S(2)}, u32[]{:S(2)}) collective-permute-start(bf16[2,2304]{1,0:T(2,128)(2,1)S(1)} %shard_map.138), channel_id=1, source_target_pairs={{0,97},{1,96},{2,99},{3,98},{4,101},{5,100},{6,103},{7,102},{8,105... | collective-permute-start | bytes 27656 | tf_op jit(solution)/shard_map/ppermute | solution.py:261
  21.1 3.2 %collective-permute-start.9 = (bf16[2,2304]{1,0:T(2,128)(2,1)S(1)}, bf16[2,2304]{1,0:T(2,128)(2,1)S(1)}, u32[]{:S(2)}, u32[]{:S(2)}) collective-permute-start(bf16[2,2304]{1,0:T(2,128)(2,1)S(1)} %shard_map.138), channel_id=1, source_target_pairs={{0,33},{1,32},{2,35},{3,34},{4,37},{5,36},{6,39},{7,38},{8,41},{9,... | collective-permute-start | bytes 27656 | tf_op jit(solution)/shard_map/ppermute | solution.py:261
  21.1 3.2 %collective-permute-start.8 = (bf16[2,2304]{1,0:T(2,128)(2,1)S(1)}, bf16[2,2304]{1,0:T(2,128)(2,1)S(1)}, u32[]{:S(2)}, u32[]{:S(2)}) collective-permute-start(bf16[2,2304]{1,0:T(2,128)(2,1)S(1)} %shard_map.138), channel_id=1, source_target_pairs={{0,1},{1,0},{2,3},{3,2},{4,5},{5,4},{6,7},{7,6},{8,9},{9,8},{10,11... | collective-permute-start | bytes 27656 | tf_op jit(solution)/shard_map/ppermute | solution.py:261
  24.3 17.7 %slice-start = ((s8[9437184]{0:T(1024)(128)(4,1)}), s8[4194304]{0:T(1024)(128)(4,1)S(1)}, s32[]{:S(2)}) async-start(s8[9437184]{0:T(1024)(128)(4,1)} %bitcast.14), calls=%async_computation.2 | async-start | bytes 8388608
  24.3 17.7 %slice-start.1 = ((s8[9437184]{0:T(1024)(128)(4,1)}), s8[4194304]{0:T(1024)(128)(4,1)S(1)}, s32[]{:S(2)}) async-start(s8[9437184]{0:T(1024)(128)(4,1)} %bitcast.14), calls=%async_computation.3 | async-start | bytes 8388608
  24.3 17.7 %slice-start.2 = ((s8[9437184]{0:T(1024)(128)(4,1)}), s8[1048576]{0:T(1024)(128)(4,1)S(1)}, s32[]{:S(2)}) async-start(s8[9437184]{0:T(1024)(128)(4,1)} %bitcast.14), calls=%async_computation.4 | async-start | bytes 2097152
  24.4 17.7 %slice-start.6 = ((s8[4718592]{0:T(1024)(128)(4,1)}), s8[4194304]{0:T(1024)(128)(4,1)S(1)}, s32[]{:S(2)}) async-start(s8[4718592]{0:T(1024)(128)(4,1)} %bitcast.19), calls=%async_computation.8 | async-start | bytes 8388608
  24.4 17.7 %copy-start = (bf16[2,2304,256]{2,1,0:T(8,128)(2,1)S(1)}, bf16[2,2304,256]{2,1,0:T(8,128)(2,1)}, u32[]{:S(2)}) copy-start(bf16[2,2304,256]{2,1,0:T(8,128)(2,1)} %refs_7_.3) | copy-start | bytes 7077892
  24.4 17.7 %copy-start.2 = (bf16[256,2304]{1,0:T(8,128)(2,1)S(1)}, bf16[256,2304]{1,0:T(8,128)(2,1)}, u32[]{:S(2)}) copy-start(bf16[256,2304]{1,0:T(8,128)(2,1)} %refs_8_.5) | copy-start | bytes 3538948
  39.3 2.7 %collective-permute-start.12 = (bf16[16,2,2304]{2,1,0:T(2,128)(2,1)S(1)}, bf16[16,2,2304]{2,1,0:T(2,128)(2,1)S(1)}, u32[]{:S(2)}, u32[]{:S(2)}) collective-permute-start(bf16[16,2,2304]{2,1,0:T(2,128)(2,1)S(1)} %all_to_all.10.refs_1_), channel_id=1, source_target_pairs={{0,1},{1,0},{2,3},{3,2},{4,5},{5,4},{6,7},{7,6},{8,9},{9,8},{10,11... | collective-permute-start | bytes 442376 | tf_op jit(solution)/shard_map/ppermute | solution.py:261
  57.9 4.7 %collective-permute-start.16 = (bf16[2,2304]{1,0:T(2,128)(2,1)S(1)}, bf16[2,2304]{1,0:T(2,128)(2,1)S(1)}, u32[]{:S(2)}, u32[]{:S(2)}) collective-permute-start(bf16[2,2304]{1,0:T(2,128)(2,1)S(1)} %shard_map.141), channel_id=1, source_target_pairs={{0,65},{1,64},{2,67},{3,66},{4,69},{5,68},{6,71},{7,70},{8,73},{9,... | collective-permute-start | bytes 27656 | tf_op jit(solution)/shard_map/ppermute | solution.py:261
  59.1 4.3 %collective-permute-start.15 = (bf16[2,2304]{1,0:T(2,128)(2,1)S(1)}, bf16[2,2304]{1,0:T(2,128)(2,1)S(1)}, u32[]{:S(2)}, u32[]{:S(2)}) collective-permute-start(bf16[2,2304]{1,0:T(2,128)(2,1)S(1)} %shard_map.141), channel_id=1, source_target_pairs={{0,97},{1,96},{2,99},{3,98},{4,101},{5,100},{6,103},{7,102},{8,105... | collective-permute-start | bytes 27656 | tf_op jit(solution)/shard_map/ppermute | solution.py:261
  60.3 3.1 %collective-permute-start.14 = (bf16[2,2304]{1,0:T(2,128)(2,1)S(1)}, bf16[2,2304]{1,0:T(2,128)(2,1)S(1)}, u32[]{:S(2)}, u32[]{:S(2)}) collective-permute-start(bf16[2,2304]{1,0:T(2,128)(2,1)S(1)} %shard_map.141), channel_id=1, source_target_pairs={{0,33},{1,32},{2,35},{3,34},{4,37},{5,36},{6,39},{7,38},{8,41},{9,... | collective-permute-start | bytes 27656 | tf_op jit(solution)/shard_map/ppermute | solution.py:261
  61.0 2.4 %collective-permute-start.13 = (bf16[2,2304]{1,0:T(2,128)(2,1)S(1)}, bf16[2,2304]{1,0:T(2,128)(2,1)S(1)}, u32[]{:S(2)}, u32[]{:S(2)}) collective-permute-start(bf16[2,2304]{1,0:T(2,128)(2,1)S(1)} %shard_map.141), channel_id=1, source_target_pairs={{0,1},{1,0},{2,3},{3,2},{4,5},{5,4},{6,7},{7,6},{8,9},{9,8},{10,11... | collective-permute-start | bytes 27656 | tf_op jit(solution)/shard_map/ppermute | solution.py:261
  (9 other events, 88.0 us)

commit v9 on v8

--- a/solution.py
+++ b/solution.py
@@ -84,7 +84,7 @@
 
 def attend_kernel(marks_ref, *refs):
     count = (len(refs) - 4) // 2
-    q_refs, part_refs = refs[:count], refs[count + 3 : -1]
+    q_refs, part_refs = (refs[0], *refs[count - 1 : 0 : -1]), refs[count + 3 : -1]
     cache_ref, token_ref, picked_ref = refs[count : count + 3]
     refs[-1][...] = picked_ref[...]
     rows, span, width = cache_ref.shape
@@ -182,14 +182,12 @@
     router_ref,
     gate_up_ref,
     down_ref,
-    shared_gate_up_ref,
-    shared_down_ref,
-    out_ref,
-    shared_ref,
+    keep_ref,
+    send_ref,
     act,
 ):
     count = act.shape[0]
-    pairs, _, group, _ = out_ref.shape
+    pairs, group, _ = keep_ref.shape
     half = count // 2
     rows = jnp.concatenate(
         [
@@ -216,21 +214,28 @@
     for n in range(0, model, step):
         answer = jnp.dot(act[...], down_ref[:, n : n + step], preferred_element_type=F32)
         answer = weight * answer.astype(BF16).astype(F32)
-        mine, other = answer[:half], answer[half:]
-        for core, part in enumerate(
-            (jnp.where(first, other, mine), jnp.where(first, mine, other))
-        ):
-            out_ref[:, core, :, n : n + step] = part.reshape(pairs, group, step).astype(BF16)
+        for out_ref, part in ((send_ref, answer[:half]), (keep_ref, answer[half:])):
+            out_ref[:, :, n : n + step] = part.reshape(pairs, group, step).astype(BF16)
+
+
+def shared_kernel(marks_ref, rows_ref, gate_up_ref, down_ref, out_ref):
+    pairs, group, model = rows_ref.shape
+    count = pairs * group
+    rows = rows_ref[...].astype(F32).reshape(count, model).astype(BF16)
     row = lax.broadcasted_iota(jnp.int32, (8, count), 0)
     column = lax.broadcasted_iota(jnp.int32, (8, count), 1)
-    first_row = half + marks_ref[:, group + 2 : group + 3]
+    first_row = marks_ref[:, group + 2 : group + 3]
     chosen = jnp.where((row < group) & (column == first_row + row), 1.0, 0.0).astype(BF16)
     chosen = jnp.dot(chosen, rows, preferred_element_type=F32).astype(BF16)
-    gate = jnp.dot(chosen, shared_gate_up_ref[0], preferred_element_type=F32)
-    up = jnp.dot(chosen, shared_gate_up_ref[1], preferred_element_type=F32)
-    shared = (jax.nn.silu(gate) * up).astype(BF16)
-    shared = jnp.dot(shared, shared_down_ref[...], preferred_element_type=F32)
-    shared_ref[...] = shared[:group]
+    gate = jnp.dot(chosen, gate_up_ref[0], preferred_element_type=F32)
+    up = jnp.dot(chosen, gate_up_ref[1], preferred_element_type=F32)
+    act = (jax.nn.silu(gate) * up).astype(BF16)
+    out_ref[...] = jnp.dot(act, down_ref[...], preferred_element_type=F32)[:group]
+
+
+def add_kernel(one_ref, two_ref, shared_ref, out_ref, kept_ref):
+    kept_ref[...] = shared_ref[...]
+    out_ref[...] = (one_ref[...].astype(F32) + two_ref[...].astype(F32)).astype(BF16)
 
 
 def gather_sum_kernel(parts_ref, shared_ref, out_ref):
@@ -316,7 +321,7 @@
         attend_kernel,
         [shape((rows * heads, width + 128), BF16)] * ctx_count
         + [shape((total_rows, experts), F32)],
-        [marks, *every_query, latent_cache[0], token_latent[0], picked],
+        [marks, own_query, *every_query[:0:-1], latent_cache[0], token_latent[0], picked],
         beside=[expert_gate_up] * 3,
     )
     parts = crossings(parts)
@@ -332,7 +337,7 @@
             shape((rows, model), F32),
             shape((batch_count // 2, rows, model), BF16),
         ),
-        [residual[0], norm_gain, *terms],
+        [residual[0], norm_gain, *terms[::-1]],
         beside=[expert_gate_up] * 4,
     )
 
@@ -343,11 +348,11 @@
     ]
     own_rows = lax.all_to_all(copies, ("ctx", "batch"), 0, 0, axis_index_groups=groups)
     other_rows = crossings([own_rows])[0]
-    weighted, shared_part = call(
+    keep, send = call(
         expert_kernel,
         (
-            shape((batch_count // 2, 2, rows, model), BF16),
-            shape((rows, model), F32),
+            shape((batch_count // 2, rows, model), BF16),
+            shape((batch_count // 2, rows, model), BF16),
         ),
         [
             marks,
@@ -357,18 +362,25 @@
             router,
             expert_gate_up[0],
             expert_down[0],
-            shared_gate_up,
-            shared_down,
         ],
         scratch=[pltpu.VMEM((total_rows, expert_down.shape[1]), BF16)],
     )
-    weighted = weighted.reshape(batch_count, rows, model)
-    weighted = lax.all_to_all(weighted, "batch", 0, 0)
+    shared_part = call(
+        shared_kernel,
+        shape((rows, model), F32),
+        [marks, other_rows, shared_gate_up, shared_down],
+    )
+    weighted, shared_part = call(
+        add_kernel,
+        (shape((batch_count // 2, rows, model), BF16), shape((rows, model), F32)),
+        [keep, crossings([send])[0], shared_part],
+    )
+    weighted = lax.all_to_all(weighted, ("ctx", "batch"), 0, 0, axis_index_groups=groups)
     totals = call(
         gather_sum_kernel, shape((rows, model), BF16), [weighted, shared_part]
     )
     totals = crossings([totals] * ctx_count)
-    return call(final_kernel, shape((rows, model), BF16), [hidden, *totals])[None]
+    return call(final_kernel, shape((rows, model), BF16), [hidden, *totals[::-1]])[None]
 
 
 def solution(mesh):

time: 64.2 us -> 63.7 us (level)
  blocking collectives: 27.5 us -> 24.5 us
  starting transfers between devices: 18.6 us -> 20.3 us
    all_to_all x1, blocking collectives: 12.7 us -> 9.7 us  [local(): lax.all_to_all(weighted, ('ctx', 'batch'), 0, 0, axis_index_groups=groups)]
    ppermute x14 -> x15, starting transfers between devices: 14.2 us -> 15.9 us  [crossings(): lax.ppermute(array, ('ctx', 'batch'), [(c * count + b, (c ^ m) * count +...]
    ppermute x14 -> x15, waiting for transfers between devices: 8.17 us -> 8.58 us  [crossings(): lax.ppermute(array, ('ctx', 'batch'), [(c * count + b, (c ^ m) * count +...]
    pallas_call x7 -> x9, Pallas kernels: 7.43 us -> 7.82 us  [call(): pl.pallas_call(body, out_shape=out_shape, in_specs=(specs or [VMEM] * cou...]
  transfers between devices with their start and end apart: 17 -> 18, of which waited for: 8 -> 8; matrix products, arithmetic and copies ran while one was open for 0% -> 0% of each run, Pallas kernels for 2% -> 3%
where the time goes in v9:
time: 63.7 us; the launch traced here: 63.6 us
  blocking collectives  24.5 us (38%)
  starting transfers between devices  20.3 us (32%)
  waiting for transfers between devices  10.5 us (16%)
  Pallas kernels  7.82 us (12%)
    ppermute x15, starting transfers between devices, crossings(): lax.ppermute(array, ('ctx', 'batch'), [(c * count + b, (c ^ m) * count +...  15.9 us
    all_to_all x1, blocking collectives, local(): lax.all_to_all(copies, ('ctx', 'batch'), 0, 0, axis_index_groups=groups)  14.8 us
    all_to_all x1, blocking collectives, local(): lax.all_to_all(weighted, ('ctx', 'batch'), 0, 0, axis_index_groups=groups)  9.7 us
    ppermute x15, waiting for transfers between devices, crossings(): lax.ppermute(array, ('ctx', 'batch'), [(c * count + b, (c ^ m) * count +...  8.58 us
    pallas_call x9, Pallas kernels, call(): pl.pallas_call(body, out_shape=out_shape, in_specs=(specs or [VMEM] * cou...  7.82 us
    ppermute x3, starting transfers between devices, swaps(): lax.ppermute(array, 'ctx', [(place, place ^ m) for place in range(size)])  4.44 us
    ppermute x3, waiting for transfers between devices, swaps(): lax.ppermute(array, 'ctx', [(place, place ^ m) for place in range(size)])  1.88 us
  transfers between devices with their start and end apart: 18, of which 8 were waited for; matrix products, arithmetic and copies ran while one was open for 0% of the time, Pallas kernels for 3%

profile of v9, /device:TPU:1, one launch (start us, length us, event | category | flops | bytes accessed | tf_op | source)
XLA Modules:
  0.0 63.6 jit_solution(12327548085551707239)
XLA Ops:
  0.0 3.6 %collective-permute-start.1 = (bf16[16,512]{1,0:T(8,128)(2,1)}, bf16[16,512]{1,0:T(8,128)(2,1)S(1)}, u32[]{:S(2)}, u32[]{:S(2)}) collective-permute-start(bf16[16,512]{1,0:T(8,128)(2,1)} %bitcast.22), channel_id=1, source_target_pairs={{0,64},{32,96},{64,0},{96,32},{1,65},{33,97},{65,1},{97,33},{2,66}... | collective-permute-start | bytes 49160 | tf_op jit(solution)/shard_map/ppermute | solution.py:257
  3.6 0.9 %collective-permute-start.2 = (bf16[16,512]{1,0:T(8,128)(2,1)}, bf16[16,512]{1,0:T(8,128)(2,1)S(1)}, u32[]{:S(2)}, u32[]{:S(2)}) collective-permute-start(bf16[16,512]{1,0:T(8,128)(2,1)} %bitcast.23), channel_id=1, source_target_pairs={{0,96},{32,64},{64,32},{96,0},{1,97},{33,65},{65,33},{97,1},{2,98}... | collective-permute-start | bytes 49160 | tf_op jit(solution)/shard_map/ppermute | solution.py:257
  4.5 1.1 %shard_map.136 = (f32[64,128]{1,0:T(8,128)S(1)}, s32[1,2]{1,0:T(1,128)S(1)}) custom-call(s32[2,8,32]{2,1,0:T(8,128)} %bitcast.29, s32[1,2]{1,0:T(1,128)} %refs_1_.3, bf16[1,2304,2048]{2,1,0:T(8,128)(2,1)} %refs_9_.3), custom_call_target="tpu_custom_call" | custom-call | tf_op jit(solution)/shard_map/pallas_call | solution.py:28
  5.7 1.9 %collective-permute-done.2.refs_3_ = bf16[16,512]{1,0:T(8,128)(2,1)S(1)} collective-permute-done((bf16[16,512]{1,0:T(8,128)(2,1)}, bf16[16,512]{1,0:T(8,128)(2,1)S(1)}, u32[]{:S(2)}, u32[]{:S(2)}) %collective-permute-start.2) | collective-permute-done | bytes 16416 | tf_op jit(solution)/shard_map/ppermute | solution.py:257
  7.6 1.1 %shard_map.137 = (bf16[16,640]{1,0:T(8,128)(2,1)S(1)}, bf16[16,640]{1,0:T(8,128)(2,1)S(1)}, bf16[16,640]{1,0:T(8,128)(2,1)S(1)}, bf16[16,640]{1,0:T(8,128)(2,1)S(1)}, f32[64,128]{1,0:T(8,128)S(1)}) custom-call(s32[1,5]{1,0:T(1,128)S(1)} %pad_add_fusion.refs_0_, bf16[16,512]{1,0:T(8,128)(2,1)S(1)} %bitcast.25, ...), custom_call_target="tpu_custom_call" | custom-call | tf_op jit(solution)/shard_map/pallas_call | solution.py:28
  8.8 3.3 %collective-permute-start.4 = (bf16[16,640]{1,0:T(8,128)(2,1)S(1)}, bf16[16,640]{1,0:T(8,128)(2,1)S(1)}, u32[]{:S(2)}, u32[]{:S(2)}) collective-permute-start(bf16[16,640]{1,0:T(8,128)(2,1)S(1)} %get-tuple-element.20), channel_id=1, source_target_pairs={{0,65},{1,64},{2,67},{3,66},{4,69},{5,68},{6,71},{7,70},{8,73},{9,... | collective-permute-start | bytes 61448 | tf_op jit(solution)/shard_map/ppermute | solution.py:266
  12.7 1.1 %collective-permute-start.6 = (bf16[16,640]{1,0:T(8,128)(2,1)S(1)}, bf16[16,640]{1,0:T(8,128)(2,1)S(1)}, u32[]{:S(2)}, u32[]{:S(2)}) collective-permute-start(bf16[16,640]{1,0:T(8,128)(2,1)S(1)} %get-tuple-element.22), channel_id=1, source_target_pairs={{0,33},{1,32},{2,35},{3,34},{4,37},{5,36},{6,39},{7,38},{8,41},{9,... | collective-permute-start | bytes 61448 | tf_op jit(solution)/shard_map/ppermute | solution.py:266
  14.3 0.8 %collective-permute-done.refs_2_ = bf16[2,512]{1,0:T(2,128)(2,1)S(1)} collective-permute-done((bf16[2,512]{1,0:T(2,128)(2,1)S(1)}, bf16[2,512]{1,0:T(2,128)(2,1)S(1)}, u32[]{:S(2)}, u32[]{:S(2)}) %collective-permute-start) | collective-permute-done | bytes 2080 | tf_op jit(solution)/shard_map/ppermute | solution.py:266
  15.1 1.4 %collective-permute-done.5.refs_4_ = bf16[16,640]{1,0:T(8,128)(2,1)S(1)} collective-permute-done((bf16[16,640]{1,0:T(8,128)(2,1)S(1)}, bf16[16,640]{1,0:T(8,128)(2,1)S(1)}, u32[]{:S(2)}, u32[]{:S(2)}) %collective-permute-start.5) | collective-permute-done | bytes 20512 | tf_op jit(solution)/shard_map/ppermute | solution.py:266
  16.5 1.4 %shard_map.138 = bf16[2,2304]{1,0:T(2,128)(2,1)S(1)} custom-call(bf16[8,512,128]{2,1,0:T(8,128)(2,1)S(1)} %copy-done.3, bf16[1024,2304]{1,0:T(8,128)(2,1)S(1)} %bitcast.20, bf16[2,512]{1,0:T(2,128)(2,1)S(1)} %collective-permute-done.refs_2_, bf16[16,640]{1,0:T(8,128)(2,1)S(1)} %collective-permute-done.4.refs_3_, ...), custom_call_target="tpu_custom_call" | custom-call | tf_op jit(solution)/shard_map/pallas_call | solution.py:28
  18.0 2.0 %collective-permute-start.8 = (bf16[2,2304]{1,0:T(2,128)(2,1)S(1)}, bf16[2,2304]{1,0:T(2,128)(2,1)S(1)}, u32[]{:S(2)}, u32[]{:S(2)}) collective-permute-start(bf16[2,2304]{1,0:T(2,128)(2,1)S(1)} %shard_map.138), channel_id=1, source_target_pairs={{0,65},{1,64},{2,67},{3,66},{4,69},{5,68},{6,71},{7,70},{8,73},{9,... | collective-permute-start | bytes 27656 | tf_op jit(solution)/shard_map/ppermute | solution.py:266
  20.0 1.1 %collective-permute-start.9 = (bf16[2,2304]{1,0:T(2,128)(2,1)S(1)}, bf16[2,2304]{1,0:T(2,128)(2,1)S(1)}, u32[]{:S(2)}, u32[]{:S(2)}) collective-permute-start(bf16[2,2304]{1,0:T(2,128)(2,1)S(1)} %shard_map.138), channel_id=1, source_target_pairs={{0,97},{1,96},{2,99},{3,98},{4,101},{5,100},{6,103},{7,102},{8,105... | collective-permute-start | bytes 27656 | tf_op jit(solution)/shard_map/ppermute | solution.py:266
  21.5 1.1 %collective-permute-done.8.refs_2_ = bf16[2,2304]{1,0:T(2,128)(2,1)S(1)} collective-permute-done((bf16[2,2304]{1,0:T(2,128)(2,1)S(1)}, bf16[2,2304]{1,0:T(2,128)(2,1)S(1)}, u32[]{:S(2)}, u32[]{:S(2)}) %collective-permute-start.8) | collective-permute-done | bytes 9248 | tf_op jit(solution)/shard_map/ppermute | solution.py:266
  22.6 1.7 %collective-permute-done.9.refs_3_ = bf16[2,2304]{1,0:T(2,128)(2,1)S(1)} collective-permute-done((bf16[2,2304]{1,0:T(2,128)(2,1)S(1)}, bf16[2,2304]{1,0:T(2,128)(2,1)S(1)}, u32[]{:S(2)}, u32[]{:S(2)}) %collective-permute-start.9) | collective-permute-done | bytes 9248 | tf_op jit(solution)/shard_map/ppermute | solution.py:266
  24.5 14.8 %all_to_all.10.refs_1_ = bf16[16,2,2304]{2,1,0:T(2,128)(2,1)S(1)} all-to-all(bf16[16,2,2304]{2,1,0:T(2,128)(2,1)S(1)} %get-tuple-element.25), channel_id=1, replica_groups={{0,2,4,6,8,10,12,14,16,18,20,22,24,26,28,30},{1,3,5,7,9,11,13,15,17,19,..., dimensions={0} | all-to-all | bytes 294912 | tf_op jit(solution)/shard_map/all_to_all | solution.py:349
  39.3 1.7 %collective-permute-start.12 = (bf16[16,2,2304]{2,1,0:T(2,128)(2,1)S(1)}, bf16[16,2,2304]{2,1,0:T(2,128)(2,1)S(1)}, u32[]{:S(2)}, u32[]{:S(2)}) collective-permute-start(bf16[16,2,2304]{2,1,0:T(2,128)(2,1)S(1)} %all_to_all.10.refs_1_), channel_id=1, source_target_pairs={{0,1},{1,0},{2,3},{3,2},{4,5},{5,4},{6,7},{7,6},{8,9},{9,8},{10,11... | collective-permute-start | bytes 442376 | tf_op jit(solution)/shard_map/ppermute | solution.py:266
  41.0 1.0 %collective-permute-done.12.refs_2_.refs_1_ = bf16[16,2,2304]{2,1,0:T(2,128)(2,1)S(1)} collective-permute-done((bf16[16,2,2304]{2,1,0:T(2,128)(2,1)S(1)}, bf16[16,2,2304]{2,1,0:T(2,128)(2,1)S(1)}, u32[]{:S(2)}, u32[]{:S(2)}) %collective-permute-start.12) | collective-permute-done | bytes 147488 | tf_op jit(solution)/shard_map/ppermute | solution.py:266
  42.1 2.3 %shard_map.140 = (bf16[16,2,2304]{2,1,0:T(2,128)(2,1)S(1)}, bf16[16,2,2304]{2,1,0:T(2,128)(2,1)S(1)}) custom-call(s32[1,5]{1,0:T(1,128)S(1)} %pad_add_fusion.refs_0_, bf16[16,2,2304]{2,1,0:T(2,128)(2,1)S(1)} %all_to_all.10.refs_1_, bf16[16,2,2304]{2,1,0:T(2,128)(2,1)S(1)} %collective-permute-done.12.refs_2_.refs_1_, ...), custom_call_target="tpu_custom_call" | custom-call | tf_op jit(solution)/shard_map/pallas_call | solution.py:28
  44.9 0.8 %shard_map.141.refs_2_ = f32[2,2304]{1,0:T(2,128)S(1)} custom-call(s32[1,5]{1,0:T(1,128)S(1)} %pad_add_fusion.refs_0_, bf16[16,2,2304]{2,1,0:T(2,128)(2,1)S(1)} %collective-permute-done.12.refs_2_.refs_1_, bf16[2,2304,256]{2,1,0:T(8,128)(2,1)S(1)} %copy-done, bf16[256,2304]{1,0:T(8,128)(2,1)S(1)} %copy-done.2), custom_call_target="tpu_custom_call" | custom-call | tf_op jit(solution)/shard_map/pallas_call | solution.py:28
  46.0 9.7 %all_to_all.11.refs_0_ = bf16[16,2,2304]{2,1,0:T(2,128)(2,1)S(1)} all-to-all(bf16[16,2,2304]{2,1,0:T(2,128)(2,1)S(1)} %get-tuple-element.29), channel_id=1, replica_groups={{0,2,4,6,8,10,12,14,16,18,20,22,24,26,28,30},{1,3,5,7,9,11,13,15,17,19,..., dimensions={0} | all-to-all | bytes 294912 | tf_op jit(solution)/shard_map/all_to_all | solution.py:378
  55.9 2.8 %collective-permute-start.14 = (bf16[2,2304]{1,0:T(2,128)(2,1)S(1)}, bf16[2,2304]{1,0:T(2,128)(2,1)S(1)}, u32[]{:S(2)}, u32[]{:S(2)}) collective-permute-start(bf16[2,2304]{1,0:T(2,128)(2,1)S(1)} %shard_map.143), channel_id=1, source_target_pairs={{0,65},{1,64},{2,67},{3,66},{4,69},{5,68},{6,71},{7,70},{8,73},{9,... | collective-permute-start | bytes 27656 | tf_op jit(solution)/shard_map/ppermute | solution.py:266
  58.7 0.6 collective-permute-start.15
  59.3 1.3 %collective-permute-start.16 = (bf16[2,2304]{1,0:T(2,128)(2,1)S(1)}, bf16[2,2304]{1,0:T(2,128)(2,1)S(1)}, u32[]{:S(2)}, u32[]{:S(2)}) collective-permute-start(bf16[2,2304]{1,0:T(2,128)(2,1)S(1)} %shard_map.143), channel_id=1, source_target_pairs={{0,33},{1,32},{2,35},{3,34},{4,37},{5,36},{6,39},{7,38},{8,41},{9,... | collective-permute-start | bytes 27656 | tf_op jit(solution)/shard_map/ppermute | solution.py:266
  60.6 2.4 %collective-permute-done.15.refs_2_ = bf16[2,2304]{1,0:T(2,128)(2,1)S(1)} collective-permute-done((bf16[2,2304]{1,0:T(2,128)(2,1)S(1)}, bf16[2,2304]{1,0:T(2,128)(2,1)S(1)}, u32[]{:S(2)}, u32[]{:S(2)}) %collective-permute-start.15) | collective-permute-done | bytes 9248 | tf_op jit(solution)/shard_map/ppermute | solution.py:266
  (61 shorter events, 3.5 us)
Async XLA Ops:
  0.0 5.7 %collective-permute-start.1 = (bf16[16,512]{1,0:T(8,128)(2,1)}, bf16[16,512]{1,0:T(8,128)(2,1)S(1)}, u32[]{:S(2)}, u32[]{:S(2)}) collective-permute-start(bf16[16,512]{1,0:T(8,128)(2,1)} %bitcast.22), channel_id=1, source_target_pairs={{0,64},{32,96},{64,0},{96,32},{1,65},{33,97},{65,1},{97,33},{2,66}... | collective-permute-start | bytes 49160 | tf_op jit(solution)/shard_map/ppermute | solution.py:257
  3.6 4.0 %collective-permute-start.2 = (bf16[16,512]{1,0:T(8,128)(2,1)}, bf16[16,512]{1,0:T(8,128)(2,1)S(1)}, u32[]{:S(2)}, u32[]{:S(2)}) collective-permute-start(bf16[16,512]{1,0:T(8,128)(2,1)} %bitcast.23), channel_id=1, source_target_pairs={{0,96},{32,64},{64,32},{96,0},{1,97},{33,65},{65,33},{97,1},{2,98}... | collective-permute-start | bytes 49160 | tf_op jit(solution)/shard_map/ppermute | solution.py:257
  4.4 3.2 %collective-permute-start.3 = (bf16[16,512]{1,0:T(8,128)(2,1)}, bf16[16,512]{1,0:T(8,128)(2,1)S(1)}, u32[]{:S(2)}, u32[]{:S(2)}) collective-permute-start(bf16[16,512]{1,0:T(8,128)(2,1)} %bitcast.24), channel_id=1, source_target_pairs={{0,32},{32,0},{64,96},{96,64},{1,33},{33,1},{65,97},{97,65},{2,34}... | collective-permute-start | bytes 49160 | tf_op jit(solution)/shard_map/ppermute | solution.py:257
  8.8 6.3 %collective-permute-start.4 = (bf16[16,640]{1,0:T(8,128)(2,1)S(1)}, bf16[16,640]{1,0:T(8,128)(2,1)S(1)}, u32[]{:S(2)}, u32[]{:S(2)}) collective-permute-start(bf16[16,640]{1,0:T(8,128)(2,1)S(1)} %get-tuple-element.20), channel_id=1, source_target_pairs={{0,65},{1,64},{2,67},{3,66},{4,69},{5,68},{6,71},{7,70},{8,73},{9,... | collective-permute-start | bytes 61448 | tf_op jit(solution)/shard_map/ppermute | solution.py:266
  12.1 4.4 %collective-permute-start.5 = (bf16[16,640]{1,0:T(8,128)(2,1)S(1)}, bf16[16,640]{1,0:T(8,128)(2,1)S(1)}, u32[]{:S(2)}, u32[]{:S(2)}) collective-permute-start(bf16[16,640]{1,0:T(8,128)(2,1)S(1)} %get-tuple-element.21), channel_id=1, source_target_pairs={{0,97},{1,96},{2,99},{3,98},{4,101},{5,100},{6,103},{7,102},{8,105... | collective-permute-start | bytes 61448 | tf_op jit(solution)/shard_map/ppermute | solution.py:266
  12.7 3.8 %collective-permute-start.6 = (bf16[16,640]{1,0:T(8,128)(2,1)S(1)}, bf16[16,640]{1,0:T(8,128)(2,1)S(1)}, u32[]{:S(2)}, u32[]{:S(2)}) collective-permute-start(bf16[16,640]{1,0:T(8,128)(2,1)S(1)} %get-tuple-element.22), channel_id=1, source_target_pairs={{0,33},{1,32},{2,35},{3,34},{4,37},{5,36},{6,39},{7,38},{8,41},{9,... | collective-permute-start | bytes 61448 | tf_op jit(solution)/shard_map/ppermute | solution.py:266
  13.8 2.7 %collective-permute-start.7 = (bf16[16,640]{1,0:T(8,128)(2,1)S(1)}, bf16[16,640]{1,0:T(8,128)(2,1)S(1)}, u32[]{:S(2)}, u32[]{:S(2)}) collective-permute-start(bf16[16,640]{1,0:T(8,128)(2,1)S(1)} %get-tuple-element.23), channel_id=1, source_target_pairs={{0,1},{1,0},{2,3},{3,2},{4,5},{5,4},{6,7},{7,6},{8,9},{9,8},{10,11... | collective-permute-start | bytes 61448 | tf_op jit(solution)/shard_map/ppermute | solution.py:266
  13.8 1.3 %collective-permute-start = (bf16[2,512]{1,0:T(2,128)(2,1)S(1)}, bf16[2,512]{1,0:T(2,128)(2,1)S(1)}, u32[]{:S(2)}, u32[]{:S(2)}) collective-permute-start(bf16[2,512]{1,0:T(2,128)(2,1)S(1)} %bitcast.28), channel_id=1, source_target_pairs={{0,1},{1,0},{2,3},{3,2},{4,5},{5,4},{6,7},{7,6},{8,9},{9,8},{10,11... | collective-permute-start | bytes 6152 | tf_op jit(solution)/shard_map/ppermute | solution.py:266
  16.5 25.5 %slice-start.3 = ((s8[4718592]{0:T(1024)(128)(4,1)}), s8[4194304]{0:T(1024)(128)(4,1)S(1)}, s32[]{:S(2)}) async-start(s8[4718592]{0:T(1024)(128)(4,1)} %bitcast.16), calls=%async_computation.5 | async-start | bytes 8388608
  18.0 4.7 %collective-permute-start.8 = (bf16[2,2304]{1,0:T(2,128)(2,1)S(1)}, bf16[2,2304]{1,0:T(2,128)(2,1)S(1)}, u32[]{:S(2)}, u32[]{:S(2)}) collective-permute-start(bf16[2,2304]{1,0:T(2,128)(2,1)S(1)} %shard_map.138), channel_id=1, source_target_pairs={{0,65},{1,64},{2,67},{3,66},{4,69},{5,68},{6,71},{7,70},{8,73},{9,... | collective-permute-start | bytes 27656 | tf_op jit(solution)/shard_map/ppermute | solution.py:266
  20.0 4.3 %collective-permute-start.9 = (bf16[2,2304]{1,0:T(2,128)(2,1)S(1)}, bf16[2,2304]{1,0:T(2,128)(2,1)S(1)}, u32[]{:S(2)}, u32[]{:S(2)}) collective-permute-start(bf16[2,2304]{1,0:T(2,128)(2,1)S(1)} %shard_map.138), channel_id=1, source_target_pairs={{0,97},{1,96},{2,99},{3,98},{4,101},{5,100},{6,103},{7,102},{8,105... | collective-permute-start | bytes 27656 | tf_op jit(solution)/shard_map/ppermute | solution.py:266
  21.1 3.2 %collective-permute-start.10 = (bf16[2,2304]{1,0:T(2,128)(2,1)S(1)}, bf16[2,2304]{1,0:T(2,128)(2,1)S(1)}, u32[]{:S(2)}, u32[]{:S(2)}) collective-permute-start(bf16[2,2304]{1,0:T(2,128)(2,1)S(1)} %shard_map.138), channel_id=1, source_target_pairs={{0,33},{1,32},{2,35},{3,34},{4,37},{5,36},{6,39},{7,38},{8,41},{9,... | collective-permute-start | bytes 27656 | tf_op jit(solution)/shard_map/ppermute | solution.py:266
  21.1 3.2 %collective-permute-start.11 = (bf16[2,2304]{1,0:T(2,128)(2,1)S(1)}, bf16[2,2304]{1,0:T(2,128)(2,1)S(1)}, u32[]{:S(2)}, u32[]{:S(2)}) collective-permute-start(bf16[2,2304]{1,0:T(2,128)(2,1)S(1)} %shard_map.138), channel_id=1, source_target_pairs={{0,1},{1,0},{2,3},{3,2},{4,5},{5,4},{6,7},{7,6},{8,9},{9,8},{10,11... | collective-permute-start | bytes 27656 | tf_op jit(solution)/shard_map/ppermute | solution.py:266
  24.3 17.7 %slice-start = ((s8[9437184]{0:T(1024)(128)(4,1)}), s8[4194304]{0:T(1024)(128)(4,1)S(1)}, s32[]{:S(2)}) async-start(s8[9437184]{0:T(1024)(128)(4,1)} %bitcast.13), calls=%async_computation.2 | async-start | bytes 8388608
  24.3 17.7 %slice-start.1 = ((s8[9437184]{0:T(1024)(128)(4,1)}), s8[4194304]{0:T(1024)(128)(4,1)S(1)}, s32[]{:S(2)}) async-start(s8[9437184]{0:T(1024)(128)(4,1)} %bitcast.13), calls=%async_computation.3 | async-start | bytes 8388608
  24.3 17.7 %slice-start.2 = ((s8[9437184]{0:T(1024)(128)(4,1)}), s8[1048576]{0:T(1024)(128)(4,1)S(1)}, s32[]{:S(2)}) async-start(s8[9437184]{0:T(1024)(128)(4,1)} %bitcast.13), calls=%async_computation.4 | async-start | bytes 2097152
  24.4 17.7 %slice-start.4 = ((s8[4718592]{0:T(1024)(128)(4,1)}), s8[524288]{0:T(1024)(128)(4,1)S(1)}, s32[]{:S(2)}) async-start(s8[4718592]{0:T(1024)(128)(4,1)} %bitcast.16), calls=%async_computation.6 | async-start | bytes 1048576
  24.4 17.7 %copy-start.4 = (bf16[2304,128]{1,0:T(8,128)(2,1)S(1)}, bf16[2304,128]{1,0:T(8,128)(2,1)}, u32[]{:S(2)}) copy-start(bf16[2304,128]{1,0:T(8,128)(2,1)} %refs_4_.1) | copy-start | bytes 1769476
  39.3 2.7 %collective-permute-start.12 = (bf16[16,2,2304]{2,1,0:T(2,128)(2,1)S(1)}, bf16[16,2,2304]{2,1,0:T(2,128)(2,1)S(1)}, u32[]{:S(2)}, u32[]{:S(2)}) collective-permute-start(bf16[16,2,2304]{2,1,0:T(2,128)(2,1)S(1)} %all_to_all.10.refs_1_), channel_id=1, source_target_pairs={{0,1},{1,0},{2,3},{3,2},{4,5},{5,4},{6,7},{7,6},{8,9},{9,8},{10,11... | collective-permute-start | bytes 442376 | tf_op jit(solution)/shard_map/ppermute | solution.py:266
  44.4 1.5 %collective-permute-start.13 = (bf16[16,2,2304]{2,1,0:T(2,128)(2,1)S(1)}, bf16[16,2,2304]{2,1,0:T(2,128)(2,1)S(1)}, u32[]{:S(2)}, u32[]{:S(2)}) collective-permute-start(bf16[16,2,2304]{2,1,0:T(2,128)(2,1)S(1)} %get-tuple-element.28), channel_id=1, source_target_pairs={{0,1},{1,0},{2,3},{3,2},{4,5},{5,4},{6,7},{7,6},{8,9},{9,8},{10,11... | collective-permute-start | bytes 442376 | tf_op jit(solution)/shard_map/ppermute | solution.py:266
  55.9 4.7 %collective-permute-start.14 = (bf16[2,2304]{1,0:T(2,128)(2,1)S(1)}, bf16[2,2304]{1,0:T(2,128)(2,1)S(1)}, u32[]{:S(2)}, u32[]{:S(2)}) collective-permute-start(bf16[2,2304]{1,0:T(2,128)(2,1)S(1)} %shard_map.143), channel_id=1, source_target_pairs={{0,65},{1,64},{2,67},{3,66},{4,69},{5,68},{6,71},{7,70},{8,73},{9,... | collective-permute-start | bytes 27656 | tf_op jit(solution)/shard_map/ppermute | solution.py:266
  58.7 4.3 %collective-permute-start.15 = (bf16[2,2304]{1,0:T(2,128)(2,1)S(1)}, bf16[2,2304]{1,0:T(2,128)(2,1)S(1)}, u32[]{:S(2)}, u32[]{:S(2)}) collective-permute-start(bf16[2,2304]{1,0:T(2,128)(2,1)S(1)} %shard_map.143), channel_id=1, source_target_pairs={{0,97},{1,96},{2,99},{3,98},{4,101},{5,100},{6,103},{7,102},{8,105... | collective-permute-start | bytes 27656 | tf_op jit(solution)/shard_map/ppermute | solution.py:266
  59.3 3.7 %collective-permute-start.16 = (bf16[2,2304]{1,0:T(2,128)(2,1)S(1)}, bf16[2,2304]{1,0:T(2,128)(2,1)S(1)}, u32[]{:S(2)}, u32[]{:S(2)}) collective-permute-start(bf16[2,2304]{1,0:T(2,128)(2,1)S(1)} %shard_map.143), channel_id=1, source_target_pairs={{0,33},{1,32},{2,35},{3,34},{4,37},{5,36},{6,39},{7,38},{8,41},{9,... | collective-permute-start | bytes 27656 | tf_op jit(solution)/shard_map/ppermute | solution.py:266
  60.6 2.4 %collective-permute-start.17 = (bf16[2,2304]{1,0:T(2,128)(2,1)S(1)}, bf16[2,2304]{1,0:T(2,128)(2,1)S(1)}, u32[]{:S(2)}, u32[]{:S(2)}) collective-permute-start(bf16[2,2304]{1,0:T(2,128)(2,1)S(1)} %shard_map.143), channel_id=1, source_target_pairs={{0,1},{1,0},{2,3},{3,2},{4,5},{5,4},{6,7},{7,6},{8,9},{9,8},{10,11... | collective-permute-start | bytes 27656 | tf_op jit(solution)/shard_map/ppermute | solution.py:266
  (10 other events, 76.0 us)
